TPU v7x, 128 devices: a whole 4x4x4 slice. The times are simulated.
128 devices in a mesh: gy: 8 (over x, core), gz: 16 (over y, z).
Axes of the slice: x: 4, y: 4, z: 4, core: 2. Of those that a mesh axis runs over, the one named last changes fastest.
Arguments:
- right_side: float32 [5, 8, 256, 4096], P(None, None, 'gy', 'gz'), may hold values from -6 to 6
- speeds: float32 [3, 8, 256, 4096], P(None, None, 'gy', 'gz'), may hold values from -1 to 1
- porosity: float32 [8, 256, 4096], P(None, 'gy', 'gz'), may hold values from 0 to 1
- coupling: float32 [3, 5, 5], replicated, may hold values from -3 to 3
- momentum: float32 [3, 8, 256, 4096], P(None, None, 'gy', 'gz'), may hold values from -6 to 6
- design_ids: int32 [2, 64, 1024], P(None, 'gy', 'gz'), may hold values from 0 to 32767, as said below
Outputs:
- adjoint: float32 [5, 8, 256, 4096], P(None, None, 'gy', 'gz')
- sensitivity: float32 [32768], P(('gy', 'gz'))
Inputs may be any that keep to these rules, and one draw needn't show every extreme that they name: `design_ids`: of the blocks that one device holds, at most 16 name variables owned by any one device, and in every draw each device sends exactly 16 to some owner.
All inputs are finite; a program needn't handle non-finite values.
Results may differ from a plain program's by a relative error of at most 0.00019.
Values sent between devices are 32-bit elements; how exact they have to be, the bound alone decides.
A program may use at most 64 MiB of HBM per device.

v0:
```python
import jax
import jax.numpy as jnp
from jax import lax
from jax.sharding import PartitionSpec as P

POWERS = 3


PENALTY = 1.0
COURANT = 0.3


def padded(block, sides, width):
    for axis, dim in sides:
        count = lax.axis_size(axis)
        forward = [(i, i + 1) for i in range(count - 1)]
        backward = [(target, source) for source, target in forward]
        low = lax.ppermute(
            lax.slice_in_dim(block, block.shape[dim] - width, None, axis=dim), axis, forward
        )
        high = lax.ppermute(lax.slice_in_dim(block, 0, width, axis=dim), axis, backward)
        block = jnp.concatenate([low, block, high], axis=dim)
    return block


def shifted(field, direction, start):
    sizes = field.shape
    index = [slice(None), slice(1, sizes[1] - 1), slice(1, sizes[2] - 1), slice(1, sizes[3] - 1)]
    length = sizes[direction + 1]
    index[direction + 1] = slice(start, length - 2 + start)
    return field[tuple(index)]


def transpose_sweep(values, speeds, porosity, coupling):
    interior = shifted(values, 0, 1)
    total = PENALTY * porosity[1:-1, 1:-1, 1:-1][None] * interior
    for direction in range(3):
        speed = speeds[direction][None]
        forward = jnp.maximum(speed, 0.0) * values
        backward = jnp.maximum(-speed, 0.0) * values
        flux = (
            jnp.abs(shifted(speed, 0, 1)) * interior
            - shifted(forward, direction, 2)
            - shifted(backward, direction, 0)
        )
        total = total + COURANT * jnp.einsum(
            "ij,ixyz->jxyz", coupling[direction], flux, precision=lax.Precision.HIGHEST
        )
    return total


def pad_first(field):
    widths = [(0, 0)] * (field.ndim - 3) + [(1, 1), (0, 0), (0, 0)]
    return jnp.pad(field, widths)


def pad_cells(field):
    widths = [(0, 0)] * (field.ndim - 3) + [(1, 1), (1, 1), (1, 1)]
    return jnp.pad(field, widths)


def least_squares(upper):
    hess = upper[:, 1:] + upper[:, :-1]
    normal = jnp.dot(hess.T, hess, precision=lax.Precision.HIGHEST)
    target = jnp.dot(hess.T, upper[:, 0], precision=lax.Precision.HIGHEST)
    factor = jnp.linalg.cholesky(normal)
    count = normal.shape[0]
    forward = []
    for place in range(count):
        value = target[place]
        for inner in range(place):
            value = value - factor[place, inner] * forward[inner]
        forward.append(value / factor[place, place])
    backward = [None] * count
    for place in reversed(range(count)):
        value = forward[place]
        for inner in range(place + 1, count):
            value = value - factor[inner, place] * backward[inner]
        backward[place] = value / factor[place, place]
    return backward


def gram_matrix(basis):
    count = len(basis)
    rows_list = []
    for first in range(count):
        rows_list.append(
            jnp.stack([jnp.sum(basis[first] * basis[second]) for second in range(count)])
        )
    return jnp.stack(rows_list)


def local(right_side, speeds, porosity, coupling, momentum, design_ids):
    local_y = right_side.shape[2]
    local_z = right_side.shape[3]
    basis = [right_side]
    stacked = jnp.concatenate([right_side, speeds], axis=0)
    widened = padded(stacked, (("gy", 2), ("gz", 3)), 1)
    speeds_wide = pad_first(widened[5:])
    porosity_wide = pad_cells(porosity)
    current = widened[:5]
    for step in range(POWERS):
        result = transpose_sweep(pad_first(current), speeds_wide, porosity_wide, coupling)
        basis.append(result)
        if step + 1 < POWERS:
            current = padded(result, (("gy", 2), ("gz", 3)), 1)
    gram_local = gram_matrix(basis)
    gram = lax.psum(gram_local, ("gy", "gz"))
    upper = jnp.linalg.cholesky(gram).T
    coeffs = least_squares(upper)
    adjoint = coeffs[0] * basis[0]
    for step in range(1, POWERS):
        adjoint = adjoint + coeffs[step] * basis[step]
    cell_term = -PENALTY * jnp.sum(adjoint[1:4] * momentum, axis=0)
    cells_x = cell_term.shape[0]
    blocks = cell_term.reshape(cells_x // 4, 4, local_y // 4, 4, local_z // 4, 4).sum(
        axis=(1, 3, 5)
    )
    devices = lax.axis_size("gy") * lax.axis_size("gz")
    number_blocks = blocks.size
    per_owner = number_blocks // 4
    total_designs = per_owner * devices
    dense = jax.ops.segment_sum(
        blocks.reshape(-1), design_ids.reshape(-1), num_segments=total_designs
    )
    sensitivity = lax.psum_scatter(dense, ("gy", "gz"), scatter_dimension=0, tiled=True)
    return (adjoint, sensitivity)


def solution(mesh):
    in_specs = (
        P(None, None, "gy", "gz"),
        P(None, None, "gy", "gz"),
        P(None, "gy", "gz"),
        P(),
        P(None, None, "gy", "gz"),
        P(None, "gy", "gz"),
    )
    out_specs = (P(None, None, "gy", "gz"), P(("gy", "gz")))
    return jax.shard_map(local, mesh=mesh, in_specs=in_specs, out_specs=out_specs, check_vma=False)
```

profile of v0, /device:TPU:1, one launch (start us, length us, event | category | flops | bytes accessed | tf_op | source)
XLA Modules:
  0.0 406.6 jit_solution(6171157222155396657)
XLA Ops:
  7.2 2.2 copy.84
  10.0 4.5 %collective-permute-start = (f32[8,8,1,256]{3,0,2,1:T(8,128)S(1)}, f32[8,8,1,256]{3,0,2,1:T(8,128)S(1)}, u32[]{:S(2)}, u32[]{:S(2)}) collective-permute-start(f32[8,8,1,256]{3,0,2,1:T(8,128)S(1)} %get-tuple-element.17), channel_id=1, source_target_pairs={{0,16},{16,32},{32,48},{48,64},{64,80},{80,96},{96,112},{1,17},{17... | collective-permute-start | bytes 196616 | tf_op jit(solution)/shard_map/ppermute | solution.py:18
  14.5 1.9 collective-permute-start.1
  16.4 0.9 abs_bitcast_fusion
  17.3 2.8 collective-permute-done.1
  20.5 1.7 fusion.103
  22.2 2.4 copy.72
  24.6 4.1 %collective-permute-start.2 = (f32[8,8,34,1]{2,1,3,0:T(8,128)}, f32[8,8,34,1]{2,1,3,0:T(8,128)}, u32[]{:S(2)}, u32[]{:S(2)}) collective-permute-start(f32[8,8,34,1]{2,1,3,0:T(8,128)} %copy.72), channel_id=1, source_target_pairs={{0,1},{1,2},{2,3},{3,4},{4,5},{5,6},{6,7},{7,8},{8,9},{9,10},{10,1... | collective-permute-start | bytes 26120 | tf_op jit(solution)/shard_map/ppermute | solution.py:18
  28.7 2.4 copy.73
  31.1 1.3 collective-permute-start.3
  32.4 0.8 fusion.106
  33.3 2.3 copy.74
  36.1 2.3 copy.75
  38.4 3.7 pad_maximum_fusion
  42.5 2.5 broadcast_maximum_fusion
  46.2 0.9 copy-done
  47.3 3.3 fusion.7
  50.7 3.1 fusion.11
  53.9 4.8 %fusion.4 = f32[5,8,32,256]{3,0,2,1:T(8,128)S(1)} fusion(f32[5,8,32,256]{3,2,1,0:T(8,128)S(1)} %copy-done, f32[8,32,256,5]{2,3,1,0:T(8,128)S(1)} %fusion.11, f32[8,32,256,5]{2,3,1,0:T(8,128)S(1)} %fusion.7, f32[5,8,34,258]{3,0,2,1:T(8,128)S(1)} %bitcast.119, f32[8,32,256]{2,1,0:T(8,128)S(1)} %slice.293, f32[8,32,256]{2,1,0:T(8,128)S(1)} %slice.292, ...), kind=kOutput, calls=%fused_computation.27 | convolution fusion | flops 23592960 | bytes 7695076 | tf_op jit(solution)/shard_map/ij,ixyz->jxyz/dot_general | solution.py:46
  58.7 3.3 collective-permute-start.4
  62.0 1.9 collective-permute-start.5
  63.9 3.6 collective-permute-done.5
  67.8 1.7 fusion.102
  69.5 2.2 copy.85
  71.7 3.7 collective-permute-start.6
  75.4 2.2 copy.86
  77.7 1.3 collective-permute-start.7
  79.0 2.3 copy.87
  81.2 1.3 collective-permute-done.7
  82.5 2.3 copy.88
  84.8 3.9 select_maximum_fusion.4
  88.7 2.8 fusion.47
  91.6 2.8 fusion.42
  94.4 3.4 bitcast_add_fusion.3
  97.9 3.3 collective-permute-start.8
  101.2 1.9 collective-permute-start.9
  103.1 3.6 collective-permute-done.9
  107.0 1.7 fusion.101
  108.7 2.2 copy.93
  110.9 3.6 collective-permute-start.10
  114.5 2.2 copy.94
  116.7 1.7 collective-permute-start.11
  118.4 1.0 multiply_reduce_fusion.6
  119.4 2.3 copy.95
  121.7 2.3 copy.96
  124.0 4.3 %select_maximum_fusion = f32[5,10,34,258]{3,0,2,1:T(8,128)S(1)} fusion(f32[5,8,34,1]{3,0,2,1:T(8,128)} %copy.96, f32[5,8,34,1]{3,0,2,1:T(8,128)} %copy.95, f32[5,8,1,256]{3,0,2,1:T(8,128)S(1)} %collective-permute-done.9, f32[5,8,32,256]{3,0,2,1:T(8,128)} %copy-done.1, f32[5,8,1,256]{3,0,2,1:T(8,128)S(1)} %collective-permute-done.8), kind=kLoop, calls=%fused_computation.3 | loop fusion | flops 5263200 | bytes 3157920 | tf_op jit(solution)/shard_map/concatenate | solution.py:22
  128.3 2.9 fusion.32
  131.3 2.9 fusion.27
  134.3 6.6 %fusion.1 = (f32[]{:T(128)}, f32[]{:T(128)}, f32[]{:T(128)}, f32[]{:T(128)}, f32[]{:T(128)}, /*index=5*/f32[]{:T(128)}, f32[]{:T(128)}, f32[]{:T(128)}, f32[]{:T(128)}) fusion(f32[5,8,32,256]{3,0,2,1:T(8,128)S(1)} %fusion.4, f32[5,8,32,256]{3,2,1,0:T(8,128)S(1)} %copy-done, f32[5,8,32,256]{3,0,2,1:T(8,128)S(1)} %copy-done.2, ...), kind=kOutput, calls=%fused_computation.24 | convolution fusion | flops 29491192 | bytes 17041956 | tf_op jit(solution)/shard_map/ij,ixyz->jxyz/dot_general | solution.py:46
  140.8 2.6 maximum_bitcast_fusion
  143.6 2.7 maximum_bitcast_fusion.1
  146.3 2.5 maximum_bitcast_fusion.2
  148.9 2.6 maximum_bitcast_fusion.3
  151.7 68.2 %psum.7 = f32[4,4]{0,1:T(4,128)S(1)} all-reduce(f32[4,4]{0,1:T(4,128)S(1)} %pad_maximum_fusion.6), channel_id=1, replica_groups=mesh['gy'=8,'gz'=16] {'gy','gz'}, use_global_device_ids=true, to_apply=%region_10.11 | all-reduce | flops 16 | bytes 128 | tf_op jit(solution)/shard_map/psum | solution.py:108
  224.3 0.7 fusion.108
  234.5 2.7 fusion.20
  237.2 1.4 copy-done.3
  238.6 1.3 fusion.59
  239.9 10.0 %mul.449 = f32[2,4,8,4,64,4]{5,4,3,2,1,0:T(8,128)} reshape(f32[8,32,256]{2,1,0:T(8,128)S(1)} %broadcast_multiply_fusion) | data formatting | bytes 524288 | tf_op jit(solution)/shard_map/mul | solution.py:114
  250.0 4.2 %reduce_sum.125 = f32[2,8,64]{2,1,0:T(8,128)S(1)} reduce(f32[2,4,8,4,64,4]{5,4,3,2,1,0:T(8,128)} %mul.449, f32[]{:T(128)} %constant.72.clone.1), dimensions={1,3,5}, to_apply=%region_16.17 | reduce | flops 64512 | bytes 266244 | tf_op jit(solution)/shard_map/reduce_sum | solution.py:116
  254.2 6.5 %scatter_custom_fusion = f32[32768]{0:T(1024)} fusion(s32[1024]{0:T(1024)S(1)} %reshape.30, f32[1024]{0:T(1024)S(1)} %reshape.32, f32[]{:T(128)} %constant.72.clone.1), kind=kCustom, calls=%fused_computation.147 | custom fusion | flops 1024 | bytes 131076 | tf_op jit(solution)/shard_map/scatter-add | solution.py:123
  260.8 1.5 copy.109
  262.3 136.0 %all-reduce.7.cloned.1.call-done = f32[32768]{0:T(1024)} async-done(((f32[32768]{0:T(1024)}), f32[32768]{0:T(1024)}) %all-reduce.7.cloned.1.call-update) | async-done | bytes 131088
  398.3 1.3 dynamic-slice
  (124 shorter events, 8.7 us)
Async XLA Ops:
  7.2 391.1 %all-reduce.7.cloned.1.call-start = ((), (), s32[]{:S(2)}) async-start(), calls=%async_computation | async-start | bytes 262144
  7.2 2.2 copy-start.23
  10.0 7.3 %collective-permute-start = (f32[8,8,1,256]{3,0,2,1:T(8,128)S(1)}, f32[8,8,1,256]{3,0,2,1:T(8,128)S(1)}, u32[]{:S(2)}, u32[]{:S(2)}) collective-permute-start(f32[8,8,1,256]{3,0,2,1:T(8,128)S(1)} %get-tuple-element.17), channel_id=1, source_target_pairs={{0,16},{16,32},{32,48},{48,64},{64,80},{80,96},{96,112},{1,17},{17... | collective-permute-start | bytes 196616 | tf_op jit(solution)/shard_map/ppermute | solution.py:18
  14.5 5.6 %collective-permute-start.1 = (f32[8,8,1,256]{3,0,2,1:T(8,128)S(1)}, f32[8,8,1,256]{3,0,2,1:T(8,128)S(1)}, u32[]{:S(2)}, u32[]{:S(2)}) collective-permute-start(f32[8,8,1,256]{3,0,2,1:T(8,128)S(1)} %get-tuple-element.18), channel_id=1, source_target_pairs={{16,0},{32,16},{48,32},{64,48},{80,64},{96,80},{112,96},{17,1},{33... | collective-permute-start | bytes 196616 | tf_op jit(solution)/shard_map/ppermute | solution.py:21
  17.3 33.3 %copy-start.17 = (f32[8,32,256]{2,1,0:T(8,128)}, f32[8,32,256]{2,1,0:T(8,128)S(1)}, u32[]{:S(2)}) copy-start(f32[8,32,256]{2,1,0:T(8,128)S(1)} %get-tuple-element.37) | copy-start | bytes 786436
  24.6 8.6 %collective-permute-start.2 = (f32[8,8,34,1]{2,1,3,0:T(8,128)}, f32[8,8,34,1]{2,1,3,0:T(8,128)}, u32[]{:S(2)}, u32[]{:S(2)}) collective-permute-start(f32[8,8,34,1]{2,1,3,0:T(8,128)} %copy.72), channel_id=1, source_target_pairs={{0,1},{1,2},{2,3},{3,4},{4,5},{5,6},{6,7},{7,8},{8,9},{9,10},{10,1... | collective-permute-start | bytes 26120 | tf_op jit(solution)/shard_map/ppermute | solution.py:18
  31.1 5.0 %collective-permute-start.3 = (f32[8,8,34,1]{2,1,3,0:T(8,128)}, f32[8,8,34,1]{2,1,3,0:T(8,128)}, u32[]{:S(2)}, u32[]{:S(2)}) collective-permute-start(f32[8,8,34,1]{2,1,3,0:T(8,128)} %copy.73), channel_id=1, source_target_pairs={{1,0},{2,1},{3,2},{4,3},{5,4},{6,5},{7,6},{8,7},{9,8},{10,9},{11,1... | collective-permute-start | bytes 26120 | tf_op jit(solution)/shard_map/ppermute | solution.py:21
  45.3 0.9 copy-start.5
  45.5 0.7 copy-start.8
  45.6 1.6 copy-start
  45.6 1.7 copy-start.20
  45.7 4.9 %copy-start.11 = (f32[8,32,256]{2,1,0:T(8,128)}, f32[8,32,256]{2,1,0:T(8,128)S(1)}, u32[]{:S(2)}) copy-start(f32[8,32,256]{2,1,0:T(8,128)S(1)} %slice.290) | copy-start | bytes 786436
  45.9 4.8 %copy-start.14 = (f32[8,32,256]{2,1,0:T(8,128)}, f32[8,32,256]{2,1,0:T(8,128)S(1)}, u32[]{:S(2)}) copy-start(f32[8,32,256]{2,1,0:T(8,128)S(1)} %slice.291) | copy-start | bytes 786436
  46.1 7.7 %copy-start.24 = (f32[8,32,256]{2,1,0:T(8,128)}, f32[8,32,256]{2,1,0:T(8,128)S(1)}, u32[]{:S(2)}) copy-start(f32[8,32,256]{2,1,0:T(8,128)S(1)} %slice.292) | copy-start | bytes 786436
  46.2 7.7 %copy-start.27 = (f32[8,32,256]{2,1,0:T(8,128)}, f32[8,32,256]{2,1,0:T(8,128)S(1)}, u32[]{:S(2)}) copy-start(f32[8,32,256]{2,1,0:T(8,128)S(1)} %slice.293) | copy-start | bytes 786436
  50.7 3.2 copy-start.30
  50.7 3.2 copy-start.33
  58.7 5.2 %collective-permute-start.4 = (f32[5,8,1,256]{3,0,2,1:T(8,128)S(1)}, f32[5,8,1,256]{3,0,2,1:T(8,128)S(1)}, u32[]{:S(2)}, u32[]{:S(2)}) collective-permute-start(f32[5,8,1,256]{3,0,2,1:T(8,128)S(1)} %get-tuple-element.27), channel_id=1, source_target_pairs={{0,16},{16,32},{32,48},{48,64},{64,80},{80,96},{96,112},{1,17},{17... | collective-permute-start | bytes 122888 | tf_op jit(solution)/shard_map/ppermute | solution.py:18
  62.0 5.6 %collective-permute-start.5 = (f32[5,8,1,256]{3,0,2,1:T(8,128)S(1)}, f32[5,8,1,256]{3,0,2,1:T(8,128)S(1)}, u32[]{:S(2)}, u32[]{:S(2)}) collective-permute-start(f32[5,8,1,256]{3,0,2,1:T(8,128)S(1)} %get-tuple-element.28), channel_id=1, source_target_pairs={{16,0},{32,16},{48,32},{64,48},{80,64},{96,80},{112,96},{17,1},{33... | collective-permute-start | bytes 122888 | tf_op jit(solution)/shard_map/ppermute | solution.py:21
  71.7 7.3 %collective-permute-start.6 = (f32[5,8,34,1]{2,1,3,0:T(8,128)}, f32[5,8,34,1]{2,1,3,0:T(8,128)}, u32[]{:S(2)}, u32[]{:S(2)}) collective-permute-start(f32[5,8,34,1]{2,1,3,0:T(8,128)} %copy.85), channel_id=1, source_target_pairs={{0,1},{1,2},{2,3},{3,4},{4,5},{5,6},{6,7},{7,8},{8,9},{9,10},{10,1... | collective-permute-start | bytes 16328 | tf_op jit(solution)/shard_map/ppermute | solution.py:18
  77.7 4.8 %collective-permute-start.7 = (f32[5,8,34,1]{2,1,3,0:T(8,128)}, f32[5,8,34,1]{2,1,3,0:T(8,128)}, u32[]{:S(2)}, u32[]{:S(2)}) collective-permute-start(f32[5,8,34,1]{2,1,3,0:T(8,128)} %copy.86), channel_id=1, source_target_pairs={{1,0},{2,1},{3,2},{4,3},{5,4},{6,5},{7,6},{8,7},{9,8},{10,9},{11,1... | collective-permute-start | bytes 16328 | tf_op jit(solution)/shard_map/ppermute | solution.py:21
  84.8 3.9 copy-start.6
  84.8 3.9 copy-start.9
  84.8 3.9 copy-start.21
  88.7 2.9 copy-start.12
  88.7 2.9 copy-start.15
  88.7 2.9 copy-start.18
  91.6 2.8 copy-start.25
  91.6 2.8 copy-start.28
  91.6 2.8 copy-start.31
  91.6 2.8 copy-start.34
  97.8 9.2 %copy-start.1 = (f32[5,8,32,256]{3,0,2,1:T(8,128)}, f32[5,8,32,256]{3,0,2,1:T(8,128)S(1)}, u32[]{:S(2)}) copy-start(f32[5,8,32,256]{3,0,2,1:T(8,128)S(1)} %bitcast_add_fusion.3) | copy-start | bytes 3932164
  97.9 5.2 %collective-permute-start.8 = (f32[5,8,1,256]{3,0,2,1:T(8,128)S(1)}, f32[5,8,1,256]{3,0,2,1:T(8,128)S(1)}, u32[]{:S(2)}, u32[]{:S(2)}) collective-permute-start(f32[5,8,1,256]{3,0,2,1:T(8,128)S(1)} %get-tuple-element.25), channel_id=1, source_target_pairs={{0,16},{16,32},{32,48},{48,64},{64,80},{80,96},{96,112},{1,17},{17... | collective-permute-start | bytes 122888 | tf_op jit(solution)/shard_map/ppermute | solution.py:18
  101.2 5.6 %collective-permute-start.9 = (f32[5,8,1,256]{3,0,2,1:T(8,128)S(1)}, f32[5,8,1,256]{3,0,2,1:T(8,128)S(1)}, u32[]{:S(2)}, u32[]{:S(2)}) collective-permute-start(f32[5,8,1,256]{3,0,2,1:T(8,128)S(1)} %get-tuple-element.26), channel_id=1, source_target_pairs={{16,0},{32,16},{48,32},{64,48},{80,64},{96,80},{112,96},{17,1},{33... | collective-permute-start | bytes 122888 | tf_op jit(solution)/shard_map/ppermute | solution.py:21
  110.9 8.5 %collective-permute-start.10 = (f32[5,8,34,1]{2,1,3,0:T(8,128)}, f32[5,8,34,1]{2,1,3,0:T(8,128)}, u32[]{:S(2)}, u32[]{:S(2)}) collective-permute-start(f32[5,8,34,1]{2,1,3,0:T(8,128)} %copy.93), channel_id=1, source_target_pairs={{0,1},{1,2},{2,3},{3,4},{4,5},{5,6},{6,7},{7,8},{8,9},{9,10},{10,1... | collective-permute-start | bytes 16328 | tf_op jit(solution)/shard_map/ppermute | solution.py:18
  116.7 5.0 %collective-permute-start.11 = (f32[5,8,34,1]{2,1,3,0:T(8,128)}, f32[5,8,34,1]{2,1,3,0:T(8,128)}, u32[]{:S(2)}, u32[]{:S(2)}) collective-permute-start(f32[5,8,34,1]{2,1,3,0:T(8,128)} %copy.94), channel_id=1, source_target_pairs={{1,0},{2,1},{3,2},{4,3},{5,4},{6,5},{7,6},{8,7},{9,8},{10,9},{11,1... | collective-permute-start | bytes 16328 | tf_op jit(solution)/shard_map/ppermute | solution.py:21
  124.0 4.3 %copy-start.2 = (f32[5,8,32,256]{3,0,2,1:T(8,128)S(1)}, f32[5,8,32,256]{3,0,2,1:T(8,128)}, u32[]{:S(2)}) copy-start(f32[5,8,32,256]{3,0,2,1:T(8,128)} %copy-done.1) | copy-start | bytes 3932164
  124.0 4.3 %copy-start.7 = (f32[8,32,256]{2,1,0:T(8,128)S(1)}, f32[8,32,256]{2,1,0:T(8,128)}, u32[]{:S(2)}) copy-start(f32[8,32,256]{2,1,0:T(8,128)} %copy-done.5) | copy-start | bytes 786436
  124.0 4.3 %copy-start.10 = (f32[8,32,256]{2,1,0:T(8,128)S(1)}, f32[8,32,256]{2,1,0:T(8,128)}, u32[]{:S(2)}) copy-start(f32[8,32,256]{2,1,0:T(8,128)} %copy-done.8) | copy-start | bytes 786436
  124.0 4.3 %copy-start.22 = (f32[8,32,256]{2,1,0:T(8,128)S(1)}, f32[8,32,256]{2,1,0:T(8,128)}, u32[]{:S(2)}) copy-start(f32[8,32,256]{2,1,0:T(8,128)} %get-tuple-element.36) | copy-start | bytes 786436
  128.3 3.0 copy-start.13
  128.3 3.0 copy-start.16
  128.3 3.0 copy-start.19
  131.3 3.0 copy-start.26
  131.3 3.0 copy-start.29
  131.3 3.0 copy-start.32
  131.3 3.0 copy-start.35
  134.2 17.4 %copy-start.37 = (s32[2,8,64]{2,1,0:T(8,128)S(1)}, s32[2,8,64]{2,1,0:T(8,128)}, u32[]{:S(2)}) copy-start(s32[2,8,64]{2,1,0:T(8,128)} %param.11) | copy-start | bytes 12292
  234.5 4.1 %copy-start.36 = (f32[3,8,32,256]{3,2,1,0:T(8,128)S(1)}, f32[3,8,32,256]{3,2,1,0:T(8,128)}, u32[]{:S(2)}) copy-start(f32[3,8,32,256]{3,2,1,0:T(8,128)} %param.10) | copy-start | bytes 2359300
  237.2 1.4 copy-start.3
  250.0 10.9 %copy-start.4 = (f32[5,8,32,256]{3,0,2,1:T(8,128)S(1)}, f32[5,8,32,256]{3,0,2,1:T(8,128)}, u32[]{:S(2)}) copy-start(f32[5,8,32,256]{3,0,2,1:T(8,128)} %copy-done.3) | copy-start | bytes 3932164
Sparse Core Ops, SparseCore 0:
  260.9 137.3 all-reduce.6
where the time goes:
time: 413 us; the launch traced here: 407 us
  waiting for transfers between devices  148 us (36%)
  blocking collectives  68.2 us (17%)
  local copies, waits for them, and re-layouts  54.8 us (13%)
  other arithmetic  45.7 us (11%)
  matrix products  32.9 us (8%)
  starting transfers between devices  32.6 us (8%)
  between operations  24.6 us (6%)
    unnamed x2, waiting for transfers between devices  136 us
    psum x1, blocking collectives, local(): gram = lax.psum(gram_local, ('gy', 'gz'))  68.2 us
    dot_general x9, matrix products, transpose_sweep(): jnp.einsum('ij,ixyz->jxyz', coupling[direction], flux, precision=lax.Prec...  32.6 us
    ppermute x6, starting transfers between devices, padded(): lax.ppermute(lax.slice_in_dim(block, block.shape[dim] - width, None, axis...  22.5 us
    concatenate x6, other arithmetic, padded(): block = jnp.concatenate([low, block, high], axis=dim)  12.7 us
    slice x8, local copies, waits for them, and re-layouts, padded(): lax.slice_in_dim(block, block.shape[dim] - width, None, axis=dim)  11.9 us
    ppermute x6, waiting for transfers between devices, padded(): lax.ppermute(lax.slice_in_dim(block, 0, width, axis=dim), axis, backward)  11.8 us
    another operation x5, other arithmetic, gram_matrix(): return jnp.stack(rows_list)  10.4 us
  transfers between devices with their start and end apart: 13, of which 6 were waited for; matrix products, arithmetic and copies ran while one was open for 4% of the time, Pallas kernels for 0%

commit v1 on v0

v1 whole, which is shorter than its diff:
```python
import functools

import jax
import jax.numpy as jnp
from jax import lax
from jax.experimental import pallas as pl
from jax.experimental.pallas import tpu as pltpu
from jax.sharding import PartitionSpec as P

PENALTY = 1.0
COURANT = 0.3
VARS = 5
SLOTS = 16
MESH = pl.DeviceIdType.MESH
F32 = jnp.float32
BF16 = jnp.bfloat16


def pieces(value):
    high = value.astype(BF16)
    rest = value - high.astype(F32)
    mid = rest.astype(BF16)
    low = (rest - mid.astype(F32)).astype(BF16)
    return high, mid, low


def dot(a, b):
    return jnp.dot(a, b, preferred_element_type=F32)


def dot_nt(a, b):
    return lax.dot_general(a, b, (((1,), (1,)), ((), ())), preferred_element_type=F32)


def iota(shape, axis):
    return lax.broadcasted_iota(jnp.int32, shape, axis)


def fold(product):
    rows = product[0:8] + product[8:16] + product[16:24] + product[24:32]
    return rows[:, 0:128] + rows[:, 128:256]


def solve(gram):
    low = [[None] * 4 for _ in range(4)]
    for col in range(4):
        diag = gram[col][col]
        for inner in range(col):
            diag = diag - low[col][inner] * low[col][inner]
        low[col][col] = jnp.sqrt(diag)
        for row in range(col + 1, 4):
            value = gram[row][col]
            for inner in range(col):
                value = value - low[row][inner] * low[col][inner]
            low[row][col] = value / low[col][col]
    zero = jnp.zeros_like(gram[0][0])
    upper = [[low[c][r] if c >= r else None for c in range(4)] for r in range(4)]

    def add(a, b):
        return b if a is None else (a if b is None else a + b)

    hess = [[add(upper[r][c + 1], upper[r][c]) for c in range(3)] for r in range(4)]

    def inner_sum(terms):
        total = None
        for a, b in terms:
            if a is not None and b is not None:
                total = add(total, a * b)
        return zero if total is None else total

    normal = [[inner_sum([(hess[r][a], hess[r][b]) for r in range(4)]) for b in range(3)] for a in range(3)]
    target = [inner_sum([(hess[r][a], upper[r][0]) for r in range(4)]) for a in range(3)]
    fac = [[None] * 3 for _ in range(3)]
    for col in range(3):
        diag = normal[col][col]
        for inner in range(col):
            diag = diag - fac[col][inner] * fac[col][inner]
        fac[col][col] = jnp.sqrt(diag)
        for row in range(col + 1, 3):
            value = normal[row][col]
            for inner in range(col):
                value = value - fac[row][inner] * fac[col][inner]
            fac[row][col] = value / fac[col][col]
    forward = []
    for place in range(3):
        value = target[place]
        for inner in range(place):
            value = value - fac[place][inner] * forward[inner]
        forward.append(value / fac[place][place])
    backward = [None] * 3
    for place in reversed(range(3)):
        value = forward[place]
        for inner in range(place + 1, 3):
            value = value - fac[inner][place] * backward[inner]
        backward[place] = value / fac[place][place]
    return backward


def kernel(ny, nz, per_owner,
           rs_hbm, sp_hbm, po_hbm, cp, mo_hbm, ids_ref,
           adj_hbm, sens_ref,
           b0, b1, b2, b3, sp, po, mo, wmat, wz, w, cf, sface,
           ysend, yrecv, zsend, zrecv,
           owner_hot, rank_hot, local_row, dsend, recv1, turned, recv2,
           gsend, grecv1, gsend2, grecv2,
           in_sem, out_sem, ysend_sem, yrecv_sem, zsend_sem, zrecv_sem,
           a1_send, a1_recv, a2_send, a2_recv, g1_send, g1_recv, g2_send, g2_recv):
    gy = lax.axis_index("gy")
    gz = lax.axis_index("gz")

    def gy_at(delta):
        return lax.rem(gy + (delta + ny), ny)

    def gz_at(delta):
        return lax.rem(gz + (delta + nz), nz)

    barrier = pltpu.get_barrier_semaphore()
    for delta in range(1, ny):
        pl.semaphore_signal(barrier, inc=1, device_id={"gy": gy_at(delta)}, device_id_type=MESH)
    for delta in range(1, nz):
        pl.semaphore_signal(barrier, inc=1, device_id={"gz": gz_at(delta)}, device_id_type=MESH)

    loads = [pltpu.make_async_copy(src, dst, in_sem.at[place]) for place, (src, dst) in enumerate(
        [(sp_hbm, sp), (rs_hbm, b0), (po_hbm, po), (mo_hbm, mo)])]
    for load in loads:
        load.start()

    basis = [b0, b1, b2, b3]

    lane = iota((16, 256), 1)
    row = iota((16, 256), 0)
    group = lane >> 4
    piece = jnp.where(group >= 10, 2, jnp.where(group >= 5, 1, 0))
    which = group - 5 * piece
    same = (lane & 15) == row
    for d in range(3):
        for j in range(VARS):
            value = jnp.zeros((16, 256), F32)
            for i in range(VARS):
                value = jnp.where(which == i, COURANT * cp[d, i, j], value)
            high = value.astype(BF16).astype(F32)
            value = jnp.where(same, jnp.where(piece == 2, value - high, high), 0.0)
            at = (d * VARS + j) * 16
            wmat[at:at + 16, :] = value[:, 0:240].astype(BF16)
    lane = iota((8, 128), 1)
    row = iota((8, 128), 0)
    for i in range(VARS):
        value = jnp.zeros((8, 128), F32)
        for j in range(VARS):
            value = jnp.where((lane >> 3) == j, -COURANT * cp[2, i, j], value)
        wz[8 * i:8 * i + 8, :] = jnp.where((lane & 7) == row, value, 0.0)
    wz[40:128, :] = jnp.zeros((88, 128), F32)

    ids = jnp.concatenate([ids_ref[0], ids_ref[1]], axis=1)
    owners = lax.div(ids, per_owner)
    local_row[...] = (ids - owners * per_owner + 1).astype(F32)
    tri = jnp.where(iota((128, 128), 0) < iota((128, 128), 1), 1.0, 0.0).astype(BF16)
    ones = jnp.ones((128, 128), BF16)
    number = ny * nz
    sub = iota((number, 128), 0)
    before = jnp.zeros((number, 128), F32)
    for p in range(8):
        hot = jnp.where(sub == owners[p:p + 1, :], 1.0, 0.0)
        hot16 = hot.astype(BF16)
        count = dot(hot16, tri) + dot(before.astype(BF16), ones)
        before = before + hot
        owner_hot[:, p * 128:(p + 1) * 128] = hot16
        rank = jnp.sum(hot * count, axis=0, keepdims=True)
        rank_hot[:, p * 128:(p + 1) * 128] = jnp.where(rank == iota((SLOTS, 128), 0).astype(F32), 1.0, 0.0)

    loads[0].wait()
    keep_low = jnp.where(gy > 0, 1.0, 0.0)
    keep_high = jnp.where(gy < ny - 1, 1.0, 0.0)
    keep_near = jnp.where(gz > 0, 1.0, 0.0)
    keep_far = jnp.where(gz < nz - 1, 1.0, 0.0)

    lanes = iota((32, 128), 1)
    near = jnp.zeros((32, 128), F32)
    far = jnp.zeros((32, 128), F32)
    for x in range(8):
        at_near = sp[2, x, :, 0:128]
        at_far = sp[2, x, :, 128:256]
        for i in range(VARS):
            s = i * 8 + x
            near = jnp.where(lanes == s, pltpu.roll(at_near, s, axis=1) if s else at_near, near)
            far = jnp.where(lanes == s, pltpu.roll(at_far, s + 1, axis=1), far)
    sface[0] = jnp.maximum(near, 0.0) * keep_near
    sface[1] = jnp.maximum(-far, 0.0) * keep_far

    def pack_z(k, fix):
        b = basis[k]
        near = jnp.zeros((32, 128), F32)
        far = jnp.zeros((32, 128), F32)
        if fix:
            from_near = zrecv[k - 1, 0]
            from_far = zrecv[k - 1, 1]
        for i in range(VARS):
            for x in range(8):
                s = i * 8 + x
                at_near = b[i, x, :, 0:128]
                at_far = b[i, x, :, 128:256]
                if fix:
                    at_near = at_near + jnp.where(lanes == 0, pltpu.roll(from_near, (128 - s) % 128, axis=1), 0.0)
                    at_far = at_far + jnp.where(lanes == 127, pltpu.roll(from_far, 127 - s, axis=1), 0.0)
                    b[i, x, :, 0:128] = at_near
                    b[i, x, :, 128:256] = at_far
                if k < 3:
                    near = jnp.where(lanes == s, pltpu.roll(at_near, s, axis=1) if s else at_near, near)
                    far = jnp.where(lanes == s, pltpu.roll(at_far, s + 1, axis=1), far)
        if k < 3:
            both = jnp.concatenate([near * sface[0], far * sface[1]], axis=0)
            out = jnp.dot(both, wz[...], preferred_element_type=F32, precision=lax.Precision.HIGHEST)
            zsend[k, 0] = out[0:32]
            zsend[k, 1] = out[32:64]

    def fix_y(k):
        b = basis[k]
        for i in range(VARS):
            for x in range(8):
                b[i, x, 0:1, :] = b[i, x, 0:1, :] + yrecv[k - 1, 0, i, x:x + 1, :]
                b[i, x, 31:32, :] = b[i, x, 31:32, :] + yrecv[k - 1, 1, i, x:x + 1, :]

    def pack_y(k):
        b = basis[k]
        for side, y in ((0, 0), (1, 31)):
            speed = sp[1, :, y, :]
            speed = jnp.maximum(speed, 0.0) * keep_low if side == 0 else jnp.maximum(-speed, 0.0) * keep_high
            faces = [b[i, :, y, :] * speed for i in range(VARS)]
            for j in range(VARS):
                total = faces[0] * (-COURANT * cp[1, 0, j])
                for i in range(1, VARS):
                    total = total + faces[i] * (-COURANT * cp[1, i, j])
                ysend[k, side, j] = total

    def halo_copies(k):
        copies = []
        for side, delta in ((0, -1), (1, 1)):
            copies.append(pltpu.make_async_remote_copy(
                src_ref=ysend.at[k, side], dst_ref=yrecv.at[k, 1 - side],
                send_sem=ysend_sem.at[k, side], recv_sem=yrecv_sem.at[k, 1 - side],
                device_id={"gy": gy_at(delta)}, device_id_type=MESH))
            copies.append(pltpu.make_async_remote_copy(
                src_ref=zsend.at[k, side], dst_ref=zrecv.at[k, 1 - side],
                send_sem=zsend_sem.at[k, side], recv_sem=zrecv_sem.at[k, 1 - side],
                device_id={"gz": gz_at(delta)}, device_id_type=MESH))
        return copies

    def couple(k, x):
        for h in (0, 16):
            high, low = [], []
            for i in range(VARS):
                v = basis[k][i, x, h:h + 16, :]
                top = v.astype(BF16)
                high.append(top)
                low.append((v - top.astype(F32)).astype(BF16))
            out = dot(wmat[...], jnp.concatenate(high + low + high, axis=0))
            for place in range(3 * VARS):
                w[place, x, h:h + 16, :] = out[place * 16:place * 16 + 16]

    def sweep(k):
        couple(k, 0)

        def body(x, sums):
            after = jnp.minimum(x + 1, 7)
            prior = jnp.maximum(x - 1, 0)
            couple(k, after)
            sums = list(sums)
            for j in range(VARS):
                v = basis[k][j, x]
                for l in range(k + 1):
                    sums[l] = sums[l] + fold(v * basis[l][j, x])
                acc = po[x] * v
                wx = w[j, x]
                wy = w[VARS + j, x]
                wv = w[2 * VARS + j, x]
                acc = acc + cf[0, x] * wx + cf[3, x] * wy + cf[6, x] * wv
                acc = acc + cf[4, x] * pltpu.roll(wy, 31, axis=0) + cf[5, x] * pltpu.roll(wy, 1, axis=0)
                acc = acc + cf[7, x] * pltpu.roll(wv, 255, axis=1) + cf[8, x] * pltpu.roll(wv, 1, axis=1)
                acc = acc + cf[1, x] * w[j, after] + cf[2, x] * w[j, prior]
                basis[k + 1][j, x] = acc
            return tuple(sums)

        return lax.fori_loop(0, 8, body, tuple(jnp.zeros((8, 128), F32) for _ in range(k + 1)))

    gram = [[None] * 4 for _ in range(4)]

    loads[1].wait()
    pack_y(0)
    pack_z(0, False)
    pl.semaphore_wait(barrier, (ny - 1) + (nz - 1))
    halos = halo_copies(0)
    for copy in halos:
        copy.start()

    row = iota((32, 256), 0)
    lane = iota((32, 256), 1)

    def coefficients(x, carry):
        after = jnp.minimum(x + 1, 7)
        prior = jnp.maximum(x - 1, 0)
        cf[0, x] = jnp.abs(sp[0, x])
        cf[1, x] = -jnp.maximum(sp[0, after], 0.0) * jnp.where(x < 7, 1.0, 0.0)
        cf[2, x] = -jnp.maximum(-sp[0, prior], 0.0) * jnp.where(x > 0, 1.0, 0.0)
        s = sp[1, x]
        cf[3, x] = jnp.abs(s)
        cf[4, x] = jnp.where(row == 31, 0.0, -jnp.maximum(pltpu.roll(s, 31, axis=0), 0.0))
        cf[5, x] = jnp.where(row == 0, 0.0, -jnp.maximum(-pltpu.roll(s, 1, axis=0), 0.0))
        s = sp[2, x]
        cf[6, x] = jnp.abs(s)
        cf[7, x] = jnp.where(lane == 255, 0.0, -jnp.maximum(pltpu.roll(s, 255, axis=1), 0.0))
        cf[8, x] = jnp.where(lane == 0, 0.0, -jnp.maximum(-pltpu.roll(s, 1, axis=1), 0.0))
        return carry

    lax.fori_loop(0, 8, coefficients, 0)
    loads[2].wait()

    for k in range(2):
        sums = sweep(k)
        for l in range(k + 1):
            gram[l][k] = sums[l]
        for copy in halos:
            copy.wait()
        fix_y(k + 1)
        pack_z(k + 1, True)
        pack_y(k + 1)
        halos = halo_copies(k + 1)
        for copy in halos:
            copy.start()

    loads[3].wait()
    low8 = iota((16, 192), 0)
    col = iota((16, 192), 1)
    within = jnp.where(col >= 96, col - 96, col) & 31
    half = jnp.where(col >= 96, 1, 0)
    ysel = jnp.where((low8 >> 3 == half) & ((low8 & 7) == (within >> 2)), 1.0, 0.0).astype(BF16)
    zrow = iota((512, 128), 0)
    zsel = jnp.where(((zrow & 255) >> 2) + (zrow >> 8) * 64 == iota((512, 128), 1), 1.0, 0.0).astype(BF16)
    parts = []
    for k in range(3):
        stack = []
        for half_x in range(2):
            total = None
            for x in range(4 * half_x, 4 * half_x + 4):
                for i in range(3):
                    term = basis[k][1 + i, x] * mo[i, x]
                    total = term if total is None else total + term
            stack.extend(pieces(total))
        t = dot(ysel, jnp.concatenate(stack, axis=0))
        for part in pieces(jnp.concatenate([t[0:8], t[8:16]], axis=1)):
            parts.append(part.astype(F32))
    t = dot(jnp.concatenate(parts, axis=0).astype(BF16), zsel)
    values = [-PENALTY * (t[24 * k:24 * k + 8] + t[24 * k + 8:24 * k + 16] + t[24 * k + 16:24 * k + 24])
              for k in range(3)]
    empty = jnp.zeros((SLOTS, 128), F32)
    chunks = [[], [], []]
    for p in range(8):
        hot = rank_hot[:, p * 128:(p + 1) * 128]
        spread = [(hot * local_row[p:p + 1, :]).astype(BF16).astype(F32), empty, empty]
        rows = [[spread[q]] for q in range(3)]
        for k in range(3):
            for q, part in enumerate(pieces(hot * values[k][p:p + 1, :])):
                rows[q].append(part.astype(F32))
        for q in range(3):
            chunks[q].append(jnp.concatenate(rows[q] + [empty] * 4, axis=0).astype(BF16))
    total = None
    for q in range(3):
        term = dot_nt(owner_hot[...], jnp.concatenate(chunks[q], axis=1))
        total = term if total is None else total + term
    dsend[...] = total.reshape(ny, nz, 128)

    def a1_copy(delta):
        return pltpu.make_async_remote_copy(
            src_ref=dsend.at[gy_at(delta)], dst_ref=recv1.at[delta],
            send_sem=a1_send.at[delta], recv_sem=a1_recv.at[delta],
            device_id={"gy": gy_at(delta)}, device_id_type=MESH)

    first = [a1_copy(delta) for delta in range(1, ny)]
    for copy in first:
        copy.start()
    recv1[0] = dsend[gy]

    sums = sweep(2)
    for l in range(3):
        gram[l][2] = sums[l]
    for copy in halos:
        copy.wait()
    fix_y(3)
    pack_z(3, True)

    def last(x, sums):
        sums = list(sums)
        for j in range(VARS):
            v = b3[j, x]
            for l in range(4):
                sums[l] = sums[l] + fold(v * basis[l][j, x])
        return tuple(sums)

    sums = lax.fori_loop(0, 8, last, tuple(jnp.zeros((8, 128), F32) for _ in range(4)))
    for l in range(4):
        gram[l][3] = sums[l]

    entries = [(l, k) for k in range(4) for l in range(k + 1)]
    lane = iota((8, 128), 1)
    packed = jnp.zeros((8, 128), F32)
    for e, (l, k) in enumerate(entries):
        value = gram[l][k]
        for shift in (64, 32, 16, 8):
            value = value + pltpu.roll(value, shift, axis=1)
        packed = jnp.where((lane >> 3) == e, value, packed)
    own = jnp.sum(packed, axis=0, keepdims=True)
    gsend[...] = own

    def g1_copy(delta):
        return pltpu.make_async_remote_copy(
            src_ref=gsend, dst_ref=grecv1.at[delta],
            send_sem=g1_send.at[delta], recv_sem=g1_recv.at[delta],
            device_id={"gy": gy_at(delta)}, device_id_type=MESH)

    gram1 = [g1_copy(delta) for delta in range(1, ny)]
    for copy in gram1:
        copy.start()

    for copy in first:
        copy.wait()
    for g in range(nz):
        turned[g] = recv1[:, g, :]

    def a2_copy(delta):
        return pltpu.make_async_remote_copy(
            src_ref=turned.at[gz_at(delta)], dst_ref=recv2.at[delta],
            send_sem=a2_send.at[delta], recv_sem=a2_recv.at[delta],
            device_id={"gz": gz_at(delta)}, device_id_type=MESH)

    second = [a2_copy(delta) for delta in range(1, nz)]
    for copy in second:
        copy.start()
    recv2[0] = turned[gz]

    for copy in gram1:
        copy.wait()
    own = gsend[...]
    for delta in range(1, ny):
        own = own + grecv1[delta]
    gsend2[...] = own

    def g2_copy(delta):
        return pltpu.make_async_remote_copy(
            src_ref=gsend2, dst_ref=grecv2.at[delta],
            send_sem=g2_send.at[delta], recv_sem=g2_recv.at[delta],
            device_id={"gz": gz_at(delta)}, device_id_type=MESH)

    gram2 = [g2_copy(delta) for delta in range(1, nz)]
    for copy in gram2:
        copy.start()

    for copy in second:
        copy.wait()
    bins = iota((8, per_owner), 1).astype(F32) + 1.0

    def collect(t, sums):
        tile = recv2[t]
        sums = list(sums)
        for r in range(SLOTS):
            hit = tile[:, r:r + 1] == bins
            for k in range(3):
                at = SLOTS * (k + 1) + r
                sums[k] = sums[k] + jnp.where(hit, tile[:, at:at + 1], 0.0)
        return tuple(sums)

    sums = lax.fori_loop(0, nz, collect, tuple(jnp.zeros((8, per_owner), F32) for _ in range(3)))
    bin_sums = [jnp.sum(value, axis=0, keepdims=True) for value in sums]

    for copy in gram2:
        copy.wait()
    own = gsend2[...]
    for delta in range(1, nz):
        own = own + grecv2[delta]
    for shift in (4, 2, 1):
        own = own + pltpu.roll(own, shift, axis=1)
    own = jnp.broadcast_to(own, (8, 128))
    splat = {}
    for e, (l, k) in enumerate(entries):
        splat[l, k] = jnp.broadcast_to(own[:, 8 * e + 7:8 * e + 8], (8, 128))
    coeffs = solve([[splat[min(a, b), max(a, b)] for b in range(4)] for a in range(4)])

    sens = None
    for k in range(3):
        c = coeffs[k][0:1]
        term = bin_sums[k] * jnp.concatenate([c] * (per_owner // 128), axis=1)
        sens = term if sens is None else sens + term
    sens_ref[...] = sens

    wide = [jnp.concatenate([jnp.concatenate([c, c], axis=1)] * 4, axis=0) for c in coeffs]
    stores = []
    for j in range(VARS):
        def combine(x, carry):
            b0[j, x] = wide[0] * b0[j, x] + wide[1] * b1[j, x] + wide[2] * b2[j, x]
            return carry
        lax.fori_loop(0, 8, combine, 0)
        store = pltpu.make_async_copy(b0.at[j], adj_hbm.at[j], out_sem.at[j])
        store.start()
        stores.append(store)
    for store in stores:
        store.wait()


def local(right_side, speeds, porosity, coupling, momentum, design_ids):
    ny = lax.axis_size("gy")
    nz = lax.axis_size("gz")
    _, nx, cy, cz = right_side.shape
    per_owner = design_ids.size // 4
    field = (VARS, nx, cy, cz)
    dma = pltpu.SemaphoreType.DMA
    any_spec = pl.BlockSpec(memory_space=pl.ANY)
    vmem_spec = pl.BlockSpec(memory_space=pltpu.VMEM)
    adjoint, sensitivity = pl.pallas_call(
        functools.partial(kernel, ny, nz, per_owner),
        out_shape=[jax.ShapeDtypeStruct(field, F32), jax.ShapeDtypeStruct((1, per_owner), F32)],
        in_specs=[any_spec, any_spec, any_spec, pl.BlockSpec(memory_space=pltpu.SMEM), any_spec, vmem_spec],
        out_specs=[any_spec, vmem_spec],
        scratch_shapes=[
            pltpu.VMEM(field, F32), pltpu.VMEM(field, F32), pltpu.VMEM(field, F32), pltpu.VMEM(field, F32),
            pltpu.VMEM((3, nx, cy, cz), F32),
            pltpu.VMEM((nx, cy, cz), F32),
            pltpu.VMEM((3, nx, cy, cz), F32),
            pltpu.VMEM((240, 240), BF16),
            pltpu.VMEM((128, 128), F32),
            pltpu.VMEM((3 * VARS, nx, cy, cz), F32),
            pltpu.VMEM((9, nx, cy, cz), F32),
            pltpu.VMEM((2, 32, 128), F32),
            pltpu.VMEM((3, 2, VARS, nx, cz), F32),
            pltpu.VMEM((3, 2, VARS, nx, cz), F32),
            pltpu.VMEM((3, 2, 32, 128), F32),
            pltpu.VMEM((3, 2, 32, 128), F32),
            pltpu.VMEM((ny * nz, 1024), BF16),
            pltpu.VMEM((SLOTS, 1024), F32),
            pltpu.VMEM((8, 128), F32),
            pltpu.VMEM((ny, nz, 128), F32),
            pltpu.VMEM((ny, nz, 128), F32),
            pltpu.VMEM((nz, ny, 128), F32),
            pltpu.VMEM((nz, ny, 128), F32),
            pltpu.VMEM((1, 128), F32),
            pltpu.VMEM((ny, 1, 128), F32),
            pltpu.VMEM((1, 128), F32),
            pltpu.VMEM((nz, 1, 128), F32),
            dma((4,)), dma((VARS,)),
            dma((3, 2)), dma((3, 2)), dma((3, 2)), dma((3, 2)),
            dma((ny,)), dma((ny,)), dma((nz,)), dma((nz,)),
            dma((ny,)), dma((ny,)), dma((nz,)), dma((nz,)),
        ],
        compiler_params=pltpu.CompilerParams(
            collective_id=0, has_side_effects=True, vmem_limit_bytes=48 * 1024 * 1024),
    )(right_side, speeds, porosity, coupling, momentum, design_ids)
    return adjoint, sensitivity.reshape(per_owner)


def solution(mesh):
    in_specs = (
        P(None, None, "gy", "gz"),
        P(None, None, "gy", "gz"),
        P(None, "gy", "gz"),
        P(),
        P(None, None, "gy", "gz"),
        P(None, "gy", "gz"),
    )
    out_specs = (P(None, None, "gy", "gz"), P(("gy", "gz")))
    return jax.shard_map(local, mesh=mesh, in_specs=in_specs, out_specs=out_specs, check_vma=False)
```

time: 413 us -> 44.7 us (0.11); the launches traced: 407 us -> 44.3 us
  waiting for transfers between devices: 148 us -> 0 us
  blocking collectives: 68.2 us -> 0 us
  local copies, waits for them, and re-layouts: 54.8 us -> 7.55 us
  other arithmetic: 45.7 us -> 0 us
  Pallas kernels: 0 us -> 36.1 us
  matrix products: 32.9 us -> 0 us
  starting transfers between devices: 32.6 us -> 0 us
  between operations: 24.6 us -> 0.64 us
    unnamed x2 -> x0, waiting for transfers between devices: 136 us -> none
    psum x1 -> x0, blocking collectives: 68.2 us -> none  [local(): gram = lax.psum(gram_local, ('gy', 'gz'))]
    pallas_call x0 -> x1, Pallas kernels: none -> 36.1 us  [local(): pl.pallas_call(functools.partial(kernel, ny, nz, per_owner), out_shape=[j...]
    dot_general x11 -> x0, matrix products: 32.9 us -> none  [the longest x9 32.6 us: transpose_sweep(): jnp.einsum('ij,ixyz->jxyz', coupling[direction], flux, precision=lax.Prec...]
    ppermute x12 -> x0, starting transfers between devices: 32.5 us -> none  [the longest x6 22.5 us: padded(): lax.ppermute(lax.slice_in_dim(block, block.shape[dim] - width, None, axis...]
    slice x21 -> x0, local copies, waits for them, and re-layouts: 21.9 us -> none  [the longest x8 11.9 us: padded(): lax.slice_in_dim(block, block.shape[dim] - width, None, axis=dim)]
    ppermute x6 -> x0, local copies, waits for them, and re-layouts: 13.7 us -> none  [the longest x3 6.88 us: padded(): lax.ppermute(lax.slice_in_dim(block, block.shape[dim] - width, None, axis...]
    concatenate x6 -> x0, other arithmetic: 12.7 us -> none  [padded(): block = jnp.concatenate([low, block, high], axis=dim)]
  transfers between devices with their start and end apart: 13 -> 0, of which waited for: 6 -> 0; matrix products, arithmetic and copies ran while one was open for 4% -> 0% of each run, Pallas kernels for 0% -> 0%
where the time goes in v1:
time: 44.7 us; the launch traced here: 44.3 us
  Pallas kernels  36.1 us (81%)
  local copies, waits for them, and re-layouts  7.55 us (17%)
  between operations  0.64 us (1%)
    pallas_call x1, Pallas kernels, local(): pl.pallas_call(functools.partial(kernel, ny, nz, per_owner), out_shape=[j...  36.1 us
    unnamed x13, local copies, waits for them, and re-layouts  7.55 us

profile of v1, /device:TPU:1, one launch (start us, length us, event | category | flops | bytes accessed | tf_op | source)
XLA Modules:
  0.0 44.3 jit_solution(6716734868572937194)
XLA Ops:
  0.6 0.7 %copy.8.cp = f32[3,5,5]{2,1,0:T(8,128)S(1)} copy(f32[3,5,5]{2,0,1:T(4,128)} %param.9) | data formatting | bytes 600 | tf_op args[3]
  1.3 0.0 copy-start
  1.3 1.3 %copy-done = f32[5,8,32,256]{3,2,1,0:T(8,128)S(1)} copy-done((f32[5,8,32,256]{3,2,1,0:T(8,128)S(1)}, f32[5,8,32,256]{3,2,1,0:T(8,128)}, u32[]{:S(2)}) %copy-start) | copy-done | bytes 1310744
  2.7 0.0 copy-start.1
  2.7 1.1 %copy-done.1 = f32[3,8,32,256]{3,2,1,0:T(8,128)S(1)} copy-done((f32[3,8,32,256]{3,2,1,0:T(8,128)S(1)}, f32[3,8,32,256]{3,2,1,0:T(8,128)}, u32[]{:S(2)}) %copy-start.1) | copy-done | bytes 786456
  3.8 0.0 copy-start.2
  3.8 1.1 %copy-done.2 = f32[3,8,32,256]{3,2,1,0:T(8,128)S(1)} copy-done((f32[3,8,32,256]{3,2,1,0:T(8,128)S(1)}, f32[3,8,32,256]{3,2,1,0:T(8,128)}, u32[]{:S(2)}) %copy-start.2) | copy-done | bytes 786456
  4.9 0.0 copy-start.3
  4.9 0.9 %copy-done.3 = f32[8,32,256]{2,1,0:T(8,128)S(1)} copy-done((f32[8,32,256]{2,1,0:T(8,128)S(1)}, f32[8,32,256]{2,1,0:T(8,128)}, u32[]{:S(2)}) %copy-start.3) | copy-done | bytes 262168
  5.9 0.0 copy-start.4
  5.9 0.7 %copy-done.4 = s32[2,8,64]{2,1,0:T(8,128)S(1)} copy-done((s32[2,8,64]{2,1,0:T(8,128)S(1)}, s32[2,8,64]{2,1,0:T(8,128)}, u32[]{:S(2)}) %copy-start.4) | copy-done | bytes 4120
  6.6 36.1 %shard_map.77 = (f32[5,8,32,256]{3,2,1,0:T(8,128)S(1)}, f32[1,256]{1,0:T(1,128)S(1)}) custom-call(f32[5,8,32,256]{3,2,1,0:T(8,128)S(1)} %copy-done, f32[3,8,32,256]{3,2,1,0:T(8,128)S(1)} %copy-done.1, f32[8,32,256]{2,1,0:T(8,128)S(1)} %copy-done.3, f32[3,5,5]{2,1,0:T(8,128)S(1)} %copy.8.cp, f32[3,8,32,256]{3,2,1,0:T(8,128)S(1)} %copy-done.2, ...), custom_call_target="tpu_custom_call" | custom-call | tf_op jit(solution)/shard_map/pallas_call | solution.py:516
  42.7 1.1 %copy.11 = f32[5,8,32,256]{3,2,1,0:T(8,128)} copy(f32[5,8,32,256]{3,2,1,0:T(8,128)S(1)} %get-tuple-element.8) | data formatting | bytes 2621440
  43.8 0.6 %copy.12 = f32[256]{0:T(256)} copy(f32[256]{0:T(256)S(1)} %bitcast.1) | data formatting | bytes 2048
Async XLA Ops:
  1.3 1.3 %copy-start = (f32[5,8,32,256]{3,2,1,0:T(8,128)S(1)}, f32[5,8,32,256]{3,2,1,0:T(8,128)}, u32[]{:S(2)}) copy-start(f32[5,8,32,256]{3,2,1,0:T(8,128)} %rs_hbm.1) | copy-start | bytes 3932164
  2.7 1.1 %copy-start.1 = (f32[3,8,32,256]{3,2,1,0:T(8,128)S(1)}, f32[3,8,32,256]{3,2,1,0:T(8,128)}, u32[]{:S(2)}) copy-start(f32[3,8,32,256]{3,2,1,0:T(8,128)} %sp_hbm.1) | copy-start | bytes 2359300
  3.8 1.1 %copy-start.2 = (f32[3,8,32,256]{3,2,1,0:T(8,128)S(1)}, f32[3,8,32,256]{3,2,1,0:T(8,128)}, u32[]{:S(2)}) copy-start(f32[3,8,32,256]{3,2,1,0:T(8,128)} %mo_hbm.1) | copy-start | bytes 2359300
  4.9 0.9 %copy-start.3 = (f32[8,32,256]{2,1,0:T(8,128)S(1)}, f32[8,32,256]{2,1,0:T(8,128)}, u32[]{:S(2)}) copy-start(f32[8,32,256]{2,1,0:T(8,128)} %po_hbm.1) | copy-start | bytes 786436
  5.9 0.7 %copy-start.4 = (s32[2,8,64]{2,1,0:T(8,128)S(1)}, s32[2,8,64]{2,1,0:T(8,128)}, u32[]{:S(2)}) copy-start(s32[2,8,64]{2,1,0:T(8,128)} %ids_ref.1) | copy-start | bytes 12292

commit v2 on v0

v2 whole, which is shorter than its diff:
```python
import functools

import jax
import jax.numpy as jnp
from jax import lax
from jax.experimental import pallas as pl
from jax.experimental.pallas import tpu as pltpu
from jax.sharding import PartitionSpec as P

PENALTY = 1.0
COURANT = 0.3
VARS = 5
SLOTS = 16
MESH = pl.DeviceIdType.MESH
F32 = jnp.float32
BF16 = jnp.bfloat16


def pieces(value):
    high = value.astype(BF16)
    rest = value - high.astype(F32)
    mid = rest.astype(BF16)
    low = (rest - mid.astype(F32)).astype(BF16)
    return high, mid, low


def dot(a, b):
    return jnp.dot(a, b, preferred_element_type=F32)


def dot_nt(a, b):
    return lax.dot_general(a, b, (((1,), (1,)), ((), ())), preferred_element_type=F32)


def iota(shape, axis):
    return lax.broadcasted_iota(jnp.int32, shape, axis)


def fold(product):
    rows = product[0:8] + product[8:16] + product[16:24] + product[24:32]
    return rows[:, 0:128] + rows[:, 128:256]


def solve(gram):
    low = [[None] * 4 for _ in range(4)]
    for col in range(4):
        diag = gram[col][col]
        for inner in range(col):
            diag = diag - low[col][inner] * low[col][inner]
        low[col][col] = jnp.sqrt(diag)
        for row in range(col + 1, 4):
            value = gram[row][col]
            for inner in range(col):
                value = value - low[row][inner] * low[col][inner]
            low[row][col] = value / low[col][col]
    zero = jnp.zeros_like(gram[0][0])
    upper = [[low[c][r] if c >= r else None for c in range(4)] for r in range(4)]

    def add(a, b):
        return b if a is None else (a if b is None else a + b)

    hess = [[add(upper[r][c + 1], upper[r][c]) for c in range(3)] for r in range(4)]

    def inner_sum(terms):
        total = None
        for a, b in terms:
            if a is not None and b is not None:
                total = add(total, a * b)
        return zero if total is None else total

    normal = [[inner_sum([(hess[r][a], hess[r][b]) for r in range(4)]) for b in range(3)] for a in range(3)]
    target = [inner_sum([(hess[r][a], upper[r][0]) for r in range(4)]) for a in range(3)]
    fac = [[None] * 3 for _ in range(3)]
    for col in range(3):
        diag = normal[col][col]
        for inner in range(col):
            diag = diag - fac[col][inner] * fac[col][inner]
        fac[col][col] = jnp.sqrt(diag)
        for row in range(col + 1, 3):
            value = normal[row][col]
            for inner in range(col):
                value = value - fac[row][inner] * fac[col][inner]
            fac[row][col] = value / fac[col][col]
    forward = []
    for place in range(3):
        value = target[place]
        for inner in range(place):
            value = value - fac[place][inner] * forward[inner]
        forward.append(value / fac[place][place])
    backward = [None] * 3
    for place in reversed(range(3)):
        value = forward[place]
        for inner in range(place + 1, 3):
            value = value - fac[inner][place] * backward[inner]
        backward[place] = value / fac[place][place]
    return backward


def kernel(ny, nz, per_owner,
           rs_hbm, sp_hbm, po_hbm, cp, mo_hbm, ids_ref,
           adj_hbm, sens_ref,
           basis, cur, nxt, sp, po, mo, wmat, wz, wa, wb, cpos, cneg, part, fprev, low_shift, high_shift, sface,
           halo_out, halo_in, yfix, block,
           owner_hot, rank_hot, owner_row, local_row, spread, dsend, recv1, turned, recv2, picked,
           gsend, grecv1, gsend2, grecv2,
           in_sem, out_sem, halo_send, halo_recv, a1_sem, a2_sem, g1_sem, g2_sem):
    gy = lax.axis_index("gy")
    gz = lax.axis_index("gz")

    def gy_at(delta):
        return lax.rem(gy + (delta + ny), ny)

    def gz_at(delta):
        return lax.rem(gz + (delta + nz), nz)

    def each(count, step, start=0):
        def body(t, carry):
            step(t)
            return carry
        lax.fori_loop(start, count, body, 0)

    barrier = pltpu.get_barrier_semaphore()

    @functools.partial(each, ny, start=1)
    def _(delta):
        pl.semaphore_signal(barrier, inc=1, device_id={"gy": gy_at(delta)}, device_id_type=MESH)

    @functools.partial(each, nz, start=1)
    def _(delta):
        pl.semaphore_signal(barrier, inc=1, device_id={"gz": gz_at(delta)}, device_id_type=MESH)

    loads = [pltpu.make_async_copy(src, dst, in_sem.at[place]) for place, (src, dst) in enumerate(
        [(sp_hbm, sp), (rs_hbm, nxt), (po_hbm, po), (mo_hbm, mo)])]
    for load in loads:
        load.start()

    lane = iota((16, 256), 1)
    row = iota((16, 256), 0)
    group = lane >> 4
    piece = jnp.where(group >= 10, 2, jnp.where(group >= 5, 1, 0))
    which = group - 5 * piece
    same = (lane & 15) == row

    @functools.partial(each, 3 * VARS)
    def _(place):
        d = lax.div(place, VARS)
        j = place - d * VARS
        value = jnp.zeros((16, 256), F32)
        for i in range(VARS):
            value = jnp.where(which == i, COURANT * cp[i, d, j], value)
        high = value.astype(BF16).astype(F32)
        value = jnp.where(same, jnp.where(piece == 2, value - high, high), 0.0)
        wmat[pl.ds(pl.multiple_of(place * 16, 16), 16), :] = value[:, 0:240].astype(BF16)

    lane = iota((16, 128), 1)
    row = iota((16, 128), 0)

    wz[80:128, :] = jnp.zeros((48, 128), F32)

    @functools.partial(each, VARS)
    def _(i):
        value = jnp.zeros((16, 128), F32)
        for j in range(VARS):
            value = jnp.where((lane >> 4) == j, -COURANT * cp[i, 2, j], value)
        wz[pl.ds(pl.multiple_of(16 * i, 16), 16), :] = jnp.where((lane & 15) == row, value, 0.0)

    ids = jnp.concatenate([ids_ref[0], ids_ref[1]], axis=1)
    owners = lax.div(ids, per_owner)
    local_row[...] = (ids - owners * per_owner + 1).astype(F32)
    number = ny * nz
    tri = jnp.where(iota((256, 128), 0) < jnp.where(iota((256, 128), 0) >= 128, 256, iota((256, 128), 1)), 1.0, 0.0).astype(BF16)
    sub = iota((number, 128), 0)
    before = jnp.zeros((number, 128), F32)
    for p in range(8):
        hot = jnp.where(sub == owners[p:p + 1, :], 1.0, 0.0)
        hot16 = hot.astype(BF16)
        count = dot(jnp.concatenate([hot16, before.astype(BF16)], axis=1), tri)
        before = before + hot
        owner_hot[:, p * 128:(p + 1) * 128] = hot16
        rank = jnp.sum(hot * count, axis=0, keepdims=True)
        rank_hot[:, p * 128:(p + 1) * 128] = jnp.where(rank == iota((SLOTS, 128), 0).astype(F32), 1.0, 0.0)

    loads[0].wait()

    @functools.partial(each, 8)
    def _(x):
        for d in range(3):
            s = sp[d, x]
            cpos[d, x] = jnp.maximum(s, 0.0)
            cneg[d, x] = jnp.maximum(-s, 0.0)

    lanes = iota((32, 128), 1)
    odd = (lanes & 1) == 1
    faces = jnp.zeros((32, 128), F32)
    for x in range(8):
        ends = jnp.where(lanes == 0, sp[2, x, :, 0:128], sp[2, x, :, 128:256])
        faces = jnp.where((lanes >> 1) == x, pltpu.roll(ends, 2 * x + 1, axis=1), faces)
    total = faces
    for i in range(1, VARS):
        total = jnp.where((lanes >> 4) == i, pltpu.roll(faces, 16 * i, axis=1), total)
    total = jnp.where((lanes >> 4) < VARS, total, 0.0)
    sface[...] = jnp.where(odd, jnp.maximum(total, 0.0), jnp.maximum(-total, 0.0))

    keep_low = jnp.where(gy > 0, 1.0, 0.0)
    keep_high = jnp.where(gy < ny - 1, 1.0, 0.0)
    keep_near = jnp.where(gz > 0, 1.0, 0.0)
    keep_far = jnp.where(gz < nz - 1, 1.0, 0.0)

    YROWS = VARS * 16
    ZAT = 2 * YROWS

    def y_at(side, j, half):
        return side * YROWS + j * 16 + half * 8

    def halo_copies(par):
        copies = []
        for side, delta in ((0, -1), (1, 1)):
            rows = pl.ds(side * YROWS, YROWS)
            other = pl.ds((1 - side) * YROWS, YROWS)
            copies.append(pltpu.make_async_remote_copy(
                src_ref=halo_out.at[par, rows], dst_ref=halo_in.at[par, other],
                send_sem=halo_send.at[par], recv_sem=halo_recv.at[par],
                device_id={"gy": gy_at(delta)}, device_id_type=MESH))
            copies.append(pltpu.make_async_remote_copy(
                src_ref=halo_out.at[par, pl.ds(ZAT, 32)], dst_ref=halo_in.at[par, pl.ds(ZAT + 32 * (1 - side), 32)],
                send_sem=halo_send.at[par], recv_sem=halo_recv.at[par],
                device_id={"gz": gz_at(delta)}, device_id_type=MESH))
        return copies

    def wait_all(ref, sem):
        pltpu.make_async_copy(ref, ref, sem).wait()

    halves = (slice(0, 128), slice(128, 256))

    def fix_and_pack(k, par, ufix):
        for i in range(VARS):
            for x in range(8):
                for side, y in ((0, 0), (1, 31)):
                    for half in range(2):
                        at = y_at(side, i, half) + x
                        nxt[i, x, y:y + 1, halves[half]] = nxt[i, x, y:y + 1, halves[half]] + yfix[at:at + 1, :]
        packed = jnp.zeros((32, 128), F32)
        for i in range(VARS):
            for x in range(8):
                s = i * 8 + x
                fix = pltpu.roll(ufix, 127 - 2 * s, axis=1)
                near = nxt[i, x, :, 0:128] + jnp.where(lanes == 0, fix, 0.0)
                far = nxt[i, x, :, 128:256] + jnp.where(lanes == 127, fix, 0.0)
                cur[i, x, :, 0:128] = near
                cur[i, x, :, 128:256] = far
                basis[k, i, x, :, 0:128] = near
                basis[k, i, x, :, 128:256] = far
                ends = jnp.where(lanes == 0, near, far)
                packed = jnp.where((lanes >> 1) == s, pltpu.roll(ends, 2 * s + 1, axis=1), packed)
        halo_out[par, ZAT:ZAT + 32, :] = jnp.dot(
            packed * sface[...], wz[...], preferred_element_type=F32, precision=lax.Precision.HIGHEST)
        for side, y in ((0, 0), (1, 31)):
            for half in range(2):
                speed = sp[1, :, y, halves[half]]
                speed = jnp.maximum(speed, 0.0) if side == 0 else jnp.maximum(-speed, 0.0)
                flux = [cur[i, :, y, halves[half]] * speed for i in range(VARS)]
                for j in range(VARS):
                    total = flux[0] * (-COURANT * cp[0, 1, j])
                    for i in range(1, VARS):
                        total = total + flux[i] * (-COURANT * cp[i, 1, j])
                    at = y_at(side, j, half)
                    halo_out[par, at:at + 8, :] = total

    def receive(par):
        wait_all(halo_in.at[par], halo_recv.at[par])
        wait_all(halo_in.at[par], halo_send.at[par])
        yfix[0:YROWS, :] = keep_low * halo_in[par, 0:YROWS, :] - halo_out[par, YROWS:ZAT, :]
        yfix[YROWS:ZAT, :] = keep_high * halo_in[par, YROWS:ZAT, :] - halo_out[par, 0:YROWS, :]
        own = halo_out[par, ZAT:ZAT + 32, :]
        from_near = pltpu.roll(keep_near * halo_in[par, ZAT:ZAT + 32, :] - own, 1, axis=1)
        from_far = pltpu.roll(keep_far * halo_in[par, ZAT + 32:ZAT + 64, :] - own, 127, axis=1)
        yfix[ZAT:ZAT + 32, :] = jnp.where(odd, from_near, from_far)

    def couple(x, w):
        for h in (0, 16):
            high, low = [], []
            for i in range(VARS):
                v = cur[i, x, h:h + 16, :]
                top = v.astype(BF16)
                high.append(top)
                low.append((v - top.astype(F32)).astype(BF16))
            out = dot(wmat[...], jnp.concatenate(high + low + high, axis=0))
            for place in range(3 * VARS):
                w[place, h:h + 16, :] = out[place * 16:place * 16 + 16]

    def stencil(x, w):
        prior = jnp.maximum(x - 1, 0)
        for j in range(VARS):
            wx = w[j]
            flux = cpos[0, x] * wx - fprev[j]
            nxt[j, prior] = part[j] - flux
            fprev[j] = cneg[0, x] * wx
            acc = po[x] * cur[j, x] + flux
            wv = w[2 * VARS + j]
            flux = cpos[2, x] * wv - pltpu.roll(cneg[2, x] * wv, 1, axis=1)
            acc = acc + flux - pltpu.roll(flux, 255, axis=1)
            for half in range(2):
                at = halves[half]
                wy = w[VARS + j, :, at]
                minus = cneg[1, x, :, at] * wy
                low_shift[j, half, 8:40, :] = minus
                low_shift[j, half, 0:8, :] = minus[24:32]
                flux = cpos[1, x, :, at] * wy - low_shift[j, half, 7:39, :]
                high_shift[j, half, 0:32, :] = flux
                high_shift[j, half, 32:40, :] = flux[0:8]
                part[j, :, at] = acc[:, at] + flux - high_shift[j, half, 1:33, :]

    def sweep():
        fprev[...] = jnp.zeros(fprev.shape, F32)
        couple(0, wa)

        @functools.partial(each, 4)
        def _(t):
            x = 2 * t
            couple(x + 1, wb)
            stencil(x, wa)
            couple(jnp.minimum(x + 2, 7), wa)
            stencil(x + 1, wb)

        for j in range(VARS):
            nxt[j, 7] = part[j] + fprev[j]

    def dispatch():
        loads[3].wait()

        @functools.partial(each, 2)
        def _(half_x):
            for k in range(3):
                total = None
                for x in range(4):
                    for i in range(3):
                        term = basis[k, 1 + i, 4 * half_x + x] * mo[i, 4 * half_x + x]
                        total = term if total is None else total + term
                block[k, half_x] = total

        low8 = iota((16, 192), 0)
        col = iota((16, 192), 1)
        within = jnp.where(col >= 96, col - 96, col) & 31
        half = jnp.where(col >= 96, 1, 0)
        ysel = jnp.where((low8 >> 3 == half) & ((low8 & 7) == (within >> 2)), 1.0, 0.0).astype(BF16)
        zrow = iota((512, 128), 0)
        zsel = jnp.where(((zrow & 255) >> 2) + (zrow >> 8) * 64 == iota((512, 128), 1), 1.0, 0.0).astype(BF16)
        parts = []
        for k in range(3):
            t = dot(ysel, jnp.concatenate(list(pieces(block[k, 0])) + list(pieces(block[k, 1])), axis=0))
            for part_ in pieces(jnp.concatenate([t[0:8], t[8:16]], axis=1)):
                parts.append(part_.astype(F32))
        t = dot(jnp.concatenate(parts, axis=0).astype(BF16), zsel)
        values = [-PENALTY * (t[24 * k:24 * k + 8] + t[24 * k + 8:24 * k + 16] + t[24 * k + 16:24 * k + 24])
                  for k in range(3)]
        tops = [value.astype(BF16).astype(F32) for value in values]
        rests = [value - top for value, top in zip(values, tops)]
        empty = jnp.zeros((SLOTS, 128), BF16)
        for p in range(8):
            hot = rank_hot[:, p * 128:(p + 1) * 128]
            rows = [local_row[...]] + tops + rests
            rows = [(hot * value[p:p + 1, :]).astype(BF16) for value in rows]
            spread[:, p * 128:(p + 1) * 128] = jnp.concatenate(rows + [empty], axis=0)
        dsend[...] = dot_nt(owner_hot[...], spread[...]).reshape(ny, nz, 128)

        @functools.partial(each, ny, start=1)
        def _(delta):
            pltpu.make_async_remote_copy(
                src_ref=dsend.at[gy_at(delta)], dst_ref=recv1.at[delta],
                send_sem=a1_sem.at[0], recv_sem=a1_sem.at[1],
                device_id={"gy": gy_at(delta)}, device_id_type=MESH).start()
        recv1[0] = dsend[gy]

    yfix[...] = jnp.zeros(yfix.shape, F32)
    loads[1].wait()
    loads[2].wait()

    @functools.partial(each, 4)
    def _(k):
        par = k & 1

        @pl.when(k > 0)
        def _():
            receive(1 - par)

        fix_and_pack(k, par, yfix[ZAT:ZAT + 32, :])

        @pl.when(k == 0)
        def _():
            pl.semaphore_wait(barrier, (ny - 1) + (nz - 1))

        @pl.when(k < 3)
        def _():
            for copy in halo_copies(par):
                copy.start()

            @pl.when(k == 2)
            def _():
                dispatch()

            sweep()

    pairs = [(l, k) for k in range(4) for l in range(k + 1)]

    def products(x, sums):
        sums = list(sums)
        for j in range(VARS):
            v = [basis[k, j, x] for k in range(4)]
            for e, (l, k) in enumerate(pairs):
                sums[e] = sums[e] + fold(v[l] * v[k])
        return tuple(sums)

    sums = lax.fori_loop(0, 8, products, tuple(jnp.zeros((8, 128), F32) for _ in pairs))

    lane = iota((8, 128), 1)
    packed = jnp.zeros((8, 128), F32)
    for e, value in enumerate(sums):
        for shift in (64, 32, 16, 8):
            value = value + pltpu.roll(value, shift, axis=1)
        packed = jnp.where((lane >> 3) == e, value, packed)
    gsend[...] = jnp.sum(packed, axis=0, keepdims=True)

    @functools.partial(each, ny, start=1)
    def _(delta):
        pltpu.make_async_remote_copy(
            src_ref=gsend, dst_ref=grecv1.at[delta], send_sem=g1_sem.at[0], recv_sem=g1_sem.at[1],
            device_id={"gy": gy_at(delta)}, device_id_type=MESH).start()

    wait_all(recv1.at[pl.ds(1, ny - 1)], a1_sem.at[1])
    wait_all(recv1.at[pl.ds(1, ny - 1)], a1_sem.at[0])
    for g in range(nz):
        turned[g] = recv1[:, g, :]

    @functools.partial(each, nz, start=1)
    def _(delta):
        pltpu.make_async_remote_copy(
            src_ref=turned.at[gz_at(delta)], dst_ref=recv2.at[delta], send_sem=a2_sem.at[0], recv_sem=a2_sem.at[1],
            device_id={"gz": gz_at(delta)}, device_id_type=MESH).start()
    recv2[0] = turned[gz]

    wait_all(grecv1.at[pl.ds(1, ny - 1)], g1_sem.at[1])
    wait_all(grecv1.at[pl.ds(1, ny - 1)], g1_sem.at[0])
    own = gsend[...]
    for delta in range(1, ny):
        own = own + grecv1[delta]
    gsend2[...] = own

    @functools.partial(each, nz, start=1)
    def _(delta):
        pltpu.make_async_remote_copy(
            src_ref=gsend2, dst_ref=grecv2.at[delta], send_sem=g2_sem.at[0], recv_sem=g2_sem.at[1],
            device_id={"gz": gz_at(delta)}, device_id_type=MESH).start()

    wait_all(recv2.at[pl.ds(1, nz - 1)], a2_sem.at[1])
    wait_all(recv2.at[pl.ds(1, nz - 1)], a2_sem.at[0])
    picked[...] = recv2[...].reshape(number, 128).T
    digit = iota((16, 128), 0)
    left, right = [], []
    for r in range(SLOTS):
        number_r = picked[r:r + 1, :].astype(jnp.int32) - 1
        high = (number_r >> 4) == digit
        right.append(jnp.where((number_r & 15) == digit, 1.0, 0.0).astype(BF16))
        left.append(jnp.concatenate(
            [jnp.where(high, picked[SLOTS * (q + 1) + r:SLOTS * (q + 1) + r + 1, :], 0.0).astype(BF16) for q in range(6)], axis=0))
    bins = dot_nt(jnp.concatenate(left, axis=1), jnp.concatenate(right, axis=1))
    bins = bins[0:48] + bins[48:96]
    wide = jnp.where((iota((16, 256), 1) & 15) == iota((16, 256), 0), 1.0, 0.0).astype(BF16)
    bins = sum(dot(part_, wide) for part_ in pieces(bins))
    bins = jnp.where((iota((48, 256), 1) >> 4) == (iota((48, 256), 0) & 15), bins, 0.0)
    bin_sums = [jnp.sum(bins[16 * k:16 * k + 16], axis=0, keepdims=True) for k in range(3)]

    wait_all(grecv2.at[pl.ds(1, nz - 1)], g2_sem.at[1])
    wait_all(grecv2.at[pl.ds(1, nz - 1)], g2_sem.at[0])
    own = gsend2[...]
    for delta in range(1, nz):
        own = own + grecv2[delta]
    for shift in (4, 2, 1):
        own = own + pltpu.roll(own, shift, axis=1)
    own = jnp.broadcast_to(own, (8, 128))
    splat = {}
    for e, (l, k) in enumerate(pairs):
        splat[l, k] = jnp.broadcast_to(own[:, 8 * e + 7:8 * e + 8], (8, 128))
    coeffs = solve([[splat[min(a, b), max(a, b)] for b in range(4)] for a in range(4)])

    sens = None
    for k in range(3):
        term = bin_sums[k] * jnp.concatenate([coeffs[k][0:1]] * (per_owner // 128), axis=1)
        sens = term if sens is None else sens + term
    sens_ref[...] = sens

    full = [jnp.concatenate([jnp.concatenate([c, c], axis=1)] * 4, axis=0) for c in coeffs]

    @functools.partial(each, VARS)
    def _(j):
        for x in range(8):
            nxt[j, x] = full[0] * basis[0, j, x] + full[1] * basis[1, j, x] + full[2] * basis[2, j, x]
        pltpu.make_async_copy(nxt.at[j], adj_hbm.at[j], out_sem).start()

    wait_all(nxt, out_sem)


def local(right_side, speeds, porosity, coupling, momentum, design_ids):
    ny = lax.axis_size("gy")
    nz = lax.axis_size("gz")
    _, nx, cy, cz = right_side.shape
    per_owner = design_ids.size // 4
    field = (VARS, nx, cy, cz)
    dma = pltpu.SemaphoreType.DMA
    hbm = pl.BlockSpec(memory_space=pltpu.HBM)
    vmem = pl.BlockSpec(memory_space=pltpu.VMEM)
    adjoint, sensitivity = pl.pallas_call(
        functools.partial(kernel, ny, nz, per_owner),
        out_shape=[jax.ShapeDtypeStruct(field, F32), jax.ShapeDtypeStruct((1, per_owner), F32)],
        in_specs=[hbm, hbm, hbm, pl.BlockSpec(memory_space=pltpu.SMEM), hbm, vmem],
        out_specs=[hbm, vmem],
        scratch_shapes=[
            pltpu.VMEM((4,) + field, F32), pltpu.VMEM(field, F32), pltpu.VMEM(field, F32),
            pltpu.VMEM((3, nx, cy, cz), F32),
            pltpu.VMEM((nx, cy, cz), F32),
            pltpu.VMEM((3, nx, cy, cz), F32),
            pltpu.VMEM((240, 240), BF16),
            pltpu.VMEM((128, 128), F32),
            pltpu.VMEM((3 * VARS, cy, cz), F32), pltpu.VMEM((3 * VARS, cy, cz), F32),
            pltpu.VMEM((3, nx, cy, cz), F32), pltpu.VMEM((3, nx, cy, cz), F32),
            pltpu.VMEM((VARS, cy, cz), F32), pltpu.VMEM((VARS, cy, cz), F32),
            pltpu.VMEM((VARS, 2, 40, 128), F32), pltpu.VMEM((VARS, 2, 40, 128), F32),
            pltpu.VMEM((32, 128), F32),
            pltpu.VMEM((2, 192, 128), F32), pltpu.VMEM((2, 224, 128), F32), pltpu.VMEM((192, 128), F32),
            pltpu.VMEM((3, 2, cy, cz), F32),
            pltpu.VMEM((ny * nz, 1024), BF16),
            pltpu.VMEM((SLOTS, 1024), F32),
            pltpu.VMEM((8, 128), F32),
            pltpu.VMEM((8, 128), F32),
            pltpu.VMEM((128, 1024), BF16),
            pltpu.VMEM((ny, nz, 128), F32),
            pltpu.VMEM((ny, nz, 128), F32),
            pltpu.VMEM((nz, ny, 128), F32),
            pltpu.VMEM((nz, ny, 128), F32),
            pltpu.VMEM((128, 128), F32),
            pltpu.VMEM((1, 128), F32),
            pltpu.VMEM((ny, 1, 128), F32),
            pltpu.VMEM((1, 128), F32),
            pltpu.VMEM((nz, 1, 128), F32),
            dma((4,)), dma, dma((2,)), dma((2,)), dma((2,)), dma((2,)), dma((2,)), dma((2,)),
        ],
        compiler_params=pltpu.CompilerParams(
            collective_id=0, has_side_effects=True, vmem_limit_bytes=48 * 1024 * 1024),
    )(right_side, speeds, porosity, coupling.transpose(1, 0, 2), momentum, design_ids)
    return adjoint, sensitivity.reshape(per_owner)


def solution(mesh):
    in_specs = (
        P(None, None, "gy", "gz"),
        P(None, None, "gy", "gz"),
        P(None, "gy", "gz"),
        P(),
        P(None, None, "gy", "gz"),
        P(None, "gy", "gz"),
    )
    out_specs = (P(None, None, "gy", "gz"), P(("gy", "gz")))
    return jax.shard_map(local, mesh=mesh, in_specs=in_specs, out_specs=out_specs, check_vma=False)
```

time: 413 us -> 43.6 us (0.11); the launches traced: 407 us -> 43.2 us
  waiting for transfers between devices: 148 us -> 0 us
  blocking collectives: 68.2 us -> 0 us
  local copies, waits for them, and re-layouts: 54.8 us -> 7.54 us
  other arithmetic: 45.7 us -> 0 us
  Pallas kernels: 0 us -> 35 us
  matrix products: 32.9 us -> 0 us
  starting transfers between devices: 32.6 us -> 0 us
  between operations: 24.6 us -> 0.65 us
    unnamed x2 -> x0, waiting for transfers between devices: 136 us -> none
    psum x1 -> x0, blocking collectives: 68.2 us -> none  [local(): gram = lax.psum(gram_local, ('gy', 'gz'))]
    pallas_call x0 -> x1, Pallas kernels: none -> 35 us  [local(): pl.pallas_call(functools.partial(kernel, ny, nz, per_owner), out_shape=[j...]
    dot_general x11 -> x0, matrix products: 32.9 us -> none  [the longest x9 32.6 us: transpose_sweep(): jnp.einsum('ij,ixyz->jxyz', coupling[direction], flux, precision=lax.Prec...]
    ppermute x12 -> x0, starting transfers between devices: 32.5 us -> none  [the longest x6 22.5 us: padded(): lax.ppermute(lax.slice_in_dim(block, block.shape[dim] - width, None, axis...]
    slice x21 -> x0, local copies, waits for them, and re-layouts: 21.9 us -> none  [the longest x8 11.9 us: padded(): lax.slice_in_dim(block, block.shape[dim] - width, None, axis=dim)]
    ppermute x6 -> x0, local copies, waits for them, and re-layouts: 13.7 us -> none  [the longest x3 6.88 us: padded(): lax.ppermute(lax.slice_in_dim(block, block.shape[dim] - width, None, axis...]
    concatenate x6 -> x0, other arithmetic: 12.7 us -> none  [padded(): block = jnp.concatenate([low, block, high], axis=dim)]
  transfers between devices with their start and end apart: 13 -> 0, of which waited for: 6 -> 0; matrix products, arithmetic and copies ran while one was open for 4% -> 0% of each run, Pallas kernels for 0% -> 0%
where the time goes in v2:
time: 43.6 us; the launch traced here: 43.2 us
  Pallas kernels  35 us (80%)
  local copies, waits for them, and re-layouts  7.54 us (17%)
  between operations  0.65 us (1%)
    pallas_call x1, Pallas kernels, local(): pl.pallas_call(functools.partial(kernel, ny, nz, per_owner), out_shape=[j...  35 us
    unnamed x14, local copies, waits for them, and re-layouts  7.54 us

profile of v2, /device:TPU:1, one launch (start us, length us, event | category | flops | bytes accessed | tf_op | source)
XLA Modules:
  0.0 43.2 jit_solution(16225328227419783743)
XLA Ops:
  0.6 0.0 copy-start
  0.6 1.3 %copy-done = f32[5,8,32,256]{3,2,1,0:T(8,128)S(1)} copy-done((f32[5,8,32,256]{3,2,1,0:T(8,128)S(1)}, f32[5,8,32,256]{3,2,1,0:T(8,128)}, u32[]{:S(2)}) %copy-start) | copy-done | bytes 1310744
  1.9 0.0 copy-start.1
  2.0 1.1 %copy-done.1 = f32[3,8,32,256]{3,2,1,0:T(8,128)S(1)} copy-done((f32[3,8,32,256]{3,2,1,0:T(8,128)S(1)}, f32[3,8,32,256]{3,2,1,0:T(8,128)}, u32[]{:S(2)}) %copy-start.1) | copy-done | bytes 786456
  3.1 0.0 copy-start.2
  3.1 1.1 %copy-done.2 = f32[3,8,32,256]{3,2,1,0:T(8,128)S(1)} copy-done((f32[3,8,32,256]{3,2,1,0:T(8,128)S(1)}, f32[3,8,32,256]{3,2,1,0:T(8,128)}, u32[]{:S(2)}) %copy-start.2) | copy-done | bytes 786456
  4.2 0.0 copy-start.3
  4.2 0.9 %copy-done.3 = f32[8,32,256]{2,1,0:T(8,128)S(1)} copy-done((f32[8,32,256]{2,1,0:T(8,128)S(1)}, f32[8,32,256]{2,1,0:T(8,128)}, u32[]{:S(2)}) %copy-start.3) | copy-done | bytes 262168
  5.2 0.0 copy-start.4
  5.2 0.7 %copy-done.4 = f32[3,5,5]{2,0,1:T(4,128)S(1)} copy-done((f32[3,5,5]{2,0,1:T(4,128)S(1)}, f32[3,5,5]{2,0,1:T(4,128)}, u32[]{:S(2)}) %copy-start.4) | copy-done | bytes 324
  5.9 0.0 copy-start.5
  5.9 0.7 %copy-done.5 = s32[2,8,64]{2,1,0:T(8,128)S(1)} copy-done((s32[2,8,64]{2,1,0:T(8,128)S(1)}, s32[2,8,64]{2,1,0:T(8,128)}, u32[]{:S(2)}) %copy-start.5) | copy-done | bytes 4120
  6.6 35.0 %shard_map.77 = (f32[5,8,32,256]{3,2,1,0:T(8,128)S(1)}, f32[1,256]{1,0:T(1,128)S(1)}) custom-call(f32[5,8,32,256]{3,2,1,0:T(8,128)S(1)} %copy-done, f32[3,8,32,256]{3,2,1,0:T(8,128)S(1)} %copy-done.1, f32[8,32,256]{2,1,0:T(8,128)S(1)} %copy-done.3, f32[5,3,5]{2,1,0:T(4,128)S(1)} %bitcast.2, f32[3,8,32,256]{3,2,1,0:T(8,128)S(1)} %copy-done.2, ...), custom_call_target="tpu_custom_call" | custom-call | tf_op jit(solution)/shard_map/pallas_call | solution.py:511
  41.6 1.1 %copy.10 = f32[5,8,32,256]{3,2,1,0:T(8,128)} copy(f32[5,8,32,256]{3,2,1,0:T(8,128)S(1)} %get-tuple-element.8) | data formatting | bytes 2621440
  42.7 0.6 %copy.11 = f32[256]{0:T(256)} copy(f32[256]{0:T(256)S(1)} %bitcast.3) | data formatting | bytes 2048
Async XLA Ops:
  0.6 1.3 %copy-start = (f32[5,8,32,256]{3,2,1,0:T(8,128)S(1)}, f32[5,8,32,256]{3,2,1,0:T(8,128)}, u32[]{:S(2)}) copy-start(f32[5,8,32,256]{3,2,1,0:T(8,128)} %rs_hbm.1) | copy-start | bytes 3932164
  1.9 1.1 %copy-start.1 = (f32[3,8,32,256]{3,2,1,0:T(8,128)S(1)}, f32[3,8,32,256]{3,2,1,0:T(8,128)}, u32[]{:S(2)}) copy-start(f32[3,8,32,256]{3,2,1,0:T(8,128)} %sp_hbm.1) | copy-start | bytes 2359300
  3.1 1.1 %copy-start.2 = (f32[3,8,32,256]{3,2,1,0:T(8,128)S(1)}, f32[3,8,32,256]{3,2,1,0:T(8,128)}, u32[]{:S(2)}) copy-start(f32[3,8,32,256]{3,2,1,0:T(8,128)} %mo_hbm.1) | copy-start | bytes 2359300
  4.2 0.9 %copy-start.3 = (f32[8,32,256]{2,1,0:T(8,128)S(1)}, f32[8,32,256]{2,1,0:T(8,128)}, u32[]{:S(2)}) copy-start(f32[8,32,256]{2,1,0:T(8,128)} %po_hbm.1) | copy-start | bytes 786436
  5.2 0.7 %copy-start.4 = (f32[3,5,5]{2,0,1:T(4,128)S(1)}, f32[3,5,5]{2,0,1:T(4,128)}, u32[]{:S(2)}) copy-start(f32[3,5,5]{2,0,1:T(4,128)} %param.9) | copy-start | bytes 904
  5.9 0.7 %copy-start.5 = (s32[2,8,64]{2,1,0:T(8,128)S(1)}, s32[2,8,64]{2,1,0:T(8,128)}, u32[]{:S(2)}) copy-start(s32[2,8,64]{2,1,0:T(8,128)} %ids_ref.1) | copy-start | bytes 12292

commit v3 on v2

--- a/solution.py
+++ b/solution.py
@@ -100,13 +100,15 @@
            rs_hbm, sp_hbm, po_hbm, cp, mo_hbm, ids_ref,
            adj_hbm, sens_ref,
            basis, cur, nxt, sp, po, mo, wmat, wz, wa, wb, cpos, cneg, part, fprev, low_shift, high_shift, sface,
-           halo_out, halo_in, yfix, block,
+           halo_out, halo_in, yfix, block, prods,
            owner_hot, rank_hot, owner_row, local_row, spread, dsend, recv1, turned, recv2, picked,
            gsend, grecv1, gsend2, grecv2,
            in_sem, out_sem, halo_send, halo_recv, a1_sem, a2_sem, g1_sem, g2_sem):
     gy = lax.axis_index("gy")
     gz = lax.axis_index("gz")
 
+    number = ny * nz
+
     def gy_at(delta):
         return lax.rem(gy + (delta + ny), ny)
 
@@ -133,24 +135,6 @@
         [(sp_hbm, sp), (rs_hbm, nxt), (po_hbm, po), (mo_hbm, mo)])]
     for load in loads:
         load.start()
-
-    lane = iota((16, 256), 1)
-    row = iota((16, 256), 0)
-    group = lane >> 4
-    piece = jnp.where(group >= 10, 2, jnp.where(group >= 5, 1, 0))
-    which = group - 5 * piece
-    same = (lane & 15) == row
-
-    @functools.partial(each, 3 * VARS)
-    def _(place):
-        d = lax.div(place, VARS)
-        j = place - d * VARS
-        value = jnp.zeros((16, 256), F32)
-        for i in range(VARS):
-            value = jnp.where(which == i, COURANT * cp[i, d, j], value)
-        high = value.astype(BF16).astype(F32)
-        value = jnp.where(same, jnp.where(piece == 2, value - high, high), 0.0)
-        wmat[pl.ds(pl.multiple_of(place * 16, 16), 16), :] = value[:, 0:240].astype(BF16)
 
     lane = iota((16, 128), 1)
     row = iota((16, 128), 0)
@@ -164,30 +148,7 @@
             value = jnp.where((lane >> 4) == j, -COURANT * cp[i, 2, j], value)
         wz[pl.ds(pl.multiple_of(16 * i, 16), 16), :] = jnp.where((lane & 15) == row, value, 0.0)
 
-    ids = jnp.concatenate([ids_ref[0], ids_ref[1]], axis=1)
-    owners = lax.div(ids, per_owner)
-    local_row[...] = (ids - owners * per_owner + 1).astype(F32)
-    number = ny * nz
-    tri = jnp.where(iota((256, 128), 0) < jnp.where(iota((256, 128), 0) >= 128, 256, iota((256, 128), 1)), 1.0, 0.0).astype(BF16)
-    sub = iota((number, 128), 0)
-    before = jnp.zeros((number, 128), F32)
-    for p in range(8):
-        hot = jnp.where(sub == owners[p:p + 1, :], 1.0, 0.0)
-        hot16 = hot.astype(BF16)
-        count = dot(jnp.concatenate([hot16, before.astype(BF16)], axis=1), tri)
-        before = before + hot
-        owner_hot[:, p * 128:(p + 1) * 128] = hot16
-        rank = jnp.sum(hot * count, axis=0, keepdims=True)
-        rank_hot[:, p * 128:(p + 1) * 128] = jnp.where(rank == iota((SLOTS, 128), 0).astype(F32), 1.0, 0.0)
-
     loads[0].wait()
-
-    @functools.partial(each, 8)
-    def _(x):
-        for d in range(3):
-            s = sp[d, x]
-            cpos[d, x] = jnp.maximum(s, 0.0)
-            cneg[d, x] = jnp.maximum(-s, 0.0)
 
     lanes = iota((32, 128), 1)
     odd = (lanes & 1) == 1
@@ -201,10 +162,7 @@
     total = jnp.where((lanes >> 4) < VARS, total, 0.0)
     sface[...] = jnp.where(odd, jnp.maximum(total, 0.0), jnp.maximum(-total, 0.0))
 
-    keep_low = jnp.where(gy > 0, 1.0, 0.0)
-    keep_high = jnp.where(gy < ny - 1, 1.0, 0.0)
-    keep_near = jnp.where(gz > 0, 1.0, 0.0)
-    keep_far = jnp.where(gz < nz - 1, 1.0, 0.0)
+    inside = (gy > 0, gy < ny - 1, gz > 0, gz < nz - 1)
 
     YROWS = VARS * 16
     ZAT = 2 * YROWS
@@ -212,20 +170,24 @@
     def y_at(side, j, half):
         return side * YROWS + j * 16 + half * 8
 
-    def halo_copies(par):
-        copies = []
-        for side, delta in ((0, -1), (1, 1)):
-            rows = pl.ds(side * YROWS, YROWS)
-            other = pl.ds((1 - side) * YROWS, YROWS)
-            copies.append(pltpu.make_async_remote_copy(
-                src_ref=halo_out.at[par, rows], dst_ref=halo_in.at[par, other],
-                send_sem=halo_send.at[par], recv_sem=halo_recv.at[par],
-                device_id={"gy": gy_at(delta)}, device_id_type=MESH))
-            copies.append(pltpu.make_async_remote_copy(
-                src_ref=halo_out.at[par, pl.ds(ZAT, 32)], dst_ref=halo_in.at[par, pl.ds(ZAT + 32 * (1 - side), 32)],
-                send_sem=halo_send.at[par], recv_sem=halo_recv.at[par],
-                device_id={"gz": gz_at(delta)}, device_id_type=MESH))
-        return copies
+    def in_rows(place):
+        return pl.ds(place * YROWS, YROWS) if place < 2 else pl.ds(ZAT + 32 * (place - 2), 32)
+
+    def send_halo(par):
+        for place, (axis, delta) in enumerate((("y", -1), ("y", 1), ("z", -1), ("z", 1))):
+            rows = in_rows(place) if axis == "y" else pl.ds(ZAT, 32)
+            target = {"gy": gy_at(delta)} if axis == "y" else {"gz": gz_at(delta)}
+            copy = pltpu.make_async_remote_copy(
+                src_ref=halo_out.at[par, rows], dst_ref=halo_in.at[par, in_rows(place ^ 1)],
+                send_sem=halo_send.at[par, place], recv_sem=halo_recv.at[par, place ^ 1],
+                device_id=target, device_id_type=MESH)
+            pl.when(inside[place])(copy.start)
+
+    for place in range(4):
+        @pl.when(jnp.logical_not(inside[place]))
+        def _():
+            for par in range(2):
+                halo_in[par, in_rows(place), :] = jnp.zeros((YROWS if place < 2 else 32, 128), F32)
 
     def wait_all(ref, sem):
         pltpu.make_async_copy(ref, ref, sem).wait()
@@ -267,14 +229,60 @@
                     halo_out[par, at:at + 8, :] = total
 
     def receive(par):
-        wait_all(halo_in.at[par], halo_recv.at[par])
-        wait_all(halo_in.at[par], halo_send.at[par])
-        yfix[0:YROWS, :] = keep_low * halo_in[par, 0:YROWS, :] - halo_out[par, YROWS:ZAT, :]
-        yfix[YROWS:ZAT, :] = keep_high * halo_in[par, YROWS:ZAT, :] - halo_out[par, 0:YROWS, :]
+        for place in range(4):
+            @pl.when(inside[place])
+            def _():
+                ref = halo_in.at[par, in_rows(place)]
+                wait_all(ref, halo_recv.at[par, place])
+                wait_all(ref, halo_send.at[par, place])
+        yfix[0:YROWS, :] = halo_in[par, 0:YROWS, :] - halo_out[par, YROWS:ZAT, :]
+        yfix[YROWS:ZAT, :] = halo_in[par, YROWS:ZAT, :] - halo_out[par, 0:YROWS, :]
         own = halo_out[par, ZAT:ZAT + 32, :]
-        from_near = pltpu.roll(keep_near * halo_in[par, ZAT:ZAT + 32, :] - own, 1, axis=1)
-        from_far = pltpu.roll(keep_far * halo_in[par, ZAT + 32:ZAT + 64, :] - own, 127, axis=1)
+        from_near = pltpu.roll(halo_in[par, ZAT:ZAT + 32, :] - own, 1, axis=1)
+        from_far = pltpu.roll(halo_in[par, ZAT + 32:ZAT + 64, :] - own, 127, axis=1)
         yfix[ZAT:ZAT + 32, :] = jnp.where(odd, from_near, from_far)
+
+    def prepare():
+        @functools.partial(each, 8)
+        def _(x):
+            for d in range(3):
+                s = sp[d, x]
+                cpos[d, x] = jnp.maximum(s, 0.0)
+                cneg[d, x] = jnp.maximum(-s, 0.0)
+
+        lane = iota((16, 256), 1)
+        row = iota((16, 256), 0)
+        group = lane >> 4
+        piece = jnp.where(group >= 10, 2, jnp.where(group >= 5, 1, 0))
+        which = group - 5 * piece
+        same = (lane & 15) == row
+
+        @functools.partial(each, 3 * VARS)
+        def _(place):
+            d = lax.div(place, VARS)
+            j = place - d * VARS
+            value = jnp.zeros((16, 256), F32)
+            for i in range(VARS):
+                value = jnp.where(which == i, COURANT * cp[i, d, j], value)
+            high = value.astype(BF16).astype(F32)
+            value = jnp.where(same, jnp.where(piece == 2, value - high, high), 0.0)
+            wmat[pl.ds(pl.multiple_of(place * 16, 16), 16), :] = value[:, 0:240].astype(BF16)
+
+        ids = jnp.concatenate([ids_ref[0], ids_ref[1]], axis=1)
+        owners = lax.div(ids, per_owner)
+        local_row[...] = (ids - owners * per_owner + 1).astype(F32)
+        tri = jnp.where(iota((256, 128), 0) < jnp.where(iota((256, 128), 0) >= 128, 256, iota((256, 128), 1)), 1.0, 0.0).astype(BF16)
+        sub = iota((number, 128), 0)
+        before = jnp.zeros((number, 128), F32)
+        for p in range(8):
+            hot = jnp.where(sub == owners[p:p + 1, :], 1.0, 0.0)
+            hot16 = hot.astype(BF16)
+            count = dot(jnp.concatenate([hot16, before.astype(BF16)], axis=1), tri)
+            before = before + hot
+            owner_hot[:, p * 128:(p + 1) * 128] = hot16
+            rank = jnp.sum(hot * count, axis=0, keepdims=True)
+            rank_hot[:, p * 128:(p + 1) * 128] = jnp.where(rank == iota((SLOTS, 128), 0).astype(F32), 1.0, 0.0)
+
 
     def couple(x, w):
         for h in (0, 16):
@@ -371,11 +379,20 @@
                 device_id={"gy": gy_at(delta)}, device_id_type=MESH).start()
         recv1[0] = dsend[gy]
 
+    pairs = [(l, k) for k in range(4) for l in range(k + 1)]
+
+    def early(x, sums):
+        sums = list(sums)
+        for j in range(VARS):
+            v = [basis[k, j, x] for k in range(3)]
+            for e, (l, k) in enumerate(pairs[:6]):
+                sums[e] = sums[e] + fold(v[l] * v[k])
+        return tuple(sums)
+
     yfix[...] = jnp.zeros(yfix.shape, F32)
     loads[1].wait()
-    loads[2].wait()
-
-    @functools.partial(each, 4)
+
+    @functools.partial(each, 3)
     def _(k):
         par = k & 1
 
@@ -389,28 +406,46 @@
         def _():
             pl.semaphore_wait(barrier, (ny - 1) + (nz - 1))
 
-        @pl.when(k < 3)
+        send_halo(par)
+
+        @pl.when(k == 0)
         def _():
-            for copy in halo_copies(par):
-                copy.start()
-
-            @pl.when(k == 2)
-            def _():
-                dispatch()
-
-            sweep()
-
-    pairs = [(l, k) for k in range(4) for l in range(k + 1)]
-
-    def products(x, sums):
+            prepare()
+            loads[2].wait()
+
+        @pl.when(k == 2)
+        def _():
+            dispatch()
+            done = lax.fori_loop(0, 8, early, tuple(jnp.zeros((8, 128), F32) for _ in range(6)))
+            for e in range(6):
+                prods[e] = done[e]
+
+        sweep()
+
+    receive(0)
+
+    def late(j, sums):
         sums = list(sums)
-        for j in range(VARS):
-            v = [basis[k, j, x] for k in range(4)]
-            for e, (l, k) in enumerate(pairs):
-                sums[e] = sums[e] + fold(v[l] * v[k])
+        for x in range(8):
+            for side, y in ((0, 0), (1, 31)):
+                for half in range(2):
+                    at = pl.ds(side * YROWS + j * 16 + half * 8 + x, 1)
+                    nxt[j, x, y:y + 1, halves[half]] = nxt[j, x, y:y + 1, halves[half]] + yfix[at, :]
+        ufix = yfix[ZAT:ZAT + 32, :]
+        for x in range(8):
+            fix = pltpu.roll(ufix, 127 - 16 * j - 2 * x, axis=1)
+            near = nxt[j, x, :, 0:128] + jnp.where(lanes == 0, fix, 0.0)
+            far = nxt[j, x, :, 128:256] + jnp.where(lanes == 127, fix, 0.0)
+            for l in range(4):
+                if l < 3:
+                    product = basis[l, j, x, :, 0:128] * near + basis[l, j, x, :, 128:256] * far
+                else:
+                    product = near * near + far * far
+                sums[l] = sums[l] + (product[0:8] + product[8:16] + product[16:24] + product[24:32])
         return tuple(sums)
 
-    sums = lax.fori_loop(0, 8, products, tuple(jnp.zeros((8, 128), F32) for _ in pairs))
+    sums = lax.fori_loop(0, VARS, late, tuple(jnp.zeros((8, 128), F32) for _ in range(4)))
+    sums = [prods[e] for e in range(6)] + list(sums)
 
     lane = iota((8, 128), 1)
     packed = jnp.zeros((8, 128), F32)
@@ -514,7 +549,7 @@
         in_specs=[hbm, hbm, hbm, pl.BlockSpec(memory_space=pltpu.SMEM), hbm, vmem],
         out_specs=[hbm, vmem],
         scratch_shapes=[
-            pltpu.VMEM((4,) + field, F32), pltpu.VMEM(field, F32), pltpu.VMEM(field, F32),
+            pltpu.VMEM((3,) + field, F32), pltpu.VMEM(field, F32), pltpu.VMEM(field, F32),
             pltpu.VMEM((3, nx, cy, cz), F32),
             pltpu.VMEM((nx, cy, cz), F32),
             pltpu.VMEM((3, nx, cy, cz), F32),
@@ -527,6 +562,7 @@
             pltpu.VMEM((32, 128), F32),
             pltpu.VMEM((2, 192, 128), F32), pltpu.VMEM((2, 224, 128), F32), pltpu.VMEM((192, 128), F32),
             pltpu.VMEM((3, 2, cy, cz), F32),
+            pltpu.VMEM((6, 8, 128), F32),
             pltpu.VMEM((ny * nz, 1024), BF16),
             pltpu.VMEM((SLOTS, 1024), F32),
             pltpu.VMEM((8, 128), F32),
@@ -541,10 +577,10 @@
             pltpu.VMEM((ny, 1, 128), F32),
             pltpu.VMEM((1, 128), F32),
             pltpu.VMEM((nz, 1, 128), F32),
-            dma((4,)), dma, dma((2,)), dma((2,)), dma((2,)), dma((2,)), dma((2,)), dma((2,)),
+            dma((4,)), dma, dma((2, 4)), dma((2, 4)), dma((2,)), dma((2,)), dma((2,)), dma((2,)),
         ],
         compiler_params=pltpu.CompilerParams(
-            collective_id=0, has_side_effects=True, vmem_limit_bytes=48 * 1024 * 1024),
+            collective_id=0, has_side_effects=True, vmem_limit_bytes=62 * 1024 * 1024),
     )(right_side, speeds, porosity, coupling.transpose(1, 0, 2), momentum, design_ids)
     return adjoint, sensitivity.reshape(per_owner)
 

time: 43.6 us -> 37.8 us (0.87)
  local copies, waits for them, and re-layouts: 7.54 us -> 3.09 us
  Pallas kernels: 35 us -> 33.9 us
    unnamed x14 -> x4, local copies, waits for them, and re-layouts: 7.54 us -> 3.09 us
    pallas_call x1, Pallas kernels: 35 us -> 33.9 us  [local(): pl.pallas_call(functools.partial(kernel, ny, nz, per_owner), out_shape=[j...]
where the time goes in v3:
time: 37.8 us; the launch traced here: 37.6 us
  Pallas kernels  33.9 us (90%)
  local copies, waits for them, and re-layouts  3.09 us (8%)
  between operations  0.65 us (2%)
    pallas_call x1, Pallas kernels, local(): pl.pallas_call(functools.partial(kernel, ny, nz, per_owner), out_shape=[j...  33.9 us
    unnamed x4, local copies, waits for them, and re-layouts  3.09 us

profile of v3, /device:TPU:1, one launch (start us, length us, event | category | flops | bytes accessed | tf_op | source)
XLA Modules:
  0.0 37.6 jit_solution(2676553748862989433)
XLA Ops:
  0.6 33.9 %shard_map.77 = (f32[5,8,32,256]{3,2,1,0:T(8,128)}, f32[1,256]{1,0:T(1,128)}) custom-call(f32[5,8,32,256]{3,2,1,0:T(8,128)} %rs_hbm.1, f32[3,8,32,256]{3,2,1,0:T(8,128)} %sp_hbm.1, f32[8,32,256]{2,1,0:T(8,128)} %po_hbm.1, f32[5,3,5]{2,1,0:T(4,128)} %bitcast.2, f32[3,8,32,256]{3,2,1,0:T(8,128)} %mo_hbm.1, s32[2,8,64]{2,1,0:T(8,128)} %ids_ref.1), custom_call_target="tpu_custom_call" | custom-call | tf_op jit(solution)/shard_map/pallas_call | solution.py:546
  34.5 0.0 copy-start
  34.6 2.5 %copy.10 = f32[5,8,32,256]{3,2,1,0:T(8,128)} copy(f32[5,8,32,256]{3,2,1,0:T(8,128)} %get-tuple-element.8) | data formatting | bytes 2621440
  37.1 0.0 copy-done
  37.1 0.6 %copy.11 = f32[256]{0:T(256)} copy(f32[256]{0:T(256)S(1)} %bitcast.3) | data formatting | bytes 2048
Async XLA Ops:
  34.5 2.5 %copy-start = (f32[1,256]{1,0:T(1,128)S(1)}, f32[1,256]{1,0:T(1,128)}, u32[]{:S(2)}) copy-start(f32[1,256]{1,0:T(1,128)} %get-tuple-element.5) | copy-start | bytes 3076

commit v4 on v3

--- a/solution.py
+++ b/solution.py
@@ -97,13 +97,13 @@
 
 
 def kernel(ny, nz, per_owner,
-           rs_hbm, sp_hbm, po_hbm, cp, mo_hbm, ids_ref,
-           adj_hbm, sens_ref,
+           rs_hbm, sp_hbm, po_hbm, cp_hbm, mo_hbm, ids_hbm,
+           adj_hbm, sens_hbm,
            basis, cur, nxt, sp, po, mo, wmat, wz, wa, wb, cpos, cneg, part, fprev, low_shift, high_shift, sface,
-           halo_out, halo_in, yfix, block, prods,
+           halo_out, halo_in, yfix, zfix, ypart, zpart, yheld, zheld, corner, turn, block, prods, cp, ids_ref, sens_ref,
            owner_hot, rank_hot, owner_row, local_row, spread, dsend, recv1, turned, recv2, picked,
            gsend, grecv1, gsend2, grecv2,
-           in_sem, out_sem, halo_send, halo_recv, a1_sem, a2_sem, g1_sem, g2_sem):
+           in_sem, out_sem, sens_sem, halo_send, halo_recv, a1_sem, a2_sem, g1_sem, g2_sem):
     gy = lax.axis_index("gy")
     gz = lax.axis_index("gz")
 
@@ -123,44 +123,53 @@
 
     barrier = pltpu.get_barrier_semaphore()
 
-    @functools.partial(each, ny, start=1)
+    def greet(target):
+        pl.semaphore_signal(barrier, inc=1, device_id=target, device_id_type=MESH)
+
+    for delta in (1, -1):
+        greet({"gz": gz_at(delta)})
+        greet({"gy": gy_at(delta)})
+
+    @functools.partial(each, ny - 1, start=2)
     def _(delta):
-        pl.semaphore_signal(barrier, inc=1, device_id={"gy": gy_at(delta)}, device_id_type=MESH)
-
-    @functools.partial(each, nz, start=1)
+        greet({"gy": gy_at(delta)})
+
+    @functools.partial(each, nz - 1, start=2)
     def _(delta):
-        pl.semaphore_signal(barrier, inc=1, device_id={"gz": gz_at(delta)}, device_id_type=MESH)
+        greet({"gz": gz_at(delta)})
 
     loads = [pltpu.make_async_copy(src, dst, in_sem.at[place]) for place, (src, dst) in enumerate(
-        [(sp_hbm, sp), (rs_hbm, nxt), (po_hbm, po), (mo_hbm, mo)])]
-    for load in loads:
-        load.start()
-
-    lane = iota((16, 128), 1)
-    row = iota((16, 128), 0)
-
-    wz[80:128, :] = jnp.zeros((48, 128), F32)
+        [(sp_hbm, sp), (rs_hbm, nxt), (po_hbm, po), (mo_hbm, mo), (cp_hbm, cp), (ids_hbm, ids_ref)])]
+    for place in (4, 0, 1, 5, 2, 3):
+        loads[place].start()
+
+    loads[4].wait()
+    lane = iota((8, 128), 1)
+    row = iota((8, 128), 0)
+    wz[40:128, :] = jnp.zeros((88, 128), F32)
 
     @functools.partial(each, VARS)
     def _(i):
-        value = jnp.zeros((16, 128), F32)
+        value = jnp.zeros((8, 128), F32)
         for j in range(VARS):
-            value = jnp.where((lane >> 4) == j, -COURANT * cp[i, 2, j], value)
-        wz[pl.ds(pl.multiple_of(16 * i, 16), 16), :] = jnp.where((lane & 15) == row, value, 0.0)
+            value = jnp.where((lane >> 3) == j, -COURANT * cp[i, 2, j], value)
+        wz[pl.ds(pl.multiple_of(8 * i, 8), 8), :] = jnp.where((lane & 7) == row, value, 0.0)
 
     loads[0].wait()
 
     lanes = iota((32, 128), 1)
-    odd = (lanes & 1) == 1
-    faces = jnp.zeros((32, 128), F32)
+    near = jnp.zeros((32, 128), F32)
+    far = jnp.zeros((32, 128), F32)
     for x in range(8):
-        ends = jnp.where(lanes == 0, sp[2, x, :, 0:128], sp[2, x, :, 128:256])
-        faces = jnp.where((lanes >> 1) == x, pltpu.roll(ends, 2 * x + 1, axis=1), faces)
-    total = faces
-    for i in range(1, VARS):
-        total = jnp.where((lanes >> 4) == i, pltpu.roll(faces, 16 * i, axis=1), total)
-    total = jnp.where((lanes >> 4) < VARS, total, 0.0)
-    sface[...] = jnp.where(odd, jnp.maximum(total, 0.0), jnp.maximum(-total, 0.0))
+        ends = pltpu.roll(jnp.where(lanes == 0, sp[2, x, :, 0:128], sp[2, x, :, 128:256]), x + 1, axis=1)
+        near = jnp.where(lanes == x + 1, ends, near)
+        far = jnp.where(lanes == x, ends, far)
+    near = pltpu.roll(near, 127, axis=1)
+    for side, face in ((0, jnp.maximum(near, 0.0)), (1, jnp.maximum(-far, 0.0))):
+        total = face
+        for i in range(1, VARS):
+            total = jnp.where((lanes >> 3) == i, pltpu.roll(face, 8 * i, axis=1), total)
+        sface[32 * side:32 * side + 32, :] = jnp.where(lanes < 8 * VARS, total, 0.0)
 
     inside = (gy > 0, gy < ny - 1, gz > 0, gz < nz - 1)
 
@@ -175,7 +184,7 @@
 
     def send_halo(par):
         for place, (axis, delta) in enumerate((("y", -1), ("y", 1), ("z", -1), ("z", 1))):
-            rows = in_rows(place) if axis == "y" else pl.ds(ZAT, 32)
+            rows = in_rows(place)
             target = {"gy": gy_at(delta)} if axis == "y" else {"gz": gz_at(delta)}
             copy = pltpu.make_async_remote_copy(
                 src_ref=halo_out.at[par, rows], dst_ref=halo_in.at[par, in_rows(place ^ 1)],
@@ -194,39 +203,83 @@
 
     halves = (slice(0, 128), slice(128, 256))
 
-    def fix_and_pack(k, par, ufix):
-        for i in range(VARS):
-            for x in range(8):
-                for side, y in ((0, 0), (1, 31)):
-                    for half in range(2):
-                        at = y_at(side, i, half) + x
-                        nxt[i, x, y:y + 1, halves[half]] = nxt[i, x, y:y + 1, halves[half]] + yfix[at:at + 1, :]
-        packed = jnp.zeros((32, 128), F32)
+    def pack():
+        near = jnp.zeros((32, 128), F32)
+        far = jnp.zeros((32, 128), F32)
         for i in range(VARS):
             for x in range(8):
                 s = i * 8 + x
-                fix = pltpu.roll(ufix, 127 - 2 * s, axis=1)
-                near = nxt[i, x, :, 0:128] + jnp.where(lanes == 0, fix, 0.0)
-                far = nxt[i, x, :, 128:256] + jnp.where(lanes == 127, fix, 0.0)
-                cur[i, x, :, 0:128] = near
-                cur[i, x, :, 128:256] = far
-                basis[k, i, x, :, 0:128] = near
-                basis[k, i, x, :, 128:256] = far
-                ends = jnp.where(lanes == 0, near, far)
-                packed = jnp.where((lanes >> 1) == s, pltpu.roll(ends, 2 * s + 1, axis=1), packed)
-        halo_out[par, ZAT:ZAT + 32, :] = jnp.dot(
-            packed * sface[...], wz[...], preferred_element_type=F32, precision=lax.Precision.HIGHEST)
+                ends = jnp.where(lanes == 0, nxt[i, x, :, 0:128], nxt[i, x, :, 128:256])
+                ends = pltpu.roll(ends, s + 1, axis=1)
+                near = jnp.where(lanes == s + 1, ends, near)
+                far = jnp.where(lanes == s, ends, far)
+        zpart[0:32, :] = pltpu.roll(near, 127, axis=1)
+        zpart[32:64, :] = far
+        for side, y in ((0, 0), (1, 31)):
+            for half in range(2):
+                for i in range(VARS):
+                    at = y_at(side, i, half)
+                    ypart[at:at + 8, :] = nxt[i, :, y, halves[half]]
+
+    lane8 = iota((8, 128), 1)
+    rows32 = iota((32, 128), 0)
+
+    def y_corners():
+        for side in range(2):
+            for i in range(VARS):
+                corner[side * 64 + i * 8:side * 64 + i * 8 + 8, :] = jnp.where(
+                    lane8 == 0, yfix[y_at(side, i, 0):y_at(side, i, 0) + 8, :],
+                    yfix[y_at(side, i, 1):y_at(side, i, 1) + 8, :])
+        turn[...] = corner[...].T
+        parts = []
+        for at in (0, 127):
+            both = jnp.broadcast_to(turn[at:at + 1, :], (32, 128))
+            parts.append(jnp.where(rows32 == 0, both, jnp.where(rows32 == 31, pltpu.roll(both, 64, axis=1), 0.0)))
+        return jnp.where(jnp.concatenate([lanes, lanes], axis=0) < 8 * VARS, jnp.concatenate(parts, axis=0), 0.0)
+
+    def finish(k, par):
+        faces = zpart[...] + zfix[...] + y_corners()
+        zheld[k] = faces
+        halo_out[par, ZAT:ZAT + 64, :] = jnp.dot(
+            faces * sface[...], wz[...], preferred_element_type=F32, precision=lax.Precision.HIGHEST)
+        turned_z = jnp.concatenate([zfix[...], jnp.zeros((64, 128), F32)], axis=0).T
         for side, y in ((0, 0), (1, 31)):
             for half in range(2):
                 speed = sp[1, :, y, halves[half]]
                 speed = jnp.maximum(speed, 0.0) if side == 0 else jnp.maximum(-speed, 0.0)
-                flux = [cur[i, :, y, halves[half]] * speed for i in range(VARS)]
+                flux = []
+                for i in range(VARS):
+                    extra = turned_z[8 * i:8 * i + 8]
+                    shift = ((0, 95), (97, 64))[side][half]
+                    extra = pltpu.roll(extra, shift, axis=1) if shift else extra
+                    at = y_at(side, i, half)
+                    value = ypart[at:at + 8, :] + yfix[at:at + 8, :] + jnp.where(lane8 == 127 * half, extra, 0.0)
+                    yheld[k, at:at + 8, :] = value
+                    flux.append(value * speed)
                 for j in range(VARS):
                     total = flux[0] * (-COURANT * cp[0, 1, j])
                     for i in range(1, VARS):
                         total = total + flux[i] * (-COURANT * cp[i, 1, j])
                     at = y_at(side, j, half)
                     halo_out[par, at:at + 8, :] = total
+
+    def settle(k):
+        @functools.partial(each, VARS)
+        def _(i):
+            for x in range(8):
+                for side, y in ((0, 0), (1, 31)):
+                    for half in range(2):
+                        at = pl.ds(side * YROWS + i * 16 + half * 8 + x, 1)
+                        nxt[i, x, y:y + 1, halves[half]] = nxt[i, x, y:y + 1, halves[half]] + yfix[at, :]
+            for x in range(8):
+                near = nxt[i, x, :, 0:128] + jnp.where(
+                    lanes == 0, pltpu.roll(zfix[0:32, :], 128 - 8 * i - x, axis=1), 0.0)
+                far = nxt[i, x, :, 128:256] + jnp.where(
+                    lanes == 127, pltpu.roll(zfix[32:64, :], 127 - 8 * i - x, axis=1), 0.0)
+                cur[i, x, :, 0:128] = near
+                cur[i, x, :, 128:256] = far
+                basis[k, i, x, :, 0:128] = near
+                basis[k, i, x, :, 128:256] = far
 
     def receive(par):
         for place in range(4):
@@ -237,10 +290,8 @@
                 wait_all(ref, halo_send.at[par, place])
         yfix[0:YROWS, :] = halo_in[par, 0:YROWS, :] - halo_out[par, YROWS:ZAT, :]
         yfix[YROWS:ZAT, :] = halo_in[par, YROWS:ZAT, :] - halo_out[par, 0:YROWS, :]
-        own = halo_out[par, ZAT:ZAT + 32, :]
-        from_near = pltpu.roll(halo_in[par, ZAT:ZAT + 32, :] - own, 1, axis=1)
-        from_far = pltpu.roll(halo_in[par, ZAT + 32:ZAT + 64, :] - own, 127, axis=1)
-        yfix[ZAT:ZAT + 32, :] = jnp.where(odd, from_near, from_far)
+        zfix[0:32, :] = halo_in[par, ZAT:ZAT + 32, :] - halo_out[par, ZAT + 32:ZAT + 64, :]
+        zfix[32:64, :] = halo_in[par, ZAT + 32:ZAT + 64, :] - halo_out[par, ZAT:ZAT + 32, :]
 
     def prepare():
         @functools.partial(each, 8)
@@ -268,6 +319,7 @@
             value = jnp.where(same, jnp.where(piece == 2, value - high, high), 0.0)
             wmat[pl.ds(pl.multiple_of(place * 16, 16), 16), :] = value[:, 0:240].astype(BF16)
 
+        loads[5].wait()
         ids = jnp.concatenate([ids_ref[0], ids_ref[1]], axis=1)
         owners = lax.div(ids, per_owner)
         local_row[...] = (ids - owners * per_owner + 1).astype(F32)
@@ -381,71 +433,86 @@
 
     pairs = [(l, k) for k in range(4) for l in range(k + 1)]
 
-    def early(x, sums):
-        sums = list(sums)
-        for j in range(VARS):
-            v = [basis[k, j, x] for k in range(3)]
-            for e, (l, k) in enumerate(pairs[:6]):
-                sums[e] = sums[e] + fold(v[l] * v[k])
-        return tuple(sums)
+    def products(entries, vectors):
+        def body(x, sums):
+            sums = list(sums)
+            for j in range(VARS):
+                v = [nxt[j, x] if k == 3 else basis[k, j, x] for k in range(vectors)]
+                for place, e in enumerate(entries):
+                    l, k = pairs[e]
+                    sums[place] = sums[place] + fold(v[l] * v[k])
+            return tuple(sums)
+
+        sums = lax.fori_loop(0, 8, body, tuple(jnp.zeros((8, 128), F32) for _ in entries))
+        for place, e in enumerate(entries):
+            prods[e] = sums[place]
+
+    def corrections():
+        sums = [jnp.zeros((8, 128), F32) for _ in range(4)]
+        for at in range(0, 2 * YROWS, 8):
+            add = yfix[at:at + 8, :]
+            for l in range(3):
+                sums[l] = sums[l] + yheld[l, at:at + 8, :] * add
+            sums[3] = sums[3] + (2.0 * ypart[at:at + 8, :] + add) * add
+        both = y_corners()
+        for at in range(0, 64, 8):
+            add = zfix[at:at + 8, :]
+            for l in range(3):
+                sums[l] = sums[l] + zheld[l, at:at + 8, :] * add
+            sums[3] = sums[3] + (2.0 * (zpart[at:at + 8, :] + both[at:at + 8]) + add) * add
+        for l in range(4):
+            prods[6 + l] = prods[6 + l] + sums[l]
 
     yfix[...] = jnp.zeros(yfix.shape, F32)
+    zfix[...] = jnp.zeros(zfix.shape, F32)
+    corner[...] = jnp.zeros(corner.shape, F32)
     loads[1].wait()
 
-    @functools.partial(each, 3)
+    @functools.partial(each, 4)
     def _(k):
         par = k & 1
+        pack()
+
+        @pl.when(k == 3)
+        def _():
+            products((6, 7, 8, 9), 4)
 
         @pl.when(k > 0)
         def _():
             receive(1 - par)
 
-        fix_and_pack(k, par, yfix[ZAT:ZAT + 32, :])
-
-        @pl.when(k == 0)
+        @pl.when(k == 3)
         def _():
-            pl.semaphore_wait(barrier, (ny - 1) + (nz - 1))
-
-        send_halo(par)
-
-        @pl.when(k == 0)
+            corrections()
+
+        @pl.when(k < 3)
         def _():
-            prepare()
-            loads[2].wait()
-
-        @pl.when(k == 2)
-        def _():
-            dispatch()
-            done = lax.fori_loop(0, 8, early, tuple(jnp.zeros((8, 128), F32) for _ in range(6)))
-            for e in range(6):
-                prods[e] = done[e]
-
-        sweep()
-
-    receive(0)
-
-    def late(j, sums):
-        sums = list(sums)
-        for x in range(8):
-            for side, y in ((0, 0), (1, 31)):
-                for half in range(2):
-                    at = pl.ds(side * YROWS + j * 16 + half * 8 + x, 1)
-                    nxt[j, x, y:y + 1, halves[half]] = nxt[j, x, y:y + 1, halves[half]] + yfix[at, :]
-        ufix = yfix[ZAT:ZAT + 32, :]
-        for x in range(8):
-            fix = pltpu.roll(ufix, 127 - 16 * j - 2 * x, axis=1)
-            near = nxt[j, x, :, 0:128] + jnp.where(lanes == 0, fix, 0.0)
-            far = nxt[j, x, :, 128:256] + jnp.where(lanes == 127, fix, 0.0)
-            for l in range(4):
-                if l < 3:
-                    product = basis[l, j, x, :, 0:128] * near + basis[l, j, x, :, 128:256] * far
-                else:
-                    product = near * near + far * far
-                sums[l] = sums[l] + (product[0:8] + product[8:16] + product[16:24] + product[24:32])
-        return tuple(sums)
-
-    sums = lax.fori_loop(0, VARS, late, tuple(jnp.zeros((8, 128), F32) for _ in range(4)))
-    sums = [prods[e] for e in range(6)] + list(sums)
+            finish(k, par)
+
+            @pl.when(k == 0)
+            def _():
+                pl.semaphore_wait(barrier, (ny - 1) + (nz - 1))
+
+            send_halo(par)
+            settle(k)
+
+            @pl.when(k == 0)
+            def _():
+                prepare()
+                loads[2].wait()
+
+            @pl.when(k == 1)
+            def _():
+                products((0, 1, 2), 2)
+
+            @pl.when(k == 2)
+            def _():
+                dispatch()
+                products((3, 4, 5), 3)
+
+            sweep()
+
+    sums = [prods[e] for e in range(10)]
 
     lane = iota((8, 128), 1)
     packed = jnp.zeros((8, 128), F32)
@@ -522,6 +589,8 @@
         term = bin_sums[k] * jnp.concatenate([coeffs[k][0:1]] * (per_owner // 128), axis=1)
         sens = term if sens is None else sens + term
     sens_ref[...] = sens
+    sens_copy = pltpu.make_async_copy(sens_ref, sens_hbm, sens_sem)
+    sens_copy.start()
 
     full = [jnp.concatenate([jnp.concatenate([c, c], axis=1)] * 4, axis=0) for c in coeffs]
 
@@ -532,6 +601,7 @@
         pltpu.make_async_copy(nxt.at[j], adj_hbm.at[j], out_sem).start()
 
     wait_all(nxt, out_sem)
+    sens_copy.wait()
 
 
 def local(right_side, speeds, porosity, coupling, momentum, design_ids):
@@ -542,12 +612,11 @@
     field = (VARS, nx, cy, cz)
     dma = pltpu.SemaphoreType.DMA
     hbm = pl.BlockSpec(memory_space=pltpu.HBM)
-    vmem = pl.BlockSpec(memory_space=pltpu.VMEM)
     adjoint, sensitivity = pl.pallas_call(
         functools.partial(kernel, ny, nz, per_owner),
         out_shape=[jax.ShapeDtypeStruct(field, F32), jax.ShapeDtypeStruct((1, per_owner), F32)],
-        in_specs=[hbm, hbm, hbm, pl.BlockSpec(memory_space=pltpu.SMEM), hbm, vmem],
-        out_specs=[hbm, vmem],
+        in_specs=[hbm] * 6,
+        out_specs=[hbm, hbm],
         scratch_shapes=[
             pltpu.VMEM((3,) + field, F32), pltpu.VMEM(field, F32), pltpu.VMEM(field, F32),
             pltpu.VMEM((3, nx, cy, cz), F32),
@@ -559,10 +628,15 @@
             pltpu.VMEM((3, nx, cy, cz), F32), pltpu.VMEM((3, nx, cy, cz), F32),
             pltpu.VMEM((VARS, cy, cz), F32), pltpu.VMEM((VARS, cy, cz), F32),
             pltpu.VMEM((VARS, 2, 40, 128), F32), pltpu.VMEM((VARS, 2, 40, 128), F32),
-            pltpu.VMEM((32, 128), F32),
-            pltpu.VMEM((2, 192, 128), F32), pltpu.VMEM((2, 224, 128), F32), pltpu.VMEM((192, 128), F32),
+            pltpu.VMEM((64, 128), F32),
+            pltpu.VMEM((2, 224, 128), F32), pltpu.VMEM((2, 224, 128), F32), pltpu.VMEM((160, 128), F32), pltpu.VMEM((64, 128), F32),
+            pltpu.VMEM((160, 128), F32), pltpu.VMEM((64, 128), F32), pltpu.VMEM((3, 160, 128), F32), pltpu.VMEM((3, 64, 128), F32),
+            pltpu.VMEM((128, 128), F32), pltpu.VMEM((128, 128), F32),
             pltpu.VMEM((3, 2, cy, cz), F32),
-            pltpu.VMEM((6, 8, 128), F32),
+            pltpu.VMEM((10, 8, 128), F32),
+            pltpu.SMEM((VARS, 3, VARS), F32),
+            pltpu.VMEM(design_ids.shape, jnp.int32),
+            pltpu.VMEM((1, per_owner), F32),
             pltpu.VMEM((ny * nz, 1024), BF16),
             pltpu.VMEM((SLOTS, 1024), F32),
             pltpu.VMEM((8, 128), F32),
@@ -577,7 +651,7 @@
             pltpu.VMEM((ny, 1, 128), F32),
             pltpu.VMEM((1, 128), F32),
             pltpu.VMEM((nz, 1, 128), F32),
-            dma((4,)), dma, dma((2, 4)), dma((2, 4)), dma((2,)), dma((2,)), dma((2,)), dma((2,)),
+            dma((6,)), dma, dma, dma((2, 4)), dma((2, 4)), dma((2,)), dma((2,)), dma((2,)), dma((2,)),
         ],
         compiler_params=pltpu.CompilerParams(
             collective_id=0, has_side_effects=True, vmem_limit_bytes=62 * 1024 * 1024),

time: 37.8 us -> 35.7 us (0.944)
  Pallas kernels: 33.9 us -> 31.7 us
    pallas_call x1, Pallas kernels: 33.9 us -> 31.7 us  [local(): pl.pallas_call(functools.partial(kernel, ny, nz, per_owner), out_shape=[j...]
where the time goes in v4:
time: 35.7 us; the launch traced here: 35.4 us
  Pallas kernels  31.7 us (89%)
  local copies, waits for them, and re-layouts  3.09 us (9%)
  between operations  0.65 us (2%)
    pallas_call x1, Pallas kernels, local(): pl.pallas_call(functools.partial(kernel, ny, nz, per_owner), out_shape=[j...  31.7 us
    unnamed x4, local copies, waits for them, and re-layouts  3.09 us

profile of v4, /device:TPU:1, one launch (start us, length us, event | category | flops | bytes accessed | tf_op | source)
XLA Modules:
  0.0 35.4 jit_solution(10583862275991141741)
XLA Ops:
  0.6 31.7 %shard_map.77 = (f32[5,8,32,256]{3,2,1,0:T(8,128)}, f32[1,256]{1,0:T(1,128)}) custom-call(f32[5,8,32,256]{3,2,1,0:T(8,128)} %rs_hbm.1, f32[3,8,32,256]{3,2,1,0:T(8,128)} %sp_hbm.1, f32[8,32,256]{2,1,0:T(8,128)} %po_hbm.1, f32[5,3,5]{2,1,0:T(4,128)} %bitcast.2, f32[3,8,32,256]{3,2,1,0:T(8,128)} %mo_hbm.1, s32[2,8,64]{2,1,0:T(8,128)} %ids_hbm.1), custom_call_target="tpu_custom_call" | custom-call | tf_op jit(solution)/shard_map/pallas_call | solution.py:615
  32.3 0.0 copy-start
  32.3 2.5 %copy.10 = f32[5,8,32,256]{3,2,1,0:T(8,128)} copy(f32[5,8,32,256]{3,2,1,0:T(8,128)} %get-tuple-element.8) | data formatting | bytes 2621440
  34.8 0.0 copy-done
  34.8 0.6 %copy.11 = f32[256]{0:T(256)} copy(f32[256]{0:T(256)S(1)} %bitcast.3) | data formatting | bytes 2048
Async XLA Ops:
  32.3 2.5 %copy-start = (f32[1,256]{1,0:T(1,128)S(1)}, f32[1,256]{1,0:T(1,128)}, u32[]{:S(2)}) copy-start(f32[1,256]{1,0:T(1,128)} %get-tuple-element.5) | copy-start | bytes 3076

commit v5 on v4

--- a/solution.py
+++ b/solution.py
@@ -98,12 +98,12 @@
 
 def kernel(ny, nz, per_owner,
            rs_hbm, sp_hbm, po_hbm, cp_hbm, mo_hbm, ids_hbm,
-           adj_hbm, sens_hbm,
+           held_hbm, small_hbm,
            basis, cur, nxt, sp, po, mo, wmat, wz, wa, wb, cpos, cneg, part, fprev, low_shift, high_shift, sface,
-           halo_out, halo_in, yfix, zfix, ypart, zpart, yheld, zheld, corner, turn, block, prods, cp, ids_ref, sens_ref,
+           halo_out, halo_in, yfix, zfix, ypart, zpart, yheld, zheld, corner, turn, block, prods, cp, ids_ref, small,
            owner_hot, rank_hot, owner_row, local_row, spread, dsend, recv1, turned, recv2, picked,
            gsend, grecv1, gsend2, grecv2,
-           in_sem, out_sem, sens_sem, halo_send, halo_recv, a1_sem, a2_sem, g1_sem, g2_sem):
+           in_sem, out_sem, small_sem, halo_send, halo_recv, a1_sem, a2_sem, g1_sem, g2_sem):
     gy = lax.axis_index("gy")
     gz = lax.axis_index("gz")
 
@@ -496,6 +496,10 @@
             send_halo(par)
             settle(k)
 
+            @pl.when(k > 0)
+            def _():
+                pltpu.make_async_copy(basis.at[k], held_hbm.at[k - 1], out_sem).start()
+
             @pl.when(k == 0)
             def _():
                 prepare()
@@ -588,20 +592,37 @@
     for k in range(3):
         term = bin_sums[k] * jnp.concatenate([coeffs[k][0:1]] * (per_owner // 128), axis=1)
         sens = term if sens is None else sens + term
-    sens_ref[...] = sens
-    sens_copy = pltpu.make_async_copy(sens_ref, sens_hbm, sens_sem)
-    sens_copy.start()
-
-    full = [jnp.concatenate([jnp.concatenate([c, c], axis=1)] * 4, axis=0) for c in coeffs]
-
-    @functools.partial(each, VARS)
-    def _(j):
+    small[0:1, :] = sens
+    for k in range(3):
+        small[8 + 8 * k:16 + 8 * k, :] = jnp.concatenate([coeffs[k]] * (per_owner // 128), axis=1)
+    copy = pltpu.make_async_copy(small, small_hbm, small_sem)
+    copy.start()
+    wait_all(basis.at[pl.ds(1, 2)], out_sem)
+    copy.wait()
+
+
+def combine(rs_hbm, held_hbm, small_hbm, adj_hbm, sens_hbm, vectors, result, small, load_sem, small_sem, out_sem, sens_sem):
+    get_small = pltpu.make_async_copy(small_hbm, small, small_sem)
+    get_small.start()
+    for j in range(VARS):
+        pltpu.make_async_copy(rs_hbm.at[j], vectors.at[j, 0], load_sem.at[j]).start()
+        for k in range(2):
+            pltpu.make_async_copy(held_hbm.at[k, j], vectors.at[j, 1 + k], load_sem.at[j]).start()
+    get_small.wait()
+    put_sens = pltpu.make_async_copy(small.at[0:1], sens_hbm, sens_sem)
+    put_sens.start()
+    full = [jnp.concatenate([small[8 + 8 * k:16 + 8 * k, :]] * 4, axis=0) for k in range(3)]
+
+    def body(j, carry):
+        pltpu.make_async_copy(vectors.at[j], vectors.at[j], load_sem.at[j]).wait()
         for x in range(8):
-            nxt[j, x] = full[0] * basis[0, j, x] + full[1] * basis[1, j, x] + full[2] * basis[2, j, x]
-        pltpu.make_async_copy(nxt.at[j], adj_hbm.at[j], out_sem).start()
-
-    wait_all(nxt, out_sem)
-    sens_copy.wait()
+            result[j, x] = full[0] * vectors[j, 0, x] + full[1] * vectors[j, 1, x] + full[2] * vectors[j, 2, x]
+        pltpu.make_async_copy(result.at[j], adj_hbm.at[j], out_sem).start()
+        return carry
+
+    lax.fori_loop(0, VARS, body, 0)
+    pltpu.make_async_copy(result, result, out_sem).wait()
+    put_sens.wait()
 
 
 def local(right_side, speeds, porosity, coupling, momentum, design_ids):
@@ -612,9 +633,9 @@
     field = (VARS, nx, cy, cz)
     dma = pltpu.SemaphoreType.DMA
     hbm = pl.BlockSpec(memory_space=pltpu.HBM)
-    adjoint, sensitivity = pl.pallas_call(
+    held, small = pl.pallas_call(
         functools.partial(kernel, ny, nz, per_owner),
-        out_shape=[jax.ShapeDtypeStruct(field, F32), jax.ShapeDtypeStruct((1, per_owner), F32)],
+        out_shape=[jax.ShapeDtypeStruct((2,) + field, F32), jax.ShapeDtypeStruct((32, per_owner), F32)],
         in_specs=[hbm] * 6,
         out_specs=[hbm, hbm],
         scratch_shapes=[
@@ -636,7 +657,7 @@
             pltpu.VMEM((10, 8, 128), F32),
             pltpu.SMEM((VARS, 3, VARS), F32),
             pltpu.VMEM(design_ids.shape, jnp.int32),
-            pltpu.VMEM((1, per_owner), F32),
+            pltpu.VMEM((32, per_owner), F32),
             pltpu.VMEM((ny * nz, 1024), BF16),
             pltpu.VMEM((SLOTS, 1024), F32),
             pltpu.VMEM((8, 128), F32),
@@ -656,6 +677,17 @@
         compiler_params=pltpu.CompilerParams(
             collective_id=0, has_side_effects=True, vmem_limit_bytes=62 * 1024 * 1024),
     )(right_side, speeds, porosity, coupling.transpose(1, 0, 2), momentum, design_ids)
+    adjoint, sensitivity = pl.pallas_call(
+        combine,
+        out_shape=[jax.ShapeDtypeStruct(field, F32), jax.ShapeDtypeStruct((1, per_owner), F32)],
+        in_specs=[hbm] * 3,
+        out_specs=[hbm, hbm],
+        scratch_shapes=[
+            pltpu.VMEM((VARS, 3, nx, cy, cz), F32), pltpu.VMEM(field, F32), pltpu.VMEM((32, per_owner), F32),
+            dma((VARS,)), dma, dma, dma,
+        ],
+        compiler_params=pltpu.CompilerParams(vmem_limit_bytes=62 * 1024 * 1024),
+    )(right_side, held, small)
     return adjoint, sensitivity.reshape(per_owner)
 
 

time: 35.7 us -> 35.1 us (0.983)
  local copies, waits for them, and re-layouts: 3.09 us -> 0 us
  Pallas kernels: 31.7 us -> 34.2 us
    unnamed x4 -> x0, local copies, waits for them, and re-layouts: 3.09 us -> none
    pallas_call x0 -> x1, Pallas kernels: none -> 3.06 us  [local(): pl.pallas_call(combine, out_shape=[jax.ShapeDtypeStruct(field, F32), jax....]
    pallas_call x1, Pallas kernels: 31.7 us -> 31.2 us  [local(): pl.pallas_call(functools.partial(kernel, ny, nz, per_owner), out_shape=[j...]
where the time goes in v5:
time: 35.1 us; the launch traced here: 34.9 us
  Pallas kernels  34.2 us (97%)
  between operations  0.64 us (2%)
    pallas_call x1, Pallas kernels, local(): pl.pallas_call(functools.partial(kernel, ny, nz, per_owner), out_shape=[j...  31.2 us
    pallas_call x1, Pallas kernels, local(): pl.pallas_call(combine, out_shape=[jax.ShapeDtypeStruct(field, F32), jax....  3.06 us

profile of v5, /device:TPU:1, one launch (start us, length us, event | category | flops | bytes accessed | tf_op | source)
XLA Modules:
  0.0 34.9 jit_solution(15979805848187309814)
XLA Ops:
  0.6 31.2 %shard_map.77 = (f32[2,5,8,32,256]{4,3,2,1,0:T(8,128)}, f32[32,256]{1,0:T(8,128)}) custom-call(f32[5,8,32,256]{3,2,1,0:T(8,128)} %rs_hbm.3, f32[3,8,32,256]{3,2,1,0:T(8,128)} %sp_hbm.1, f32[8,32,256]{2,1,0:T(8,128)} %po_hbm.1, f32[5,3,5]{2,1,0:T(4,128)} %bitcast.2, f32[3,8,32,256]{3,2,1,0:T(8,128)} %mo_hbm.1, s32[2,8,64]{2,1,0:T(8,128)} %ids_hbm.1), custom_call_target="tpu_custom_call" | custom-call | tf_op jit(solution)/shard_map/pallas_call | solution.py:636
  31.8 3.1 %shard_map.78 = (f32[5,8,32,256]{3,2,1,0:T(8,128)}, f32[1,256]{1,0:T(1,128)}) custom-call(f32[5,8,32,256]{3,2,1,0:T(8,128)} %rs_hbm.3, f32[2,5,8,32,256]{4,3,2,1,0:T(8,128)} %get-tuple-element.6.held_hbm, f32[32,256]{1,0:T(8,128)} %get-tuple-element.7.small_hbm), custom_call_target="tpu_custom_call" | custom-call | tf_op jit(solution)/shard_map/pallas_call | solution.py:680

commit v6 on v5

--- a/solution.py
+++ b/solution.py
@@ -601,22 +601,15 @@
     copy.wait()
 
 
-def combine(rs_hbm, held_hbm, small_hbm, adj_hbm, sens_hbm, vectors, result, small, load_sem, small_sem, out_sem, sens_sem):
-    get_small = pltpu.make_async_copy(small_hbm, small, small_sem)
-    get_small.start()
-    for j in range(VARS):
-        pltpu.make_async_copy(rs_hbm.at[j], vectors.at[j, 0], load_sem.at[j]).start()
-        for k in range(2):
-            pltpu.make_async_copy(held_hbm.at[k, j], vectors.at[j, 1 + k], load_sem.at[j]).start()
-    get_small.wait()
-    put_sens = pltpu.make_async_copy(small.at[0:1], sens_hbm, sens_sem)
+def combine(rs, held, small, adj_hbm, sens_hbm, result, sens, out_sem, sens_sem):
+    sens[...] = small[0:1, :]
+    put_sens = pltpu.make_async_copy(sens, sens_hbm, sens_sem)
     put_sens.start()
     full = [jnp.concatenate([small[8 + 8 * k:16 + 8 * k, :]] * 4, axis=0) for k in range(3)]
 
     def body(j, carry):
-        pltpu.make_async_copy(vectors.at[j], vectors.at[j], load_sem.at[j]).wait()
         for x in range(8):
-            result[j, x] = full[0] * vectors[j, 0, x] + full[1] * vectors[j, 1, x] + full[2] * vectors[j, 2, x]
+            result[j, x] = full[0] * rs[j, x] + full[1] * held[0, j, x] + full[2] * held[1, j, x]
         pltpu.make_async_copy(result.at[j], adj_hbm.at[j], out_sem).start()
         return carry
 
@@ -637,7 +630,7 @@
         functools.partial(kernel, ny, nz, per_owner),
         out_shape=[jax.ShapeDtypeStruct((2,) + field, F32), jax.ShapeDtypeStruct((32, per_owner), F32)],
         in_specs=[hbm] * 6,
-        out_specs=[hbm, hbm],
+        out_specs=[pl.BlockSpec(memory_space=pl.ANY)] * 2,
         scratch_shapes=[
             pltpu.VMEM((3,) + field, F32), pltpu.VMEM(field, F32), pltpu.VMEM(field, F32),
             pltpu.VMEM((3, nx, cy, cz), F32),
@@ -675,18 +668,16 @@
             dma((6,)), dma, dma, dma((2, 4)), dma((2, 4)), dma((2,)), dma((2,)), dma((2,)), dma((2,)),
         ],
         compiler_params=pltpu.CompilerParams(
-            collective_id=0, has_side_effects=True, vmem_limit_bytes=62 * 1024 * 1024),
-    )(right_side, speeds, porosity, coupling.transpose(1, 0, 2), momentum, design_ids)
+            collective_id=0, has_side_effects=True, vmem_limit_bytes=40 * 1024 * 1024),
+    )(*[pltpu.with_memory_space_constraint(value, pltpu.HBM) for value in (
+        right_side, speeds, porosity, coupling.transpose(1, 0, 2), momentum, design_ids)])
     adjoint, sensitivity = pl.pallas_call(
         combine,
         out_shape=[jax.ShapeDtypeStruct(field, F32), jax.ShapeDtypeStruct((1, per_owner), F32)],
-        in_specs=[hbm] * 3,
+        in_specs=[pl.BlockSpec(memory_space=pltpu.VMEM)] * 3,
         out_specs=[hbm, hbm],
-        scratch_shapes=[
-            pltpu.VMEM((VARS, 3, nx, cy, cz), F32), pltpu.VMEM(field, F32), pltpu.VMEM((32, per_owner), F32),
-            dma((VARS,)), dma, dma, dma,
-        ],
-        compiler_params=pltpu.CompilerParams(vmem_limit_bytes=62 * 1024 * 1024),
+        scratch_shapes=[pltpu.VMEM(field, F32), pltpu.VMEM((1, per_owner), F32), dma, dma],
+        compiler_params=pltpu.CompilerParams(vmem_limit_bytes=24 * 1024 * 1024),
     )(right_side, held, small)
     return adjoint, sensitivity.reshape(per_owner)
 

time: 35.1 us -> 32.7 us (0.932)
  Pallas kernels: 34.2 us -> 31.9 us
    pallas_call x1, Pallas kernels: 3.06 us -> 1.11 us  [local(): pl.pallas_call(combine, out_shape=[jax.ShapeDtypeStruct(field, F32), jax....]
    pallas_call x1, Pallas kernels: 31.2 us -> 30.8 us  [local(): pl.pallas_call(functools.partial(kernel, ny, nz, per_owner), out_shape=[j...]
where the time goes in v6:
time: 32.7 us; the launch traced here: 32.5 us
  Pallas kernels  31.9 us (98%)
  between operations  0.66 us (2%)
    pallas_call x1, Pallas kernels, local(): pl.pallas_call(functools.partial(kernel, ny, nz, per_owner), out_shape=[j...  30.8 us
    pallas_call x1, Pallas kernels, local(): pl.pallas_call(combine, out_shape=[jax.ShapeDtypeStruct(field, F32), jax....  1.11 us

profile of v6, /device:TPU:1, one launch (start us, length us, event | category | flops | bytes accessed | tf_op | source)
XLA Modules:
  0.0 32.5 jit_solution(6883163713551477915)
XLA Ops:
  0.6 0.0 copy-start
  0.6 30.8 %shard_map.77 = (f32[2,5,8,32,256]{4,3,2,1,0:T(8,128)S(1)}, f32[32,256]{1,0:T(8,128)S(1)}) custom-call(f32[5,8,32,256]{3,2,1,0:T(8,128)} %rs.1, f32[3,8,32,256]{3,2,1,0:T(8,128)} %sp_hbm.1, f32[8,32,256]{2,1,0:T(8,128)} %po_hbm.1, f32[5,3,5]{2,1,0:T(4,128)} %bitcast.2, f32[3,8,32,256]{3,2,1,0:T(8,128)} %mo_hbm.1, s32[2,8,64]{2,1,0:T(8,128)} %ids_hbm.1), custom_call_target="tpu_custom_call" | custom-call | tf_op jit(solution)/shard_map/pallas_call | solution.py:629
  31.4 0.0 copy-done
  31.4 1.1 %shard_map.78 = (f32[5,8,32,256]{3,2,1,0:T(8,128)}, f32[1,256]{1,0:T(1,128)}) custom-call(f32[5,8,32,256]{3,2,1,0:T(8,128)S(1)} %copy-done, f32[2,5,8,32,256]{4,3,2,1,0:T(8,128)S(1)} %get-tuple-element.6.held, f32[32,256]{1,0:T(8,128)S(1)} %get-tuple-element.7.small), custom_call_target="tpu_custom_call" | custom-call | tf_op jit(solution)/shard_map/pallas_call | solution.py:674
Async XLA Ops:
  0.6 30.8 %copy-start = (f32[5,8,32,256]{3,2,1,0:T(8,128)S(1)}, f32[5,8,32,256]{3,2,1,0:T(8,128)}, u32[]{:S(2)}) copy-start(f32[5,8,32,256]{3,2,1,0:T(8,128)} %rs.1) | copy-start | bytes 3932164

commit v7 on v6

--- a/solution.py
+++ b/solution.py
@@ -98,12 +98,12 @@
 
 def kernel(ny, nz, per_owner,
            rs_hbm, sp_hbm, po_hbm, cp_hbm, mo_hbm, ids_hbm,
-           held_hbm, small_hbm,
+           held_hbm, small,
            basis, cur, nxt, sp, po, mo, wmat, wz, wa, wb, cpos, cneg, part, fprev, low_shift, high_shift, sface,
-           halo_out, halo_in, yfix, zfix, ypart, zpart, yheld, zheld, corner, turn, block, prods, cp, ids_ref, small,
+           halo_out, halo_in, yfix, zfix, ypart, zpart, yheld, zheld, corner, turn, block, prods, cp, ids_ref,
            owner_hot, rank_hot, owner_row, local_row, spread, dsend, recv1, turned, recv2, picked,
            gsend, grecv1, gsend2, grecv2,
-           in_sem, out_sem, small_sem, halo_send, halo_recv, a1_sem, a2_sem, g1_sem, g2_sem):
+           in_sem, out_sem, halo_send, halo_recv, a1_sem, a2_sem, g1_sem, g2_sem):
     gy = lax.axis_index("gy")
     gz = lax.axis_index("gz")
 
@@ -130,6 +130,11 @@
         greet({"gz": gz_at(delta)})
         greet({"gy": gy_at(delta)})
 
+    loads = [pltpu.make_async_copy(src, dst, in_sem.at[place]) for place, (src, dst) in enumerate(
+        [(sp_hbm, sp), (rs_hbm, nxt), (po_hbm, po), (mo_hbm, mo), (cp_hbm, cp), (ids_hbm, ids_ref)])]
+    for place in (4, 0, 1):
+        loads[place].start()
+
     @functools.partial(each, ny - 1, start=2)
     def _(delta):
         greet({"gy": gy_at(delta)})
@@ -138,9 +143,7 @@
     def _(delta):
         greet({"gz": gz_at(delta)})
 
-    loads = [pltpu.make_async_copy(src, dst, in_sem.at[place]) for place, (src, dst) in enumerate(
-        [(sp_hbm, sp), (rs_hbm, nxt), (po_hbm, po), (mo_hbm, mo), (cp_hbm, cp), (ids_hbm, ids_ref)])]
-    for place in (4, 0, 1, 5, 2, 3):
+    for place in (2, 5, 3):
         loads[place].start()
 
     loads[4].wait()
@@ -319,6 +322,7 @@
             value = jnp.where(same, jnp.where(piece == 2, value - high, high), 0.0)
             wmat[pl.ds(pl.multiple_of(place * 16, 16), 16), :] = value[:, 0:240].astype(BF16)
 
+    def rank_slots():
         loads[5].wait()
         ids = jnp.concatenate([ids_ref[0], ids_ref[1]], axis=1)
         owners = lax.div(ids, per_owner)
@@ -508,6 +512,7 @@
             @pl.when(k == 1)
             def _():
                 products((0, 1, 2), 2)
+                rank_slots()
 
             @pl.when(k == 2)
             def _():
@@ -595,10 +600,7 @@
     small[0:1, :] = sens
     for k in range(3):
         small[8 + 8 * k:16 + 8 * k, :] = jnp.concatenate([coeffs[k]] * (per_owner // 128), axis=1)
-    copy = pltpu.make_async_copy(small, small_hbm, small_sem)
-    copy.start()
     wait_all(basis.at[pl.ds(1, 2)], out_sem)
-    copy.wait()
 
 
 def combine(rs, held, small, adj_hbm, sens_hbm, result, sens, out_sem, sens_sem):
@@ -630,7 +632,7 @@
         functools.partial(kernel, ny, nz, per_owner),
         out_shape=[jax.ShapeDtypeStruct((2,) + field, F32), jax.ShapeDtypeStruct((32, per_owner), F32)],
         in_specs=[hbm] * 6,
-        out_specs=[pl.BlockSpec(memory_space=pl.ANY)] * 2,
+        out_specs=[pl.BlockSpec(memory_space=pl.ANY), pl.BlockSpec(memory_space=pltpu.VMEM)],
         scratch_shapes=[
             pltpu.VMEM((3,) + field, F32), pltpu.VMEM(field, F32), pltpu.VMEM(field, F32),
             pltpu.VMEM((3, nx, cy, cz), F32),
@@ -650,7 +652,6 @@
             pltpu.VMEM((10, 8, 128), F32),
             pltpu.SMEM((VARS, 3, VARS), F32),
             pltpu.VMEM(design_ids.shape, jnp.int32),
-            pltpu.VMEM((32, per_owner), F32),
             pltpu.VMEM((ny * nz, 1024), BF16),
             pltpu.VMEM((SLOTS, 1024), F32),
             pltpu.VMEM((8, 128), F32),
@@ -665,7 +666,7 @@
             pltpu.VMEM((ny, 1, 128), F32),
             pltpu.VMEM((1, 128), F32),
             pltpu.VMEM((nz, 1, 128), F32),
-            dma((6,)), dma, dma, dma((2, 4)), dma((2, 4)), dma((2,)), dma((2,)), dma((2,)), dma((2,)),
+            dma((6,)), dma, dma((2, 4)), dma((2, 4)), dma((2,)), dma((2,)), dma((2,)), dma((2,)),
         ],
         compiler_params=pltpu.CompilerParams(
             collective_id=0, has_side_effects=True, vmem_limit_bytes=40 * 1024 * 1024),

time: 32.7 us -> 32.6 us (level)
  no operation moved by 1% of the time
where the time goes in v7:
time: 32.6 us; the launch traced here: 32.4 us
  Pallas kernels  31.7 us (97%)
  between operations  0.66 us (2%)
    pallas_call x1, Pallas kernels, local(): pl.pallas_call(functools.partial(kernel, ny, nz, per_owner), out_shape=[j...  30.6 us
    pallas_call x1, Pallas kernels, local(): pl.pallas_call(combine, out_shape=[jax.ShapeDtypeStruct(field, F32), jax....  1.11 us

profile of v7, /device:TPU:1, one launch (start us, length us, event | category | flops | bytes accessed | tf_op | source)
XLA Modules:
  0.0 32.4 jit_solution(2423714216357543778)
XLA Ops:
  0.6 0.0 copy-start
  0.6 30.6 %shard_map.77 = (f32[2,5,8,32,256]{4,3,2,1,0:T(8,128)S(1)}, f32[32,256]{1,0:T(8,128)S(1)}) custom-call(f32[5,8,32,256]{3,2,1,0:T(8,128)} %rs.1, f32[3,8,32,256]{3,2,1,0:T(8,128)} %sp_hbm.1, f32[8,32,256]{2,1,0:T(8,128)} %po_hbm.1, f32[5,3,5]{2,1,0:T(4,128)} %bitcast.2, f32[3,8,32,256]{3,2,1,0:T(8,128)} %mo_hbm.1, s32[2,8,64]{2,1,0:T(8,128)} %ids_hbm.1), custom_call_target="tpu_custom_call" | custom-call | tf_op jit(solution)/shard_map/pallas_call | solution.py:631
  31.3 0.0 copy-done
  31.3 1.1 %shard_map.78 = (f32[5,8,32,256]{3,2,1,0:T(8,128)}, f32[1,256]{1,0:T(1,128)}) custom-call(f32[5,8,32,256]{3,2,1,0:T(8,128)S(1)} %copy-done, f32[2,5,8,32,256]{4,3,2,1,0:T(8,128)S(1)} %get-tuple-element.6.held, f32[32,256]{1,0:T(8,128)S(1)} %get-tuple-element.7.small), custom_call_target="tpu_custom_call" | custom-call | tf_op jit(solution)/shard_map/pallas_call | solution.py:675
Async XLA Ops:
  0.6 30.6 %copy-start = (f32[5,8,32,256]{3,2,1,0:T(8,128)S(1)}, f32[5,8,32,256]{3,2,1,0:T(8,128)}, u32[]{:S(2)}) copy-start(f32[5,8,32,256]{3,2,1,0:T(8,128)} %rs.1) | copy-start | bytes 3932164

commit v8 on v7

--- a/solution.py
+++ b/solution.py
@@ -102,8 +102,8 @@
            basis, cur, nxt, sp, po, mo, wmat, wz, wa, wb, cpos, cneg, part, fprev, low_shift, high_shift, sface,
            halo_out, halo_in, yfix, zfix, ypart, zpart, yheld, zheld, corner, turn, block, prods, cp, ids_ref,
            owner_hot, rank_hot, owner_row, local_row, spread, dsend, recv1, turned, recv2, picked,
-           gsend, grecv1, gsend2, grecv2,
-           in_sem, out_sem, halo_send, halo_recv, a1_sem, a2_sem, g1_sem, g2_sem):
+           gsend, grecv,
+           in_sem, out_sem, halo_send, halo_recv, a1_sem, a2_sem, g_sem, known_sem):
     gy = lax.axis_index("gy")
     gz = lax.axis_index("gz")
 
@@ -498,6 +498,13 @@
                 pl.semaphore_wait(barrier, (ny - 1) + (nz - 1))
 
             send_halo(par)
+
+            @pl.when(k == 0)
+            def _():
+                @functools.partial(each, nz, start=1)
+                def _(delta):
+                    pl.semaphore_signal(known_sem, inc=1, device_id={"gz": gz_at(delta)}, device_id_type=MESH)
+
             settle(k)
 
             @pl.when(k > 0)
@@ -531,11 +538,18 @@
         packed = jnp.where((lane >> 3) == e, value, packed)
     gsend[...] = jnp.sum(packed, axis=0, keepdims=True)
 
-    @functools.partial(each, ny, start=1)
-    def _(delta):
-        pltpu.make_async_remote_copy(
-            src_ref=gsend, dst_ref=grecv1.at[delta], send_sem=g1_sem.at[0], recv_sem=g1_sem.at[1],
-            device_id={"gy": gy_at(delta)}, device_id_type=MESH).start()
+    pl.semaphore_wait(known_sem, nz - 1)
+
+    def send_gram(a):
+        @functools.partial(each, nz, start=0 if a else 1)
+        def _(b):
+            pltpu.make_async_remote_copy(
+                src_ref=gsend, dst_ref=grecv.at[pl.ds(a * nz + b, 1)], send_sem=g_sem.at[0], recv_sem=g_sem.at[1],
+                device_id={"gy": gy_at(a), "gz": gz_at(b)}, device_id_type=MESH).start()
+
+    order = sorted(range(ny), key=lambda a: -min(a, ny - a))
+    for a in order[:ny // 2]:
+        send_gram(a)
 
     wait_all(recv1.at[pl.ds(1, ny - 1)], a1_sem.at[1])
     wait_all(recv1.at[pl.ds(1, ny - 1)], a1_sem.at[0])
@@ -549,18 +563,8 @@
             device_id={"gz": gz_at(delta)}, device_id_type=MESH).start()
     recv2[0] = turned[gz]
 
-    wait_all(grecv1.at[pl.ds(1, ny - 1)], g1_sem.at[1])
-    wait_all(grecv1.at[pl.ds(1, ny - 1)], g1_sem.at[0])
-    own = gsend[...]
-    for delta in range(1, ny):
-        own = own + grecv1[delta]
-    gsend2[...] = own
-
-    @functools.partial(each, nz, start=1)
-    def _(delta):
-        pltpu.make_async_remote_copy(
-            src_ref=gsend2, dst_ref=grecv2.at[delta], send_sem=g2_sem.at[0], recv_sem=g2_sem.at[1],
-            device_id={"gz": gz_at(delta)}, device_id_type=MESH).start()
+    for a in order[ny // 2:]:
+        send_gram(a)
 
     wait_all(recv2.at[pl.ds(1, nz - 1)], a2_sem.at[1])
     wait_all(recv2.at[pl.ds(1, nz - 1)], a2_sem.at[0])
@@ -580,11 +584,12 @@
     bins = jnp.where((iota((48, 256), 1) >> 4) == (iota((48, 256), 0) & 15), bins, 0.0)
     bin_sums = [jnp.sum(bins[16 * k:16 * k + 16], axis=0, keepdims=True) for k in range(3)]
 
-    wait_all(grecv2.at[pl.ds(1, nz - 1)], g2_sem.at[1])
-    wait_all(grecv2.at[pl.ds(1, nz - 1)], g2_sem.at[0])
-    own = gsend2[...]
-    for delta in range(1, nz):
-        own = own + grecv2[delta]
+    wait_all(grecv.at[pl.ds(1, number - 1)], g_sem.at[1])
+    wait_all(grecv.at[pl.ds(1, number - 1)], g_sem.at[0])
+    own = jnp.where(iota((8, 128), 0) == 0, gsend[...], grecv[0:8, :])
+    for at in range(8, number, 8):
+        own = own + grecv[at:at + 8, :]
+    own = jnp.sum(own, axis=0, keepdims=True)
     for shift in (4, 2, 1):
         own = own + pltpu.roll(own, shift, axis=1)
     own = jnp.broadcast_to(own, (8, 128))
@@ -663,10 +668,8 @@
             pltpu.VMEM((nz, ny, 128), F32),
             pltpu.VMEM((128, 128), F32),
             pltpu.VMEM((1, 128), F32),
-            pltpu.VMEM((ny, 1, 128), F32),
-            pltpu.VMEM((1, 128), F32),
-            pltpu.VMEM((nz, 1, 128), F32),
-            dma((6,)), dma, dma((2, 4)), dma((2, 4)), dma((2,)), dma((2,)), dma((2,)), dma((2,)),
+            pltpu.VMEM((ny * nz, 128), F32),
+            dma((6,)), dma, dma((2, 4)), dma((2, 4)), dma((2,)), dma((2,)), dma((2,)), pltpu.SemaphoreType.REGULAR,
         ],
         compiler_params=pltpu.CompilerParams(
             collective_id=0, has_side_effects=True, vmem_limit_bytes=40 * 1024 * 1024),

time: 32.6 us -> 31.9 us (0.979)
  Pallas kernels: 31.7 us -> 31.1 us
    pallas_call x1, Pallas kernels: 30.6 us -> 30 us  [local(): pl.pallas_call(functools.partial(kernel, ny, nz, per_owner), out_shape=[j...]
where the time goes in v8:
time: 31.9 us; the launch traced here: 31.8 us
  Pallas kernels  31.1 us (97%)
  between operations  0.66 us (2%)
    pallas_call x1, Pallas kernels, local(): pl.pallas_call(functools.partial(kernel, ny, nz, per_owner), out_shape=[j...  30 us
    pallas_call x1, Pallas kernels, local(): pl.pallas_call(combine, out_shape=[jax.ShapeDtypeStruct(field, F32), jax....  1.11 us

profile of v8, /device:TPU:1, one launch (start us, length us, event | category | flops | bytes accessed | tf_op | source)
XLA Modules:
  0.0 31.8 jit_solution(1206730061606166177)
XLA Ops:
  0.6 0.0 copy-start
  0.6 30.0 %shard_map.77 = (f32[2,5,8,32,256]{4,3,2,1,0:T(8,128)S(1)}, f32[32,256]{1,0:T(8,128)S(1)}) custom-call(f32[5,8,32,256]{3,2,1,0:T(8,128)} %rs.1, f32[3,8,32,256]{3,2,1,0:T(8,128)} %sp_hbm.1, f32[8,32,256]{2,1,0:T(8,128)} %po_hbm.1, f32[5,3,5]{2,1,0:T(4,128)} %bitcast.2, f32[3,8,32,256]{3,2,1,0:T(8,128)} %mo_hbm.1, s32[2,8,64]{2,1,0:T(8,128)} %ids_hbm.1), custom_call_target="tpu_custom_call" | custom-call | tf_op jit(solution)/shard_map/pallas_call | solution.py:636
  30.7 0.0 copy-done
  30.7 1.1 %shard_map.78 = (f32[5,8,32,256]{3,2,1,0:T(8,128)}, f32[1,256]{1,0:T(1,128)}) custom-call(f32[5,8,32,256]{3,2,1,0:T(8,128)S(1)} %copy-done, f32[2,5,8,32,256]{4,3,2,1,0:T(8,128)S(1)} %get-tuple-element.6.held, f32[32,256]{1,0:T(8,128)S(1)} %get-tuple-element.7.small), custom_call_target="tpu_custom_call" | custom-call | tf_op jit(solution)/shard_map/pallas_call | solution.py:678
Async XLA Ops:
  0.6 30.0 %copy-start = (f32[5,8,32,256]{3,2,1,0:T(8,128)S(1)}, f32[5,8,32,256]{3,2,1,0:T(8,128)}, u32[]{:S(2)}) copy-start(f32[5,8,32,256]{3,2,1,0:T(8,128)} %rs.1) | copy-start | bytes 3932164

commit v9 on v8

--- a/solution.py
+++ b/solution.py
@@ -110,16 +110,16 @@
     number = ny * nz
 
     def gy_at(delta):
-        return lax.rem(gy + (delta + ny), ny)
+        return (gy + (delta + ny)) & (ny - 1)
 
     def gz_at(delta):
-        return lax.rem(gz + (delta + nz), nz)
-
-    def each(count, step, start=0):
+        return (gz + (delta + nz)) & (nz - 1)
+
+    def each(count, step, start=0, unroll=1):
         def body(t, carry):
             step(t)
             return carry
-        lax.fori_loop(start, count, body, 0)
+        lax.fori_loop(start, count, body, 0, unroll=unroll)
 
     barrier = pltpu.get_barrier_semaphore()
 
@@ -267,22 +267,26 @@
                     halo_out[par, at:at + 8, :] = total
 
     def settle(k):
-        @functools.partial(each, VARS)
-        def _(i):
+        even = (lanes & 1) == 0
+        near_columns = zfix[0:32, :]
+        far_columns = pltpu.roll(zfix[32:64, :], 127, axis=1)
+        columns = [jnp.where(even, near_columns, far_columns), jnp.where(even, far_columns, near_columns)]
+        row8 = iota((8, 128), 0)
+        for i in range(VARS):
             for x in range(8):
-                for side, y in ((0, 0), (1, 31)):
-                    for half in range(2):
-                        at = pl.ds(side * YROWS + i * 16 + half * 8 + x, 1)
-                        nxt[i, x, y:y + 1, halves[half]] = nxt[i, x, y:y + 1, halves[half]] + yfix[at, :]
-            for x in range(8):
-                near = nxt[i, x, :, 0:128] + jnp.where(
-                    lanes == 0, pltpu.roll(zfix[0:32, :], 128 - 8 * i - x, axis=1), 0.0)
-                far = nxt[i, x, :, 128:256] + jnp.where(
-                    lanes == 127, pltpu.roll(zfix[32:64, :], 127 - 8 * i - x, axis=1), 0.0)
-                cur[i, x, :, 0:128] = near
-                cur[i, x, :, 128:256] = far
-                basis[k, i, x, :, 0:128] = near
-                basis[k, i, x, :, 128:256] = far
+                s = i * 8 + x
+                fix = pltpu.roll(columns[s & 1], 128 - s, axis=1) if s else columns[0]
+                for half in range(2):
+                    at = y_at(0, i, half) + x
+                    top = jnp.where(row8 == 0, yfix[at:at + 1, :], 0.0)
+                    at = y_at(1, i, half) + x
+                    bottom = jnp.where(row8 == 7, yfix[at:at + 1, :], 0.0)
+                    side = jnp.where(lanes == 127 * half, fix, 0.0)
+                    value = jnp.concatenate([
+                        nxt[i, x, 0:8, halves[half]] + top, nxt[i, x, 8:24, halves[half]],
+                        nxt[i, x, 24:32, halves[half]] + bottom], axis=0) + side
+                    cur[i, x, :, halves[half]] = value
+                    basis[k, i, x, :, halves[half]] = value
 
     def receive(par):
         for place in range(4):
@@ -541,11 +545,13 @@
     pl.semaphore_wait(known_sem, nz - 1)
 
     def send_gram(a):
-        @functools.partial(each, nz, start=0 if a else 1)
+        row = gy_at(a)
+
+        @functools.partial(each, nz, start=0 if a else 1, unroll=8 if a else 5)
         def _(b):
             pltpu.make_async_remote_copy(
                 src_ref=gsend, dst_ref=grecv.at[pl.ds(a * nz + b, 1)], send_sem=g_sem.at[0], recv_sem=g_sem.at[1],
-                device_id={"gy": gy_at(a), "gz": gz_at(b)}, device_id_type=MESH).start()
+                device_id={"gy": row, "gz": gz_at(b)}, device_id_type=MESH).start()
 
     order = sorted(range(ny), key=lambda a: -min(a, ny - a))
     for a in order[:ny // 2]:

time: 31.9 us -> 30.8 us (0.966)
  Pallas kernels: 31.1 us -> 30 us
    pallas_call x1, Pallas kernels: 30 us -> 28.9 us  [local(): pl.pallas_call(functools.partial(kernel, ny, nz, per_owner), out_shape=[j...]
where the time goes in v9:
time: 30.8 us; the launch traced here: 30.7 us
  Pallas kernels  30 us (97%)
  between operations  0.66 us (2%)
    pallas_call x1, Pallas kernels, local(): pl.pallas_call(functools.partial(kernel, ny, nz, per_owner), out_shape=[j...  28.9 us
    pallas_call x1, Pallas kernels, local(): pl.pallas_call(combine, out_shape=[jax.ShapeDtypeStruct(field, F32), jax....  1.11 us

profile of v9, /device:TPU:1, one launch (start us, length us, event | category | flops | bytes accessed | tf_op | source)
XLA Modules:
  0.0 30.7 jit_solution(13098905483950870861)
XLA Ops:
  0.6 0.0 copy-start
  0.6 28.9 %shard_map.77 = (f32[2,5,8,32,256]{4,3,2,1,0:T(8,128)S(1)}, f32[32,256]{1,0:T(8,128)S(1)}) custom-call(f32[5,8,32,256]{3,2,1,0:T(8,128)} %rs.1, f32[3,8,32,256]{3,2,1,0:T(8,128)} %sp_hbm.1, f32[8,32,256]{2,1,0:T(8,128)} %po_hbm.1, f32[5,3,5]{2,1,0:T(4,128)} %bitcast.2, f32[3,8,32,256]{3,2,1,0:T(8,128)} %mo_hbm.1, s32[2,8,64]{2,1,0:T(8,128)} %ids_hbm.1), custom_call_target="tpu_custom_call" | custom-call | tf_op jit(solution)/shard_map/pallas_call | solution.py:642
  29.6 0.0 copy-done
  29.6 1.1 %shard_map.78 = (f32[5,8,32,256]{3,2,1,0:T(8,128)}, f32[1,256]{1,0:T(1,128)}) custom-call(f32[5,8,32,256]{3,2,1,0:T(8,128)S(1)} %copy-done, f32[2,5,8,32,256]{4,3,2,1,0:T(8,128)S(1)} %get-tuple-element.6.held, f32[32,256]{1,0:T(8,128)S(1)} %get-tuple-element.7.small), custom_call_target="tpu_custom_call" | custom-call | tf_op jit(solution)/shard_map/pallas_call | solution.py:684
Async XLA Ops:
  0.6 28.9 %copy-start = (f32[5,8,32,256]{3,2,1,0:T(8,128)S(1)}, f32[5,8,32,256]{3,2,1,0:T(8,128)}, u32[]{:S(2)}) copy-start(f32[5,8,32,256]{3,2,1,0:T(8,128)} %rs.1) | copy-start | bytes 3932164

commit v10 on v9

--- a/solution.py
+++ b/solution.py
@@ -132,7 +132,7 @@
 
     loads = [pltpu.make_async_copy(src, dst, in_sem.at[place]) for place, (src, dst) in enumerate(
         [(sp_hbm, sp), (rs_hbm, nxt), (po_hbm, po), (mo_hbm, mo), (cp_hbm, cp), (ids_hbm, ids_ref)])]
-    for place in (4, 0, 1):
+    for place in (4, 5, 0, 1):
         loads[place].start()
 
     @functools.partial(each, ny - 1, start=2)
@@ -143,7 +143,7 @@
     def _(delta):
         greet({"gz": gz_at(delta)})
 
-    for place in (2, 5, 3):
+    for place in (2, 3):
         loads[place].start()
 
     loads[4].wait()
@@ -157,6 +157,40 @@
         for j in range(VARS):
             value = jnp.where((lane >> 3) == j, -COURANT * cp[i, 2, j], value)
         wz[pl.ds(pl.multiple_of(8 * i, 8), 8), :] = jnp.where((lane & 7) == row, value, 0.0)
+
+    lane = iota((16, 256), 1)
+    row = iota((16, 256), 0)
+    group = lane >> 4
+    piece = jnp.where(group >= 10, 2, jnp.where(group >= 5, 1, 0))
+    which = group - 5 * piece
+    same = (lane & 15) == row
+
+    @functools.partial(each, 3 * VARS)
+    def _(place):
+        d = lax.div(place, VARS)
+        j = place - d * VARS
+        value = jnp.zeros((16, 256), F32)
+        for i in range(VARS):
+            value = jnp.where(which == i, COURANT * cp[i, d, j], value)
+        high = value.astype(BF16).astype(F32)
+        value = jnp.where(same, jnp.where(piece == 2, value - high, high), 0.0)
+        wmat[pl.ds(pl.multiple_of(place * 16, 16), 16), :] = value[:, 0:240].astype(BF16)
+
+    loads[5].wait()
+    ids = jnp.concatenate([ids_ref[0], ids_ref[1]], axis=1)
+    owners = lax.div(ids, per_owner)
+    local_row[...] = (ids - owners * per_owner + 1).astype(F32)
+    tri = jnp.where(iota((256, 128), 0) < jnp.where(iota((256, 128), 0) >= 128, 256, iota((256, 128), 1)), 1.0, 0.0).astype(BF16)
+    sub = iota((number, 128), 0)
+    before = jnp.zeros((number, 128), F32)
+    for p in range(8):
+        hot = jnp.where(sub == owners[p:p + 1, :], 1.0, 0.0)
+        hot16 = hot.astype(BF16)
+        count = dot(jnp.concatenate([hot16, before.astype(BF16)], axis=1), tri)
+        before = before + hot
+        owner_hot[:, p * 128:(p + 1) * 128] = hot16
+        rank = jnp.sum(hot * count, axis=0, keepdims=True)
+        rank_hot[:, p * 128:(p + 1) * 128] = jnp.where(rank == iota((SLOTS, 128), 0).astype(F32), 1.0, 0.0)
 
     loads[0].wait()
 
@@ -308,42 +342,6 @@
                 cpos[d, x] = jnp.maximum(s, 0.0)
                 cneg[d, x] = jnp.maximum(-s, 0.0)
 
-        lane = iota((16, 256), 1)
-        row = iota((16, 256), 0)
-        group = lane >> 4
-        piece = jnp.where(group >= 10, 2, jnp.where(group >= 5, 1, 0))
-        which = group - 5 * piece
-        same = (lane & 15) == row
-
-        @functools.partial(each, 3 * VARS)
-        def _(place):
-            d = lax.div(place, VARS)
-            j = place - d * VARS
-            value = jnp.zeros((16, 256), F32)
-            for i in range(VARS):
-                value = jnp.where(which == i, COURANT * cp[i, d, j], value)
-            high = value.astype(BF16).astype(F32)
-            value = jnp.where(same, jnp.where(piece == 2, value - high, high), 0.0)
-            wmat[pl.ds(pl.multiple_of(place * 16, 16), 16), :] = value[:, 0:240].astype(BF16)
-
-    def rank_slots():
-        loads[5].wait()
-        ids = jnp.concatenate([ids_ref[0], ids_ref[1]], axis=1)
-        owners = lax.div(ids, per_owner)
-        local_row[...] = (ids - owners * per_owner + 1).astype(F32)
-        tri = jnp.where(iota((256, 128), 0) < jnp.where(iota((256, 128), 0) >= 128, 256, iota((256, 128), 1)), 1.0, 0.0).astype(BF16)
-        sub = iota((number, 128), 0)
-        before = jnp.zeros((number, 128), F32)
-        for p in range(8):
-            hot = jnp.where(sub == owners[p:p + 1, :], 1.0, 0.0)
-            hot16 = hot.astype(BF16)
-            count = dot(jnp.concatenate([hot16, before.astype(BF16)], axis=1), tri)
-            before = before + hot
-            owner_hot[:, p * 128:(p + 1) * 128] = hot16
-            rank = jnp.sum(hot * count, axis=0, keepdims=True)
-            rank_hot[:, p * 128:(p + 1) * 128] = jnp.where(rank == iota((SLOTS, 128), 0).astype(F32), 1.0, 0.0)
-
-
     def couple(x, w):
         for h in (0, 16):
             high, low = [], []
@@ -523,7 +521,6 @@
             @pl.when(k == 1)
             def _():
                 products((0, 1, 2), 2)
-                rank_slots()
 
             @pl.when(k == 2)
             def _():

time: 30.8 us -> 30.6 us (level)
  no operation moved by 1% of the time
where the time goes in v10:
time: 30.6 us; the launch traced here: 30.5 us
  Pallas kernels  29.9 us (98%)
  between operations  0.66 us (2%)
    pallas_call x1, Pallas kernels, local(): pl.pallas_call(functools.partial(kernel, ny, nz, per_owner), out_shape=[j...  28.8 us
    pallas_call x1, Pallas kernels, local(): pl.pallas_call(combine, out_shape=[jax.ShapeDtypeStruct(field, F32), jax....  1.11 us

profile of v10, /device:TPU:1, one launch (start us, length us, event | category | flops | bytes accessed | tf_op | source)
XLA Modules:
  0.0 30.5 jit_solution(16112226257413341334)
XLA Ops:
  0.6 0.0 copy-start
  0.6 28.8 %shard_map.77 = (f32[2,5,8,32,256]{4,3,2,1,0:T(8,128)S(1)}, f32[32,256]{1,0:T(8,128)S(1)}) custom-call(f32[5,8,32,256]{3,2,1,0:T(8,128)} %rs.1, f32[3,8,32,256]{3,2,1,0:T(8,128)} %sp_hbm.1, f32[8,32,256]{2,1,0:T(8,128)} %po_hbm.1, f32[5,3,5]{2,1,0:T(4,128)} %bitcast.2, f32[3,8,32,256]{3,2,1,0:T(8,128)} %mo_hbm.1, s32[2,8,64]{2,1,0:T(8,128)} %ids_hbm.1), custom_call_target="tpu_custom_call" | custom-call | tf_op jit(solution)/shard_map/pallas_call | solution.py:639
  29.4 0.0 copy-done
  29.4 1.1 %shard_map.78 = (f32[5,8,32,256]{3,2,1,0:T(8,128)}, f32[1,256]{1,0:T(1,128)}) custom-call(f32[5,8,32,256]{3,2,1,0:T(8,128)S(1)} %copy-done, f32[2,5,8,32,256]{4,3,2,1,0:T(8,128)S(1)} %get-tuple-element.6.held, f32[32,256]{1,0:T(8,128)S(1)} %get-tuple-element.7.small), custom_call_target="tpu_custom_call" | custom-call | tf_op jit(solution)/shard_map/pallas_call | solution.py:681
Async XLA Ops:
  0.6 28.8 %copy-start = (f32[5,8,32,256]{3,2,1,0:T(8,128)S(1)}, f32[5,8,32,256]{3,2,1,0:T(8,128)}, u32[]{:S(2)}) copy-start(f32[5,8,32,256]{3,2,1,0:T(8,128)} %rs.1) | copy-start | bytes 3932164

commit v11 on v10

--- a/solution.py
+++ b/solution.py
@@ -131,8 +131,9 @@
         greet({"gy": gy_at(delta)})
 
     loads = [pltpu.make_async_copy(src, dst, in_sem.at[place]) for place, (src, dst) in enumerate(
-        [(sp_hbm, sp), (rs_hbm, nxt), (po_hbm, po), (mo_hbm, mo), (cp_hbm, cp), (ids_hbm, ids_ref)])]
-    for place in (4, 5, 0, 1):
+        [(sp_hbm, sp), (rs_hbm, basis.at[0]), (po_hbm, po), (mo_hbm, mo), (cp_hbm, cp), (ids_hbm, ids_ref)]
+        + [(rs_hbm.at[i], cur.at[i]) for i in range(VARS)])]
+    for place in [4, 5, 0] + list(range(6, 6 + VARS)):
         loads[place].start()
 
     @functools.partial(each, ny - 1, start=2)
@@ -143,7 +144,7 @@
     def _(delta):
         greet({"gz": gz_at(delta)})
 
-    for place in (2, 3):
+    for place in (2, 1, 3):
         loads[place].start()
 
     loads[4].wait()
@@ -240,13 +241,15 @@
 
     halves = (slice(0, 128), slice(128, 256))
 
-    def pack():
+    def pack(src, arrive=None):
         near = jnp.zeros((32, 128), F32)
         far = jnp.zeros((32, 128), F32)
         for i in range(VARS):
+            if arrive is not None:
+                arrive(i)
             for x in range(8):
                 s = i * 8 + x
-                ends = jnp.where(lanes == 0, nxt[i, x, :, 0:128], nxt[i, x, :, 128:256])
+                ends = jnp.where(lanes == 0, src[i, x, :, 0:128], src[i, x, :, 128:256])
                 ends = pltpu.roll(ends, s + 1, axis=1)
                 near = jnp.where(lanes == s + 1, ends, near)
                 far = jnp.where(lanes == s, ends, far)
@@ -256,7 +259,7 @@
             for half in range(2):
                 for i in range(VARS):
                     at = y_at(side, i, half)
-                    ypart[at:at + 8, :] = nxt[i, :, y, halves[half]]
+                    ypart[at:at + 8, :] = src[i, :, y, halves[half]]
 
     lane8 = iota((8, 128), 1)
     rows32 = iota((32, 128), 0)
@@ -274,23 +277,26 @@
             parts.append(jnp.where(rows32 == 0, both, jnp.where(rows32 == 31, pltpu.roll(both, 64, axis=1), 0.0)))
         return jnp.where(jnp.concatenate([lanes, lanes], axis=0) < 8 * VARS, jnp.concatenate(parts, axis=0), 0.0)
 
-    def finish(k, par):
-        faces = zpart[...] + zfix[...] + y_corners()
+    def finish(k, par, fixed=True):
+        faces = zpart[...] + zfix[...] + y_corners() if fixed else zpart[...]
         zheld[k] = faces
         halo_out[par, ZAT:ZAT + 64, :] = jnp.dot(
             faces * sface[...], wz[...], preferred_element_type=F32, precision=lax.Precision.HIGHEST)
-        turned_z = jnp.concatenate([zfix[...], jnp.zeros((64, 128), F32)], axis=0).T
+        if fixed:
+            turned_z = jnp.concatenate([zfix[...], jnp.zeros((64, 128), F32)], axis=0).T
         for side, y in ((0, 0), (1, 31)):
             for half in range(2):
                 speed = sp[1, :, y, halves[half]]
                 speed = jnp.maximum(speed, 0.0) if side == 0 else jnp.maximum(-speed, 0.0)
                 flux = []
                 for i in range(VARS):
-                    extra = turned_z[8 * i:8 * i + 8]
-                    shift = ((0, 95), (97, 64))[side][half]
-                    extra = pltpu.roll(extra, shift, axis=1) if shift else extra
                     at = y_at(side, i, half)
-                    value = ypart[at:at + 8, :] + yfix[at:at + 8, :] + jnp.where(lane8 == 127 * half, extra, 0.0)
+                    value = ypart[at:at + 8, :]
+                    if fixed:
+                        extra = turned_z[8 * i:8 * i + 8]
+                        shift = ((0, 95), (97, 64))[side][half]
+                        extra = pltpu.roll(extra, shift, axis=1) if shift else extra
+                        value = value + yfix[at:at + 8, :] + jnp.where(lane8 == 127 * half, extra, 0.0)
                     yheld[k, at:at + 8, :] = value
                     flux.append(value * speed)
                 for j in range(VARS):
@@ -356,25 +362,38 @@
 
     def stencil(x, w):
         prior = jnp.maximum(x - 1, 0)
-        for j in range(VARS):
-            wx = w[j]
-            flux = cpos[0, x] * wx - fprev[j]
-            nxt[j, prior] = part[j] - flux
-            fprev[j] = cneg[0, x] * wx
-            acc = po[x] * cur[j, x] + flux
-            wv = w[2 * VARS + j]
-            flux = cpos[2, x] * wv - pltpu.roll(cneg[2, x] * wv, 1, axis=1)
-            acc = acc + flux - pltpu.roll(flux, 255, axis=1)
-            for half in range(2):
-                at = halves[half]
-                wy = w[VARS + j, :, at]
-                minus = cneg[1, x, :, at] * wy
-                low_shift[j, half, 8:40, :] = minus
-                low_shift[j, half, 0:8, :] = minus[24:32]
-                flux = cpos[1, x, :, at] * wy - low_shift[j, half, 7:39, :]
-                high_shift[j, half, 0:32, :] = flux
-                high_shift[j, half, 32:40, :] = flux[0:8]
-                part[j, :, at] = acc[:, at] + flux - high_shift[j, half, 1:33, :]
+        tiles = [(slice(c, c + 8), half) for c in range(0, 32, 8) for half in range(2)]
+        for rows, half in tiles:
+            coefficient = cneg[1, x, rows, halves[half]]
+            for j in range(VARS):
+                minus = coefficient * w[VARS + j, rows, halves[half]]
+                low_shift[j, half, rows.start + 8:rows.start + 16, :] = minus
+                if rows.start == 24:
+                    low_shift[j, half, 0:8, :] = minus
+        for rows, half in tiles:
+            coefficient = cpos[1, x, rows, halves[half]]
+            for j in range(VARS):
+                flux = coefficient * w[VARS + j, rows, halves[half]] - low_shift[j, half, rows.start + 7:rows.start + 15, :]
+                high_shift[j, half, rows, :] = flux
+                if rows.start == 0:
+                    high_shift[j, half, 32:40, :] = flux
+        for c in range(0, 32, 8):
+            rows = slice(c, c + 8)
+            z_pos, z_neg, solid = cpos[2, x, rows], cneg[2, x, rows], po[x, rows]
+            x_pos, x_neg = cpos[0, x, rows], cneg[0, x, rows]
+            for j in range(VARS):
+                wx = w[j, rows]
+                flux = x_pos * wx - fprev[j, rows]
+                nxt[j, prior, rows] = part[j, rows] - flux
+                fprev[j, rows] = x_neg * wx
+                acc = solid * cur[j, x, rows] + flux
+                wv = w[2 * VARS + j, rows]
+                flux = z_pos * wv - pltpu.roll(z_neg * wv, 1, axis=1)
+                acc = acc + flux - pltpu.roll(flux, 255, axis=1)
+                for half in range(2):
+                    at = halves[half]
+                    part[j, rows, at] = acc[:, at] + (
+                        high_shift[j, half, rows, :] - high_shift[j, half, c + 1:c + 9, :])
 
     def sweep():
         fprev[...] = jnp.zeros(fprev.shape, F32)
@@ -469,23 +488,31 @@
         for l in range(4):
             prods[6 + l] = prods[6 + l] + sums[l]
 
-    yfix[...] = jnp.zeros(yfix.shape, F32)
-    zfix[...] = jnp.zeros(zfix.shape, F32)
     corner[...] = jnp.zeros(corner.shape, F32)
+    pack(cur, lambda i: loads[6 + i].wait())
+    finish(0, 0, fixed=False)
+    pl.semaphore_wait(barrier, (ny - 1) + (nz - 1))
+    send_halo(0)
+
+    @functools.partial(each, nz, start=1)
+    def _(delta):
+        pl.semaphore_signal(known_sem, inc=1, device_id={"gz": gz_at(delta)}, device_id_type=MESH)
+
+    prepare()
+    loads[2].wait()
     loads[1].wait()
 
-    @functools.partial(each, 4)
+    @functools.partial(each, 4, start=1)
     def _(k):
         par = k & 1
-        pack()
+        sweep()
+        pack(nxt)
 
         @pl.when(k == 3)
         def _():
             products((6, 7, 8, 9), 4)
 
-        @pl.when(k > 0)
-        def _():
-            receive(1 - par)
+        receive(1 - par)
 
         @pl.when(k == 3)
         def _():
@@ -494,29 +521,9 @@
         @pl.when(k < 3)
         def _():
             finish(k, par)
-
-            @pl.when(k == 0)
-            def _():
-                pl.semaphore_wait(barrier, (ny - 1) + (nz - 1))
-
             send_halo(par)
-
-            @pl.when(k == 0)
-            def _():
-                @functools.partial(each, nz, start=1)
-                def _(delta):
-                    pl.semaphore_signal(known_sem, inc=1, device_id={"gz": gz_at(delta)}, device_id_type=MESH)
-
             settle(k)
-
-            @pl.when(k > 0)
-            def _():
-                pltpu.make_async_copy(basis.at[k], held_hbm.at[k - 1], out_sem).start()
-
-            @pl.when(k == 0)
-            def _():
-                prepare()
-                loads[2].wait()
+            pltpu.make_async_copy(basis.at[k], held_hbm.at[k - 1], out_sem).start()
 
             @pl.when(k == 1)
             def _():
@@ -526,8 +533,6 @@
             def _():
                 dispatch()
                 products((3, 4, 5), 3)
-
-            sweep()
 
     sums = [prods[e] for e in range(10)]
 
@@ -672,7 +677,7 @@
             pltpu.VMEM((128, 128), F32),
             pltpu.VMEM((1, 128), F32),
             pltpu.VMEM((ny * nz, 128), F32),
-            dma((6,)), dma, dma((2, 4)), dma((2, 4)), dma((2,)), dma((2,)), dma((2,)), pltpu.SemaphoreType.REGULAR,
+            dma((6 + VARS,)), dma, dma((2, 4)), dma((2, 4)), dma((2,)), dma((2,)), dma((2,)), pltpu.SemaphoreType.REGULAR,
         ],
         compiler_params=pltpu.CompilerParams(
             collective_id=0, has_side_effects=True, vmem_limit_bytes=40 * 1024 * 1024),

time: 30.6 us -> 30.8 us (level)
  no operation moved by 1% of the time
where the time goes in v11:
time: 30.8 us; the launch traced here: 30.7 us
  Pallas kernels  30 us (97%)
  between operations  0.66 us (2%)
    pallas_call x1, Pallas kernels, local(): pl.pallas_call(functools.partial(kernel, ny, nz, per_owner), out_shape=[j...  28.9 us
    pallas_call x1, Pallas kernels, local(): pl.pallas_call(combine, out_shape=[jax.ShapeDtypeStruct(field, F32), jax....  1.11 us

profile of v11, /device:TPU:1, one launch (start us, length us, event | category | flops | bytes accessed | tf_op | source)
XLA Modules:
  0.0 30.7 jit_solution(17224407510825194599)
XLA Ops:
  0.6 0.0 copy-start
  0.6 28.9 %shard_map.77 = (f32[2,5,8,32,256]{4,3,2,1,0:T(8,128)S(1)}, f32[32,256]{1,0:T(8,128)S(1)}) custom-call(f32[5,8,32,256]{3,2,1,0:T(8,128)} %rs.1, f32[3,8,32,256]{3,2,1,0:T(8,128)} %sp_hbm.1, f32[8,32,256]{2,1,0:T(8,128)} %po_hbm.1, f32[5,3,5]{2,1,0:T(4,128)} %bitcast.2, f32[3,8,32,256]{3,2,1,0:T(8,128)} %mo_hbm.1, s32[2,8,64]{2,1,0:T(8,128)} %ids_hbm.1), custom_call_target="tpu_custom_call" | custom-call | tf_op jit(solution)/shard_map/pallas_call | solution.py:644
  29.6 0.0 copy-done
  29.6 1.1 %shard_map.78 = (f32[5,8,32,256]{3,2,1,0:T(8,128)}, f32[1,256]{1,0:T(1,128)}) custom-call(f32[5,8,32,256]{3,2,1,0:T(8,128)S(1)} %copy-done, f32[2,5,8,32,256]{4,3,2,1,0:T(8,128)S(1)} %get-tuple-element.6.held, f32[32,256]{1,0:T(8,128)S(1)} %get-tuple-element.7.small), custom_call_target="tpu_custom_call" | custom-call | tf_op jit(solution)/shard_map/pallas_call | solution.py:686
Async XLA Ops:
  0.6 28.9 %copy-start = (f32[5,8,32,256]{3,2,1,0:T(8,128)S(1)}, f32[5,8,32,256]{3,2,1,0:T(8,128)}, u32[]{:S(2)}) copy-start(f32[5,8,32,256]{3,2,1,0:T(8,128)} %rs.1) | copy-start | bytes 3932164

commit v12 on v11

--- a/solution.py
+++ b/solution.py
@@ -139,10 +139,6 @@
     @functools.partial(each, ny - 1, start=2)
     def _(delta):
         greet({"gy": gy_at(delta)})
-
-    @functools.partial(each, nz - 1, start=2)
-    def _(delta):
-        greet({"gz": gz_at(delta)})
 
     for place in (2, 1, 3):
         loads[place].start()
@@ -491,13 +487,14 @@
     corner[...] = jnp.zeros(corner.shape, F32)
     pack(cur, lambda i: loads[6 + i].wait())
     finish(0, 0, fixed=False)
-    pl.semaphore_wait(barrier, (ny - 1) + (nz - 1))
+    pl.semaphore_wait(barrier, (ny - 1) + 2)
     send_halo(0)
 
-    @functools.partial(each, nz, start=1)
-    def _(delta):
-        pl.semaphore_signal(known_sem, inc=1, device_id={"gz": gz_at(delta)}, device_id_type=MESH)
-
+    def tell(k, distance):
+        for delta in (distance, -distance):
+            pl.semaphore_signal(known_sem.at[k], inc=1, device_id={"gz": gz_at(delta)}, device_id_type=MESH)
+
+    tell(0, 1)
     prepare()
     loads[2].wait()
     loads[1].wait()
@@ -506,6 +503,16 @@
     def _(k):
         par = k & 1
         sweep()
+        pl.semaphore_wait(known_sem.at[k - 1], 2)
+
+        @pl.when(k < 3)
+        def _():
+            tell(k, 2 * k)
+
+        @pl.when(k == 3)
+        def _():
+            pl.semaphore_signal(known_sem.at[3], inc=1, device_id={"gz": gz_at(nz // 2)}, device_id_type=MESH)
+
         pack(nxt)
 
         @pl.when(k == 3)
@@ -544,20 +551,25 @@
         packed = jnp.where((lane >> 3) == e, value, packed)
     gsend[...] = jnp.sum(packed, axis=0, keepdims=True)
 
-    pl.semaphore_wait(known_sem, nz - 1)
-
-    def send_gram(a):
+    def send_gram(a, start, count):
         row = gy_at(a)
 
-        @functools.partial(each, nz, start=0 if a else 1, unroll=8 if a else 5)
+        @functools.partial(each, start + count, start=start, unroll=count)
         def _(b):
             pltpu.make_async_remote_copy(
                 src_ref=gsend, dst_ref=grecv.at[pl.ds(a * nz + b, 1)], send_sem=g_sem.at[0], recv_sem=g_sem.at[1],
                 device_id={"gy": row, "gz": gz_at(b)}, device_id_type=MESH).start()
 
+    def send_most(a):
+        if a == 0:
+            send_gram(0, 1, nz - 1)
+        else:
+            send_gram(a, 0, nz // 2)
+            send_gram(a, nz // 2 + 1, nz // 2 - 1)
+
     order = sorted(range(ny), key=lambda a: -min(a, ny - a))
     for a in order[:ny // 2]:
-        send_gram(a)
+        send_most(a)
 
     wait_all(recv1.at[pl.ds(1, ny - 1)], a1_sem.at[1])
     wait_all(recv1.at[pl.ds(1, ny - 1)], a1_sem.at[0])
@@ -572,7 +584,10 @@
     recv2[0] = turned[gz]
 
     for a in order[ny // 2:]:
-        send_gram(a)
+        send_most(a)
+    pl.semaphore_wait(known_sem.at[3], 1)
+    for a in range(1, ny):
+        send_gram(a, nz // 2, 1)
 
     wait_all(recv2.at[pl.ds(1, nz - 1)], a2_sem.at[1])
     wait_all(recv2.at[pl.ds(1, nz - 1)], a2_sem.at[0])
@@ -677,7 +692,7 @@
             pltpu.VMEM((128, 128), F32),
             pltpu.VMEM((1, 128), F32),
             pltpu.VMEM((ny * nz, 128), F32),
-            dma((6 + VARS,)), dma, dma((2, 4)), dma((2, 4)), dma((2,)), dma((2,)), dma((2,)), pltpu.SemaphoreType.REGULAR,
+            dma((6 + VARS,)), dma, dma((2, 4)), dma((2, 4)), dma((2,)), dma((2,)), dma((2,)), pltpu.SemaphoreType.REGULAR((4,)),
         ],
         compiler_params=pltpu.CompilerParams(
             collective_id=0, has_side_effects=True, vmem_limit_bytes=40 * 1024 * 1024),

time: 30.8 us -> 30.8 us (level)
  no operation moved by 1% of the time
where the time goes in v12:
time: 30.8 us; the launch traced here: 30.7 us
  Pallas kernels  30 us (97%)
  between operations  0.66 us (2%)
    pallas_call x1, Pallas kernels, local(): pl.pallas_call(functools.partial(kernel, ny, nz, per_owner), out_shape=[j...  28.9 us
    pallas_call x1, Pallas kernels, local(): pl.pallas_call(combine, out_shape=[jax.ShapeDtypeStruct(field, F32), jax....  1.11 us

profile of v12, /device:TPU:1, one launch (start us, length us, event | category | flops | bytes accessed | tf_op | source)
XLA Modules:
  0.0 30.7 jit_solution(6524463303330924204)
XLA Ops:
  0.6 0.0 copy-start
  0.6 28.9 %shard_map.77 = (f32[2,5,8,32,256]{4,3,2,1,0:T(8,128)S(1)}, f32[32,256]{1,0:T(8,128)S(1)}) custom-call(f32[5,8,32,256]{3,2,1,0:T(8,128)} %rs.1, f32[3,8,32,256]{3,2,1,0:T(8,128)} %sp_hbm.1, f32[8,32,256]{2,1,0:T(8,128)} %po_hbm.1, f32[5,3,5]{2,1,0:T(4,128)} %bitcast.2, f32[3,8,32,256]{3,2,1,0:T(8,128)} %mo_hbm.1, s32[2,8,64]{2,1,0:T(8,128)} %ids_hbm.1), custom_call_target="tpu_custom_call" | custom-call | tf_op jit(solution)/shard_map/pallas_call | solution.py:659
  29.5 0.0 copy-done
  29.5 1.1 %shard_map.78 = (f32[5,8,32,256]{3,2,1,0:T(8,128)}, f32[1,256]{1,0:T(1,128)}) custom-call(f32[5,8,32,256]{3,2,1,0:T(8,128)S(1)} %copy-done, f32[2,5,8,32,256]{4,3,2,1,0:T(8,128)S(1)} %get-tuple-element.6.held, f32[32,256]{1,0:T(8,128)S(1)} %get-tuple-element.7.small), custom_call_target="tpu_custom_call" | custom-call | tf_op jit(solution)/shard_map/pallas_call | solution.py:701
Async XLA Ops:
  0.6 28.9 %copy-start = (f32[5,8,32,256]{3,2,1,0:T(8,128)S(1)}, f32[5,8,32,256]{3,2,1,0:T(8,128)}, u32[]{:S(2)}) copy-start(f32[5,8,32,256]{3,2,1,0:T(8,128)} %rs.1) | copy-start | bytes 3932164

commit v13 on v12

--- a/solution.py
+++ b/solution.py
@@ -543,33 +543,32 @@
 
     sums = [prods[e] for e in range(10)]
 
-    lane = iota((8, 128), 1)
-    packed = jnp.zeros((8, 128), F32)
+    row8 = iota((8, 128), 0)
+    stacked = [jnp.zeros((8, 128), F32), jnp.zeros((8, 128), F32)]
     for e, value in enumerate(sums):
-        for shift in (64, 32, 16, 8):
-            value = value + pltpu.roll(value, shift, axis=1)
-        packed = jnp.where((lane >> 3) == e, value, packed)
+        stacked[e // 8] = jnp.where(row8 == e % 8, jnp.sum(value, axis=0, keepdims=True), stacked[e // 8])
+    split = jnp.concatenate(pieces(jnp.concatenate(stacked, axis=0)), axis=0)
+    totals = dot(split, jnp.ones((128, 128), BF16))
+    totals = totals[0:16] + totals[16:32] + totals[32:48]
+    packed = jnp.where((iota((16, 128), 1) >> 3) == iota((16, 128), 0), totals, 0.0)
     gsend[...] = jnp.sum(packed, axis=0, keepdims=True)
 
-    def send_gram(a, start, count):
-        row = gy_at(a)
-
-        @functools.partial(each, start + count, start=start, unroll=count)
-        def _(b):
-            pltpu.make_async_remote_copy(
-                src_ref=gsend, dst_ref=grecv.at[pl.ds(a * nz + b, 1)], send_sem=g_sem.at[0], recv_sem=g_sem.at[1],
-                device_id={"gy": row, "gz": gz_at(b)}, device_id_type=MESH).start()
-
-    def send_most(a):
-        if a == 0:
-            send_gram(0, 1, nz - 1)
-        else:
-            send_gram(a, 0, nz // 2)
-            send_gram(a, nz // 2 + 1, nz // 2 - 1)
-
-    order = sorted(range(ny), key=lambda a: -min(a, ny - a))
-    for a in order[:ny // 2]:
-        send_most(a)
+    def send_gram(a, b):
+        pltpu.make_async_remote_copy(
+            src_ref=gsend, dst_ref=grecv.at[pl.ds(a * nz + b, 1)], send_sem=g_sem.at[0], recv_sem=g_sem.at[1],
+            device_id={"gy": gy_at(a), "gz": gz_at(b)}, device_id_type=MESH).start()
+
+    def ring(offset, size):
+        return min(offset % size, size - offset % size)
+
+    def hops(place):
+        a, b = place
+        return ring(a, ny) / 2 + ring(b, 4) + ring(b // 4, nz // 4)
+
+    places = [(a, b) for a in range(ny) for b in range(nz) if a + b and (a == 0 or b != nz // 2)]
+    places = sorted(places, key=lambda place: -hops(place))
+    for a, b in places[:number // 2]:
+        send_gram(a, b)
 
     wait_all(recv1.at[pl.ds(1, ny - 1)], a1_sem.at[1])
     wait_all(recv1.at[pl.ds(1, ny - 1)], a1_sem.at[0])
@@ -583,11 +582,11 @@
             device_id={"gz": gz_at(delta)}, device_id_type=MESH).start()
     recv2[0] = turned[gz]
 
-    for a in order[ny // 2:]:
-        send_most(a)
+    for a, b in places[number // 2:]:
+        send_gram(a, b)
     pl.semaphore_wait(known_sem.at[3], 1)
     for a in range(1, ny):
-        send_gram(a, nz // 2, 1)
+        send_gram(a, nz // 2)
 
     wait_all(recv2.at[pl.ds(1, nz - 1)], a2_sem.at[1])
     wait_all(recv2.at[pl.ds(1, nz - 1)], a2_sem.at[0])
@@ -613,8 +612,6 @@
     for at in range(8, number, 8):
         own = own + grecv[at:at + 8, :]
     own = jnp.sum(own, axis=0, keepdims=True)
-    for shift in (4, 2, 1):
-        own = own + pltpu.roll(own, shift, axis=1)
     own = jnp.broadcast_to(own, (8, 128))
     splat = {}
     for e, (l, k) in enumerate(pairs):

time: 30.8 us -> 30.4 us (0.987)
  Pallas kernels: 30 us -> 29.6 us
    pallas_call x1, Pallas kernels: 28.9 us -> 28.5 us  [local(): pl.pallas_call(functools.partial(kernel, ny, nz, per_owner), out_shape=[j...]
where the time goes in v13:
time: 30.4 us; the launch traced here: 30.3 us
  Pallas kernels  29.6 us (97%)
  between operations  0.66 us (2%)
    pallas_call x1, Pallas kernels, local(): pl.pallas_call(functools.partial(kernel, ny, nz, per_owner), out_shape=[j...  28.5 us
    pallas_call x1, Pallas kernels, local(): pl.pallas_call(combine, out_shape=[jax.ShapeDtypeStruct(field, F32), jax....  1.11 us

profile of v13, /device:TPU:1, one launch (start us, length us, event | category | flops | bytes accessed | tf_op | source)
XLA Modules:
  0.0 30.3 jit_solution(9889667963145077642)
XLA Ops:
  0.6 0.0 copy-start
  0.6 28.5 %shard_map.77 = (f32[2,5,8,32,256]{4,3,2,1,0:T(8,128)S(1)}, f32[32,256]{1,0:T(8,128)S(1)}) custom-call(f32[5,8,32,256]{3,2,1,0:T(8,128)} %rs.1, f32[3,8,32,256]{3,2,1,0:T(8,128)} %sp_hbm.1, f32[8,32,256]{2,1,0:T(8,128)} %po_hbm.1, f32[5,3,5]{2,1,0:T(4,128)} %bitcast.2, f32[3,8,32,256]{3,2,1,0:T(8,128)} %mo_hbm.1, s32[2,8,64]{2,1,0:T(8,128)} %ids_hbm.1), custom_call_target="tpu_custom_call" | custom-call | tf_op jit(solution)/shard_map/pallas_call | solution.py:656
  29.2 0.0 copy-done
  29.2 1.1 %shard_map.78 = (f32[5,8,32,256]{3,2,1,0:T(8,128)}, f32[1,256]{1,0:T(1,128)}) custom-call(f32[5,8,32,256]{3,2,1,0:T(8,128)S(1)} %copy-done, f32[2,5,8,32,256]{4,3,2,1,0:T(8,128)S(1)} %get-tuple-element.6.held, f32[32,256]{1,0:T(8,128)S(1)} %get-tuple-element.7.small), custom_call_target="tpu_custom_call" | custom-call | tf_op jit(solution)/shard_map/pallas_call | solution.py:698
Async XLA Ops:
  0.6 28.5 %copy-start = (f32[5,8,32,256]{3,2,1,0:T(8,128)S(1)}, f32[5,8,32,256]{3,2,1,0:T(8,128)}, u32[]{:S(2)}) copy-start(f32[5,8,32,256]{3,2,1,0:T(8,128)} %rs.1) | copy-start | bytes 3932164

commit v14 on v13

--- a/solution.py
+++ b/solution.py
@@ -273,11 +273,17 @@
             parts.append(jnp.where(rows32 == 0, both, jnp.where(rows32 == 31, pltpu.roll(both, 64, axis=1), 0.0)))
         return jnp.where(jnp.concatenate([lanes, lanes], axis=0) < 8 * VARS, jnp.concatenate(parts, axis=0), 0.0)
 
+    def couple_faces(flux):
+        top = flux.astype(BF16)
+        rest = (flux - top.astype(F32)).astype(BF16)
+        heavy = wz[...].astype(BF16)
+        light = (wz[...] - heavy.astype(F32)).astype(BF16)
+        return dot(top, heavy) + (dot(rest, heavy) + dot(top, light))
+
     def finish(k, par, fixed=True):
         faces = zpart[...] + zfix[...] + y_corners() if fixed else zpart[...]
         zheld[k] = faces
-        halo_out[par, ZAT:ZAT + 64, :] = jnp.dot(
-            faces * sface[...], wz[...], preferred_element_type=F32, precision=lax.Precision.HIGHEST)
+        halo_out[par, ZAT:ZAT + 64, :] = couple_faces(faces * sface[...])
         if fixed:
             turned_z = jnp.concatenate([zfix[...], jnp.zeros((64, 128), F32)], axis=0).T
         for side, y in ((0, 0), (1, 31)):
@@ -567,7 +573,7 @@
 
     places = [(a, b) for a in range(ny) for b in range(nz) if a + b and (a == 0 or b != nz // 2)]
     places = sorted(places, key=lambda place: -hops(place))
-    for a, b in places[:number // 2]:
+    for a, b in places[:96]:
         send_gram(a, b)
 
     wait_all(recv1.at[pl.ds(1, ny - 1)], a1_sem.at[1])
@@ -582,7 +588,7 @@
             device_id={"gz": gz_at(delta)}, device_id_type=MESH).start()
     recv2[0] = turned[gz]
 
-    for a, b in places[number // 2:]:
+    for a, b in places[96:]:
         send_gram(a, b)
     pl.semaphore_wait(known_sem.at[3], 1)
     for a in range(1, ny):

time: 30.4 us -> 30.3 us (level)
  no operation moved by 1% of the time
where the time goes in v14:
time: 30.3 us; the launch traced here: 30.2 us
  Pallas kernels  29.5 us (97%)
  between operations  0.66 us (2%)
    pallas_call x1, Pallas kernels, local(): pl.pallas_call(functools.partial(kernel, ny, nz, per_owner), out_shape=[j...  28.4 us
    pallas_call x1, Pallas kernels, local(): pl.pallas_call(combine, out_shape=[jax.ShapeDtypeStruct(field, F32), jax....  1.11 us

profile of v14, /device:TPU:1, one launch (start us, length us, event | category | flops | bytes accessed | tf_op | source)
XLA Modules:
  0.0 30.2 jit_solution(18348523408320975916)
XLA Ops:
  0.6 0.0 copy-start
  0.6 28.4 %shard_map.77 = (f32[2,5,8,32,256]{4,3,2,1,0:T(8,128)S(1)}, f32[32,256]{1,0:T(8,128)S(1)}) custom-call(f32[5,8,32,256]{3,2,1,0:T(8,128)} %rs.1, f32[3,8,32,256]{3,2,1,0:T(8,128)} %sp_hbm.1, f32[8,32,256]{2,1,0:T(8,128)} %po_hbm.1, f32[5,3,5]{2,1,0:T(4,128)} %bitcast.2, f32[3,8,32,256]{3,2,1,0:T(8,128)} %mo_hbm.1, s32[2,8,64]{2,1,0:T(8,128)} %ids_hbm.1), custom_call_target="tpu_custom_call" | custom-call | tf_op jit(solution)/shard_map/pallas_call | solution.py:662
  29.1 0.0 copy-done
  29.1 1.1 %shard_map.78 = (f32[5,8,32,256]{3,2,1,0:T(8,128)}, f32[1,256]{1,0:T(1,128)}) custom-call(f32[5,8,32,256]{3,2,1,0:T(8,128)S(1)} %copy-done, f32[2,5,8,32,256]{4,3,2,1,0:T(8,128)S(1)} %get-tuple-element.6.held, f32[32,256]{1,0:T(8,128)S(1)} %get-tuple-element.7.small), custom_call_target="tpu_custom_call" | custom-call | tf_op jit(solution)/shard_map/pallas_call | solution.py:704
Async XLA Ops:
  0.6 28.4 %copy-start = (f32[5,8,32,256]{3,2,1,0:T(8,128)S(1)}, f32[5,8,32,256]{3,2,1,0:T(8,128)}, u32[]{:S(2)}) copy-start(f32[5,8,32,256]{3,2,1,0:T(8,128)} %rs.1) | copy-start | bytes 3932164
